TPU v7x, 32 devices: a whole 2x2x4 slice. The times are simulated.
32 devices in a mesh: groups: 2 (over y), tm: 2 (over core), space: 8 (over z, x).
Axes of the slice: x: 2, y: 2, z: 4, core: 2. Of those that a mesh axis runs over, the one named last changes fastest.
Arguments:
- initial: float32 [32, 192, 256], P(('groups', 'space')), parts along dimension 0, may hold values from -6 to 6
- reaction: float32 [32, 192, 256], P(('groups', 'space')), parts along dimension 0, may hold values from 0.01 to 0.15
Outputs:
- slab_ends: float32 [4, 16, 192, 256], P(('groups', 'tm'), 'space'), parts along dimension 0
There are 2 independent parts, one for each index of `groups`. A program takes and returns all parts, laid end to end along the dimension named above; each array names one. Nothing has to cross between parts.
All inputs are finite; a program needn't handle non-finite values.
Results may differ from a plain program's by a relative error of at most 0.0001.
Values sent between devices are 32-bit elements; how exact they have to be, the bound alone decides.
No kernel may reach another device: no remote copies, remote signals or barrier semaphores. Data moves between devices by JAX's collectives and lax.ppermute only.
A program may use at most 64 MiB of HBM per device.

v0:
```python
import jax
import jax.numpy as jnp
from jax import lax
from jax.sharding import PartitionSpec as P

FSTEPS = 16
CSTEPS = 4


def with_halo(cells, sides, width):
    for axis, dim in sides:
        count = lax.axis_size(axis)
        ends = count - 1
        head = lax.slice_in_dim(cells, 0, width, axis=dim)
        tail = lax.slice_in_dim(cells, cells.shape[dim] - width, cells.shape[dim], axis=dim)
        cells = jnp.concatenate(
            [
                lax.ppermute(tail, axis, [(i, (i + 1) % count) for i in range(ends)]),
                cells,
                lax.ppermute(head, axis, [((i + 1) % count, i) for i in range(ends)]),
            ],
            axis=dim,
        )
    return cells


def passed_along(x, axis, by):
    count = lax.axis_size(axis)
    pairs = [(i, i + by) for i in range(count) if 0 <= i + by < count]
    return lax.ppermute(x, axis, pairs)


def stencil(padded, reaction_rate, step_len, diffusion, upwind_scale):
    middle = padded[1:-1]
    lower_plane = padded[:-2]
    upper_plane = padded[2:]
    x_minus = jnp.roll(middle, 1, 1)
    x_plus = jnp.roll(middle, -1, 1)
    y_minus = jnp.roll(middle, 1, 2)
    y_plus = jnp.roll(middle, -1, 2)
    laplace = upper_plane + lower_plane + x_plus + x_minus + y_plus + y_minus - 6.0 * middle
    upwind = 0.13 * (middle - lower_plane) + 0.12 * (middle - x_minus) + 0.1 * (middle - y_minus)
    return middle + step_len * (
        diffusion * laplace - upwind_scale * upwind - reaction_rate * middle
    )


def restrict(field):
    depth, rows, cols = field.shape
    return field.reshape(depth // 2, 2, rows // 2, 2, cols // 2, 2).mean(axis=(1, 3, 5))


def prolong(coarse_field):
    return jnp.repeat(jnp.repeat(jnp.repeat(coarse_field, 2, 0), 2, 1), 2, 2)


def advance(field, rate_padded, width, steps, exchanger, constants, first_plane, planes_total):
    planes = field.shape[0]

    def block_turn(turn_index, current):
        padded = exchanger(current)
        for inner in range(width):
            rim_after = width - 1 - inner
            rate_slice = rate_padded[inner + 1 : inner + 1 + planes + 2 * rim_after]
            updated = stencil(padded, rate_slice, constants[0], constants[1], constants[2])
            global_plane = first_plane - rim_after + lax.iota(jnp.int32, planes + 2 * rim_after)
            inside = (global_plane >= 0) & (global_plane < planes_total)
            padded = jnp.where(inside[:, None, None], updated, 0.0)
        return padded

    return lax.fori_loop(0, steps // width, block_turn, field)


def local(initial, reaction):
    planes = initial.shape[0]
    planes_total = planes * lax.axis_size("space")
    first_plane = lax.axis_index("space") * planes
    slab_index = lax.axis_index("tm")
    slab_count = lax.axis_size("tm")
    coarse_rate = restrict(reaction)
    no_rim = ((1, 1), (0, 0), (0, 0))
    fine_width = min(planes, FSTEPS)
    fine_rate = with_halo(reaction, (("space", 0),), fine_width)

    def fine_exchange(current):
        return with_halo(current, (("space", 0),), fine_width)

    coarse_width = 1
    coarse_padded = jnp.pad(coarse_rate, no_rim)

    def coarse_exchange(current):
        return with_halo(current, (("space", 0),), 1)

    def coarse_run(field):
        small = advance(
            restrict(field),
            coarse_padded,
            coarse_width,
            CSTEPS,
            coarse_exchange,
            (2.0, 0.025, 0.5),
            first_plane // 2,
            planes_total // 2,
        )
        return prolong(small)

    def sweep(fine_values, previous):
        state = initial
        result = initial
        guess = initial
        for sweep_turn in range(slab_count):
            guess = coarse_run(state)
            if fine_values is None:
                result = guess
            else:
                result = guess + fine_values - previous
            if sweep_turn < slab_count - 1:
                incoming = passed_along(result, "tm", 1)
                state = jnp.where(slab_index == 0, initial, incoming)
        return (result, guess, state)

    result, previous, start = sweep(None, None)
    fine_values = advance(
        start,
        fine_rate,
        fine_width,
        FSTEPS,
        fine_exchange,
        (0.5, 0.1, 1.0),
        first_plane,
        planes_total,
    )
    result, previous, start = sweep(fine_values, previous)
    return result[None]


def solution(mesh):
    in_specs = (P(("groups", "space"), None, None), P(("groups", "space"), None, None))
    out_specs = P(("groups", "tm"), "space", None, None)
    return jax.shard_map(local, mesh=mesh, in_specs=in_specs, out_specs=out_specs, check_vma=False)
```

profile of v0, /device:TPU:0, one launch (start us, length us, event | category | flops | bytes accessed | tf_op | source)
XLA Modules:
  0.0 408.5 jit_solution(9851005696565650180)
XLA Ops:
  1.0 13.9 %reduce_sum.54 = f32[96,2,128,2]{3,2,1,0:T(8,128)} reshape(f32[192,256]{1,0:T(8,128)S(1)} %reduce_sum.53) | data formatting | bytes 393216 | tf_op jit(solution)/shard_map/reduce_sum | solution.py:50
  15.0 6.3 %reduce_sum.55 = f32[96,128]{1,0:T(8,128)S(1)} reduce(f32[96,2,128,2]{3,2,1,0:T(8,128)} %reduce_sum.54, f32[]{:T(128)} %constant.239.clone.1), dimensions={1,3}, to_apply=%region_1.2 | reduce | flops 36864 | bytes 245764 | tf_op jit(solution)/shard_map/reduce_sum | solution.py:50
  21.4 13.9 %reduce_sum.72 = f32[96,2,128,2]{3,2,1,0:T(8,128)} reshape(f32[192,256]{1,0:T(8,128)S(1)} %reduce_sum.59) | data formatting | bytes 393216 | tf_op jit(solution)/shard_map/reduce_sum | solution.py:50
  35.3 6.3 %reduce_sum.73 = f32[96,128]{1,0:T(8,128)S(1)} reduce(f32[96,2,128,2]{3,2,1,0:T(8,128)} %reduce_sum.72, f32[]{:T(128)} %constant.239.clone.1), dimensions={1,3}, to_apply=%region_3.4 | reduce | flops 36864 | bytes 245764 | tf_op jit(solution)/shard_map/reduce_sum | solution.py:50
  41.6 41.4 %while.61 = (s32[]{:T(128)}, f32[1,96,128]{2,1,0:T(8,128)S(1)}, pred[1]{0:T(512)(128)(4,1)}, f32[3,96,128]{2,1,0:T(8,128)S(1)}, s32[]{:T(128)}) while((s32[]{:T(128)}, f32[1,96,128]{2,1,0:T(8,128)S(1)}, pred[1]{0:T(512)(128)(4,1)}, f32[3,96,128]{2,1,0:T(8,128)S(1)}, s32[]{:T(128)}) %tuple.153), condition=%wide.region_5.6_spmd, body=%wide.region_4.5_spmd.sunk | while | flops 331778 | bytes 1228942 | solution.py:71
  41.6 4.8 %collective-permute-start = (f32[1,96,128]{2,1,0:T(8,128)S(1)}, f32[1,96,128]{2,1,0:T(8,128)S(1)}, u32[]{:S(2)}, u32[]{:S(2)}) collective-permute-start(f32[1,96,128]{2,1,0:T(8,128)S(1)} %get-tuple-element.527), channel_id=1, source_target_pairs={{0,1},{1,2},{2,3},{3,4},{4,5},{5,6},{6,7},{8,9},{9,10},{10,11},{11... | collective-permute-start | bytes 147464 | tf_op jit(solution)/shard_map/while/body/eval_jaxpr/ppermute | solution.py:18
  48.2 4.3 %collective-permute-done.1 = f32[1,96,128]{2,1,0:T(8,128)S(1)} collective-permute-done((f32[1,96,128]{2,1,0:T(8,128)S(1)}, f32[1,96,128]{2,1,0:T(8,128)S(1)}, u32[]{:S(2)}, u32[]{:S(2)}) %collective-permute-start.1) | collective-permute-done | bytes 49184 | tf_op jit(solution)/shard_map/while/body/eval_jaxpr/ppermute | solution.py:20
  52.6 4.4 %collective-permute-start = (f32[1,96,128]{2,1,0:T(8,128)S(1)}, f32[1,96,128]{2,1,0:T(8,128)S(1)}, u32[]{:S(2)}, u32[]{:S(2)}) collective-permute-start(f32[1,96,128]{2,1,0:T(8,128)S(1)} %get-tuple-element.527), channel_id=1, source_target_pairs={{0,1},{1,2},{2,3},{3,4},{4,5},{5,6},{6,7},{8,9},{9,10},{10,11},{11... | collective-permute-start | bytes 147464 | tf_op jit(solution)/shard_map/while/body/eval_jaxpr/ppermute | solution.py:18
  58.7 4.3 %collective-permute-done.1 = f32[1,96,128]{2,1,0:T(8,128)S(1)} collective-permute-done((f32[1,96,128]{2,1,0:T(8,128)S(1)}, f32[1,96,128]{2,1,0:T(8,128)S(1)}, u32[]{:S(2)}, u32[]{:S(2)}) %collective-permute-start.1) | collective-permute-done | bytes 49184 | tf_op jit(solution)/shard_map/while/body/eval_jaxpr/ppermute | solution.py:20
  63.1 3.4 collective-permute-start
  68.6 3.8 collective-permute-done.1
  72.6 4.4 %collective-permute-start = (f32[1,96,128]{2,1,0:T(8,128)S(1)}, f32[1,96,128]{2,1,0:T(8,128)S(1)}, u32[]{:S(2)}, u32[]{:S(2)}) collective-permute-start(f32[1,96,128]{2,1,0:T(8,128)S(1)} %get-tuple-element.527), channel_id=1, source_target_pairs={{0,1},{1,2},{2,3},{3,4},{4,5},{5,6},{6,7},{8,9},{9,10},{10,11},{11... | collective-permute-start | bytes 147464 | tf_op jit(solution)/shard_map/while/body/eval_jaxpr/ppermute | solution.py:18
  78.7 4.3 %collective-permute-done.1 = f32[1,96,128]{2,1,0:T(8,128)S(1)} collective-permute-done((f32[1,96,128]{2,1,0:T(8,128)S(1)}, f32[1,96,128]{2,1,0:T(8,128)S(1)}, u32[]{:S(2)}, u32[]{:S(2)}) %collective-permute-start.1) | collective-permute-done | bytes 49184 | tf_op jit(solution)/shard_map/while/body/eval_jaxpr/ppermute | solution.py:20
  83.6 1.3 collective-permute-start.8
  86.3 5.3 %collective-permute-start.9 = (f32[2,192,256]{2,1,0:T(8,128)S(1)}, f32[2,192,256]{2,1,0:T(8,128)}, u32[]{:S(2)}, u32[]{:S(2)}) collective-permute-start(f32[2,192,256]{2,1,0:T(8,128)S(1)} %copy-done), channel_id=1, source_target_pairs={{0,1},{1,2},{2,3},{3,4},{4,5},{5,6},{6,7},{8,9},{9,10},{10,11},{11... | collective-permute-start | bytes 1179656 | tf_op jit(solution)/shard_map/ppermute | solution.py:18
  91.7 13.9 %reduce_sum.75 = f32[96,2,128,2]{3,2,1,0:T(8,128)} reshape(f32[192,256]{1,0:T(8,128)S(1)} %get-tuple-element.275) | data formatting | bytes 393216 | tf_op jit(solution)/shard_map/reduce_sum | solution.py:50
  105.6 6.3 %reduce_sum.76 = f32[96,128]{1,0:T(8,128)S(1)} reduce(f32[96,2,128,2]{3,2,1,0:T(8,128)} %reduce_sum.75, f32[]{:T(128)} %constant.239.clone.1), dimensions={1,3}, to_apply=%region_9.10 | reduce | flops 36864 | bytes 245764 | tf_op jit(solution)/shard_map/reduce_sum | solution.py:50
  111.9 39.7 %while.63 = (s32[]{:T(128)}, f32[1,96,128]{2,1,0:T(8,128)S(1)}, pred[1]{0:T(512)(128)(4,1)}, f32[3,96,128]{2,1,0:T(8,128)S(1)}, s32[]{:T(128)}) while((s32[]{:T(128)}, f32[1,96,128]{2,1,0:T(8,128)S(1)}, pred[1]{0:T(512)(128)(4,1)}, f32[3,96,128]{2,1,0:T(8,128)S(1)}, s32[]{:T(128)}) %tuple.166), condition=%wide.region_11.12_spmd, body=%wide.region_10.11_spmd.sunk | while | flops 331778 | bytes 1228942 | solution.py:71
  111.9 3.7 collective-permute-start.4
  117.4 4.3 %collective-permute-done.5 = f32[1,96,128]{2,1,0:T(8,128)S(1)} collective-permute-done((f32[1,96,128]{2,1,0:T(8,128)S(1)}, f32[1,96,128]{2,1,0:T(8,128)S(1)}, u32[]{:S(2)}, u32[]{:S(2)}) %collective-permute-start.5) | collective-permute-done | bytes 49184 | tf_op jit(solution)/shard_map/while/body/eval_jaxpr/ppermute | solution.py:20
  121.7 3.5 collective-permute-start.4
  126.9 4.3 %collective-permute-done.5 = f32[1,96,128]{2,1,0:T(8,128)S(1)} collective-permute-done((f32[1,96,128]{2,1,0:T(8,128)S(1)}, f32[1,96,128]{2,1,0:T(8,128)S(1)}, u32[]{:S(2)}, u32[]{:S(2)}) %collective-permute-start.5) | collective-permute-done | bytes 49184 | tf_op jit(solution)/shard_map/while/body/eval_jaxpr/ppermute | solution.py:20
  131.3 4.6 %collective-permute-start.4 = (f32[1,96,128]{2,1,0:T(8,128)S(1)}, f32[1,96,128]{2,1,0:T(8,128)S(1)}, u32[]{:S(2)}, u32[]{:S(2)}) collective-permute-start(f32[1,96,128]{2,1,0:T(8,128)S(1)} %get-tuple-element.563), channel_id=1, source_target_pairs={{0,1},{1,2},{2,3},{3,4},{4,5},{5,6},{6,7},{8,9},{9,10},{10,11},{11... | collective-permute-start | bytes 147464 | tf_op jit(solution)/shard_map/while/body/eval_jaxpr/ppermute | solution.py:18
  137.7 4.3 %collective-permute-done.5 = f32[1,96,128]{2,1,0:T(8,128)S(1)} collective-permute-done((f32[1,96,128]{2,1,0:T(8,128)S(1)}, f32[1,96,128]{2,1,0:T(8,128)S(1)}, u32[]{:S(2)}, u32[]{:S(2)}) %collective-permute-start.5) | collective-permute-done | bytes 49184 | tf_op jit(solution)/shard_map/while/body/eval_jaxpr/ppermute | solution.py:20
  142.1 2.9 collective-permute-start.4
  146.8 4.7 %collective-permute-done.5 = f32[1,96,128]{2,1,0:T(8,128)S(1)} collective-permute-done((f32[1,96,128]{2,1,0:T(8,128)S(1)}, f32[1,96,128]{2,1,0:T(8,128)S(1)}, u32[]{:S(2)}, u32[]{:S(2)}) %collective-permute-start.5) | collective-permute-done | bytes 49184 | tf_op jit(solution)/shard_map/while/body/eval_jaxpr/ppermute | solution.py:20
  154.1 188.8 %while.62 = (s32[]{:T(128)}, f32[2,192,256]{2,1,0:T(8,128)S(1)}, s32[]{:T(128)}, s32[]{:T(128)}, f32[6,192,256]{2,1,0:T(8,128)S(1)}, /*index=5*/f32[2,192,256]{2,1,0:T(8,128)S(1)}, s32[]{:T(128)}) while((s32[]{:T(128)}, f32[2,192,256]{2,1,0:T(8,128)S(1)}, s32[]{:T(128)}, s32[]{:T(128)}, f32[6,192,256]{2,1,0:T(8,128)S(1)}, ...), condition=%wide.region_7.8_spmd, body=%wide.region_6.7_spmd.sunk | while | flops 7864346 | bytes 26345648 | solution.py:71
  154.1 3.4 collective-permute-start.2
  158.9 4.4 %collective-permute-done.2 = f32[2,192,256]{2,1,0:T(8,128)S(1)} collective-permute-done((f32[2,192,256]{2,1,0:T(8,128)S(1)}, f32[2,192,256]{2,1,0:T(8,128)S(1)}, u32[]{:S(2)}, u32[]{:S(2)}) %collective-permute-start.2) | collective-permute-done | bytes 393248 | tf_op jit(solution)/shard_map/while/body/eval_jaxpr/ppermute | solution.py:18
  163.5 5.9 %collective-permute-done.3 = f32[2,192,256]{2,1,0:T(8,128)S(1)} collective-permute-done((f32[2,192,256]{2,1,0:T(8,128)S(1)}, f32[2,192,256]{2,1,0:T(8,128)S(1)}, u32[]{:S(2)}, u32[]{:S(2)}) %collective-permute-start.3) | collective-permute-done | bytes 393248 | tf_op jit(solution)/shard_map/while/body/eval_jaxpr/ppermute | solution.py:20
  171.7 5.8 %collective-permute-start.2 = (f32[2,192,256]{2,1,0:T(8,128)S(1)}, f32[2,192,256]{2,1,0:T(8,128)S(1)}, u32[]{:S(2)}, u32[]{:S(2)}) collective-permute-start(f32[2,192,256]{2,1,0:T(8,128)S(1)} %get-tuple-element.544), channel_id=1, source_target_pairs={{0,1},{1,2},{2,3},{3,4},{4,5},{5,6},{6,7},{8,9},{9,10},{10,11},{11... | collective-permute-start | bytes 1179656 | tf_op jit(solution)/shard_map/while/body/eval_jaxpr/ppermute | solution.py:18
  178.8 4.4 %collective-permute-done.2 = f32[2,192,256]{2,1,0:T(8,128)S(1)} collective-permute-done((f32[2,192,256]{2,1,0:T(8,128)S(1)}, f32[2,192,256]{2,1,0:T(8,128)S(1)}, u32[]{:S(2)}, u32[]{:S(2)}) %collective-permute-start.2) | collective-permute-done | bytes 393248 | tf_op jit(solution)/shard_map/while/body/eval_jaxpr/ppermute | solution.py:18
  183.3 13.4 %collective-permute-done.3 = f32[2,192,256]{2,1,0:T(8,128)S(1)} collective-permute-done((f32[2,192,256]{2,1,0:T(8,128)S(1)}, f32[2,192,256]{2,1,0:T(8,128)S(1)}, u32[]{:S(2)}, u32[]{:S(2)}) %collective-permute-start.3) | collective-permute-done | bytes 393248 | tf_op jit(solution)/shard_map/while/body/eval_jaxpr/ppermute | solution.py:20
  199.0 4.6 %collective-permute-start.2 = (f32[2,192,256]{2,1,0:T(8,128)S(1)}, f32[2,192,256]{2,1,0:T(8,128)S(1)}, u32[]{:S(2)}, u32[]{:S(2)}) collective-permute-start(f32[2,192,256]{2,1,0:T(8,128)S(1)} %get-tuple-element.544), channel_id=1, source_target_pairs={{0,1},{1,2},{2,3},{3,4},{4,5},{5,6},{6,7},{8,9},{9,10},{10,11},{11... | collective-permute-start | bytes 1179656 | tf_op jit(solution)/shard_map/while/body/eval_jaxpr/ppermute | solution.py:18
  204.9 6.1 %collective-permute-done.2 = f32[2,192,256]{2,1,0:T(8,128)S(1)} collective-permute-done((f32[2,192,256]{2,1,0:T(8,128)S(1)}, f32[2,192,256]{2,1,0:T(8,128)S(1)}, u32[]{:S(2)}, u32[]{:S(2)}) %collective-permute-start.2) | collective-permute-done | bytes 393248 | tf_op jit(solution)/shard_map/while/body/eval_jaxpr/ppermute | solution.py:18
  211.1 10.1 %collective-permute-done.3 = f32[2,192,256]{2,1,0:T(8,128)S(1)} collective-permute-done((f32[2,192,256]{2,1,0:T(8,128)S(1)}, f32[2,192,256]{2,1,0:T(8,128)S(1)}, u32[]{:S(2)}, u32[]{:S(2)}) %collective-permute-start.3) | collective-permute-done | bytes 393248 | tf_op jit(solution)/shard_map/while/body/eval_jaxpr/ppermute | solution.py:20
  223.5 4.6 %collective-permute-start.2 = (f32[2,192,256]{2,1,0:T(8,128)S(1)}, f32[2,192,256]{2,1,0:T(8,128)S(1)}, u32[]{:S(2)}, u32[]{:S(2)}) collective-permute-start(f32[2,192,256]{2,1,0:T(8,128)S(1)} %get-tuple-element.544), channel_id=1, source_target_pairs={{0,1},{1,2},{2,3},{3,4},{4,5},{5,6},{6,7},{8,9},{9,10},{10,11},{11... | collective-permute-start | bytes 1179656 | tf_op jit(solution)/shard_map/while/body/eval_jaxpr/ppermute | solution.py:18
  229.4 6.0 %collective-permute-done.2 = f32[2,192,256]{2,1,0:T(8,128)S(1)} collective-permute-done((f32[2,192,256]{2,1,0:T(8,128)S(1)}, f32[2,192,256]{2,1,0:T(8,128)S(1)}, u32[]{:S(2)}, u32[]{:S(2)}) %collective-permute-start.2) | collective-permute-done | bytes 393248 | tf_op jit(solution)/shard_map/while/body/eval_jaxpr/ppermute | solution.py:18
  235.6 10.2 %collective-permute-done.3 = f32[2,192,256]{2,1,0:T(8,128)S(1)} collective-permute-done((f32[2,192,256]{2,1,0:T(8,128)S(1)}, f32[2,192,256]{2,1,0:T(8,128)S(1)}, u32[]{:S(2)}, u32[]{:S(2)}) %collective-permute-start.3) | collective-permute-done | bytes 393248 | tf_op jit(solution)/shard_map/while/body/eval_jaxpr/ppermute | solution.py:20
  248.1 4.6 %collective-permute-start.2 = (f32[2,192,256]{2,1,0:T(8,128)S(1)}, f32[2,192,256]{2,1,0:T(8,128)S(1)}, u32[]{:S(2)}, u32[]{:S(2)}) collective-permute-start(f32[2,192,256]{2,1,0:T(8,128)S(1)} %get-tuple-element.544), channel_id=1, source_target_pairs={{0,1},{1,2},{2,3},{3,4},{4,5},{5,6},{6,7},{8,9},{9,10},{10,11},{11... | collective-permute-start | bytes 1179656 | tf_op jit(solution)/shard_map/while/body/eval_jaxpr/ppermute | solution.py:18
  254.0 6.0 %collective-permute-done.2 = f32[2,192,256]{2,1,0:T(8,128)S(1)} collective-permute-done((f32[2,192,256]{2,1,0:T(8,128)S(1)}, f32[2,192,256]{2,1,0:T(8,128)S(1)}, u32[]{:S(2)}, u32[]{:S(2)}) %collective-permute-start.2) | collective-permute-done | bytes 393248 | tf_op jit(solution)/shard_map/while/body/eval_jaxpr/ppermute | solution.py:18
  260.1 10.2 %collective-permute-done.3 = f32[2,192,256]{2,1,0:T(8,128)S(1)} collective-permute-done((f32[2,192,256]{2,1,0:T(8,128)S(1)}, f32[2,192,256]{2,1,0:T(8,128)S(1)}, u32[]{:S(2)}, u32[]{:S(2)}) %collective-permute-start.3) | collective-permute-done | bytes 393248 | tf_op jit(solution)/shard_map/while/body/eval_jaxpr/ppermute | solution.py:20
  272.6 4.6 %collective-permute-start.2 = (f32[2,192,256]{2,1,0:T(8,128)S(1)}, f32[2,192,256]{2,1,0:T(8,128)S(1)}, u32[]{:S(2)}, u32[]{:S(2)}) collective-permute-start(f32[2,192,256]{2,1,0:T(8,128)S(1)} %get-tuple-element.544), channel_id=1, source_target_pairs={{0,1},{1,2},{2,3},{3,4},{4,5},{5,6},{6,7},{8,9},{9,10},{10,11},{11... | collective-permute-start | bytes 1179656 | tf_op jit(solution)/shard_map/while/body/eval_jaxpr/ppermute | solution.py:18
  278.5 6.0 %collective-permute-done.2 = f32[2,192,256]{2,1,0:T(8,128)S(1)} collective-permute-done((f32[2,192,256]{2,1,0:T(8,128)S(1)}, f32[2,192,256]{2,1,0:T(8,128)S(1)}, u32[]{:S(2)}, u32[]{:S(2)}) %collective-permute-start.2) | collective-permute-done | bytes 393248 | tf_op jit(solution)/shard_map/while/body/eval_jaxpr/ppermute | solution.py:18
  284.7 10.2 %collective-permute-done.3 = f32[2,192,256]{2,1,0:T(8,128)S(1)} collective-permute-done((f32[2,192,256]{2,1,0:T(8,128)S(1)}, f32[2,192,256]{2,1,0:T(8,128)S(1)}, u32[]{:S(2)}, u32[]{:S(2)}) %collective-permute-start.3) | collective-permute-done | bytes 393248 | tf_op jit(solution)/shard_map/while/body/eval_jaxpr/ppermute | solution.py:20
  297.1 4.6 %collective-permute-start.2 = (f32[2,192,256]{2,1,0:T(8,128)S(1)}, f32[2,192,256]{2,1,0:T(8,128)S(1)}, u32[]{:S(2)}, u32[]{:S(2)}) collective-permute-start(f32[2,192,256]{2,1,0:T(8,128)S(1)} %get-tuple-element.544), channel_id=1, source_target_pairs={{0,1},{1,2},{2,3},{3,4},{4,5},{5,6},{6,7},{8,9},{9,10},{10,11},{11... | collective-permute-start | bytes 1179656 | tf_op jit(solution)/shard_map/while/body/eval_jaxpr/ppermute | solution.py:18
  303.0 6.0 %collective-permute-done.2 = f32[2,192,256]{2,1,0:T(8,128)S(1)} collective-permute-done((f32[2,192,256]{2,1,0:T(8,128)S(1)}, f32[2,192,256]{2,1,0:T(8,128)S(1)}, u32[]{:S(2)}, u32[]{:S(2)}) %collective-permute-start.2) | collective-permute-done | bytes 393248 | tf_op jit(solution)/shard_map/while/body/eval_jaxpr/ppermute | solution.py:18
  309.2 10.2 %collective-permute-done.3 = f32[2,192,256]{2,1,0:T(8,128)S(1)} collective-permute-done((f32[2,192,256]{2,1,0:T(8,128)S(1)}, f32[2,192,256]{2,1,0:T(8,128)S(1)}, u32[]{:S(2)}, u32[]{:S(2)}) %collective-permute-start.3) | collective-permute-done | bytes 393248 | tf_op jit(solution)/shard_map/while/body/eval_jaxpr/ppermute | solution.py:20
  321.7 4.6 %collective-permute-start.2 = (f32[2,192,256]{2,1,0:T(8,128)S(1)}, f32[2,192,256]{2,1,0:T(8,128)S(1)}, u32[]{:S(2)}, u32[]{:S(2)}) collective-permute-start(f32[2,192,256]{2,1,0:T(8,128)S(1)} %get-tuple-element.544), channel_id=1, source_target_pairs={{0,1},{1,2},{2,3},{3,4},{4,5},{5,6},{6,7},{8,9},{9,10},{10,11},{11... | collective-permute-start | bytes 1179656 | tf_op jit(solution)/shard_map/while/body/eval_jaxpr/ppermute | solution.py:18
  327.6 3.9 collective-permute-done.2
  331.6 9.0 %collective-permute-done.3 = f32[2,192,256]{2,1,0:T(8,128)S(1)} collective-permute-done((f32[2,192,256]{2,1,0:T(8,128)S(1)}, f32[2,192,256]{2,1,0:T(8,128)S(1)}, u32[]{:S(2)}, u32[]{:S(2)}) %collective-permute-start.3) | collective-permute-done | bytes 393248 | tf_op jit(solution)/shard_map/while/body/eval_jaxpr/ppermute | solution.py:20
  343.9 1.3 collective-permute-start.11
  345.3 1.3 collective-permute-done.11
  346.6 13.9 %reduce_sum.78 = f32[96,2,128,2]{3,2,1,0:T(8,128)} reshape(f32[192,256]{1,0:T(8,128)S(1)} %select_reduce_fusion) | data formatting | bytes 393216 | tf_op jit(solution)/shard_map/reduce_sum | solution.py:50
  360.5 6.3 %reduce_sum.79 = f32[96,128]{1,0:T(8,128)S(1)} reduce(f32[96,2,128,2]{3,2,1,0:T(8,128)} %reduce_sum.78, f32[]{:T(128)} %constant.239.clone.1), dimensions={1,3}, to_apply=%region_13.14 | reduce | flops 36864 | bytes 245764 | tf_op jit(solution)/shard_map/reduce_sum | solution.py:50
  366.8 40.3 %while.64 = (s32[]{:T(128)}, f32[1,96,128]{2,1,0:T(8,128)S(1)}, pred[1]{0:T(512)(128)(4,1)}, f32[3,96,128]{2,1,0:T(8,128)S(1)}, s32[]{:T(128)}) while((s32[]{:T(128)}, f32[1,96,128]{2,1,0:T(8,128)S(1)}, pred[1]{0:T(512)(128)(4,1)}, f32[3,96,128]{2,1,0:T(8,128)S(1)}, s32[]{:T(128)}) %tuple.167), condition=%wide.region_15.16_spmd, body=%wide.region_14.15_spmd.sunk | while | flops 331778 | bytes 1228942 | solution.py:71
  366.8 4.8 %collective-permute-start.6 = (f32[1,96,128]{2,1,0:T(8,128)S(1)}, f32[1,96,128]{2,1,0:T(8,128)S(1)}, u32[]{:S(2)}, u32[]{:S(2)}) collective-permute-start(f32[1,96,128]{2,1,0:T(8,128)S(1)} %get-tuple-element.578), channel_id=1, source_target_pairs={{0,1},{1,2},{2,3},{3,4},{4,5},{5,6},{6,7},{8,9},{9,10},{10,11},{11... | collective-permute-start | bytes 147464 | tf_op jit(solution)/shard_map/while/body/eval_jaxpr/ppermute | solution.py:18
  373.4 4.5 %collective-permute-done.7 = f32[1,96,128]{2,1,0:T(8,128)S(1)} collective-permute-done((f32[1,96,128]{2,1,0:T(8,128)S(1)}, f32[1,96,128]{2,1,0:T(8,128)S(1)}, u32[]{:S(2)}, u32[]{:S(2)}) %collective-permute-start.7) | collective-permute-done | bytes 49184 | tf_op jit(solution)/shard_map/while/body/eval_jaxpr/ppermute | solution.py:20
  378.1 4.8 %collective-permute-start.6 = (f32[1,96,128]{2,1,0:T(8,128)S(1)}, f32[1,96,128]{2,1,0:T(8,128)S(1)}, u32[]{:S(2)}, u32[]{:S(2)}) collective-permute-start(f32[1,96,128]{2,1,0:T(8,128)S(1)} %get-tuple-element.578), channel_id=1, source_target_pairs={{0,1},{1,2},{2,3},{3,4},{4,5},{5,6},{6,7},{8,9},{9,10},{10,11},{11... | collective-permute-start | bytes 147464 | tf_op jit(solution)/shard_map/while/body/eval_jaxpr/ppermute | solution.py:18
  384.6 4.3 %collective-permute-done.7 = f32[1,96,128]{2,1,0:T(8,128)S(1)} collective-permute-done((f32[1,96,128]{2,1,0:T(8,128)S(1)}, f32[1,96,128]{2,1,0:T(8,128)S(1)}, u32[]{:S(2)}, u32[]{:S(2)}) %collective-permute-start.7) | collective-permute-done | bytes 49184 | tf_op jit(solution)/shard_map/while/body/eval_jaxpr/ppermute | solution.py:20
  389.0 2.8 collective-permute-start.6
  393.8 4.0 collective-permute-done.7
  397.9 3.1 collective-permute-start.6
  402.8 4.3 %collective-permute-done.7 = f32[1,96,128]{2,1,0:T(8,128)S(1)} collective-permute-done((f32[1,96,128]{2,1,0:T(8,128)S(1)}, f32[1,96,128]{2,1,0:T(8,128)S(1)}, u32[]{:S(2)}, u32[]{:S(2)}) %collective-permute-start.7) | collective-permute-done | bytes 49184 | tf_op jit(solution)/shard_map/while/body/eval_jaxpr/ppermute | solution.py:20
  (252 shorter events, 59.5 us)
Async XLA Ops:
  15.0 6.4 %copy-start = (f32[2,192,256]{2,1,0:T(8,128)S(1)}, f32[2,192,256]{2,1,0:T(8,128)}, u32[]{:S(2)}) copy-start(f32[2,192,256]{2,1,0:T(8,128)} %param.11) | copy-start | bytes 1179652
  41.6 6.6 %collective-permute-start = (f32[1,96,128]{2,1,0:T(8,128)S(1)}, f32[1,96,128]{2,1,0:T(8,128)S(1)}, u32[]{:S(2)}, u32[]{:S(2)}) collective-permute-start(f32[1,96,128]{2,1,0:T(8,128)S(1)} %get-tuple-element.527), channel_id=1, source_target_pairs={{0,1},{1,2},{2,3},{3,4},{4,5},{5,6},{6,7},{8,9},{9,10},{10,11},{11... | collective-permute-start | bytes 147464 | tf_op jit(solution)/shard_map/while/body/eval_jaxpr/ppermute | solution.py:18
  46.5 6.0 %collective-permute-start.1 = (f32[1,96,128]{2,1,0:T(8,128)S(1)}, f32[1,96,128]{2,1,0:T(8,128)S(1)}, u32[]{:S(2)}, u32[]{:S(2)}) collective-permute-start(f32[1,96,128]{2,1,0:T(8,128)S(1)} %get-tuple-element.527), channel_id=1, source_target_pairs={{1,0},{2,1},{3,2},{4,3},{5,4},{6,5},{7,6},{9,8},{10,9},{11,10},{12... | collective-permute-start | bytes 147464 | tf_op jit(solution)/shard_map/while/body/eval_jaxpr/ppermute | solution.py:20
  52.6 6.1 %collective-permute-start = (f32[1,96,128]{2,1,0:T(8,128)S(1)}, f32[1,96,128]{2,1,0:T(8,128)S(1)}, u32[]{:S(2)}, u32[]{:S(2)}) collective-permute-start(f32[1,96,128]{2,1,0:T(8,128)S(1)} %get-tuple-element.527), channel_id=1, source_target_pairs={{0,1},{1,2},{2,3},{3,4},{4,5},{5,6},{6,7},{8,9},{9,10},{10,11},{11... | collective-permute-start | bytes 147464 | tf_op jit(solution)/shard_map/while/body/eval_jaxpr/ppermute | solution.py:18
  56.9 6.0 %collective-permute-start.1 = (f32[1,96,128]{2,1,0:T(8,128)S(1)}, f32[1,96,128]{2,1,0:T(8,128)S(1)}, u32[]{:S(2)}, u32[]{:S(2)}) collective-permute-start(f32[1,96,128]{2,1,0:T(8,128)S(1)} %get-tuple-element.527), channel_id=1, source_target_pairs={{1,0},{2,1},{3,2},{4,3},{5,4},{6,5},{7,6},{9,8},{10,9},{11,10},{12... | collective-permute-start | bytes 147464 | tf_op jit(solution)/shard_map/while/body/eval_jaxpr/ppermute | solution.py:20
  63.1 5.6 %collective-permute-start = (f32[1,96,128]{2,1,0:T(8,128)S(1)}, f32[1,96,128]{2,1,0:T(8,128)S(1)}, u32[]{:S(2)}, u32[]{:S(2)}) collective-permute-start(f32[1,96,128]{2,1,0:T(8,128)S(1)} %get-tuple-element.527), channel_id=1, source_target_pairs={{0,1},{1,2},{2,3},{3,4},{4,5},{5,6},{6,7},{8,9},{9,10},{10,11},{11... | collective-permute-start | bytes 147464 | tf_op jit(solution)/shard_map/while/body/eval_jaxpr/ppermute | solution.py:18
  66.5 6.0 %collective-permute-start.1 = (f32[1,96,128]{2,1,0:T(8,128)S(1)}, f32[1,96,128]{2,1,0:T(8,128)S(1)}, u32[]{:S(2)}, u32[]{:S(2)}) collective-permute-start(f32[1,96,128]{2,1,0:T(8,128)S(1)} %get-tuple-element.527), channel_id=1, source_target_pairs={{1,0},{2,1},{3,2},{4,3},{5,4},{6,5},{7,6},{9,8},{10,9},{11,10},{12... | collective-permute-start | bytes 147464 | tf_op jit(solution)/shard_map/while/body/eval_jaxpr/ppermute | solution.py:20
  72.6 6.1 %collective-permute-start = (f32[1,96,128]{2,1,0:T(8,128)S(1)}, f32[1,96,128]{2,1,0:T(8,128)S(1)}, u32[]{:S(2)}, u32[]{:S(2)}) collective-permute-start(f32[1,96,128]{2,1,0:T(8,128)S(1)} %get-tuple-element.527), channel_id=1, source_target_pairs={{0,1},{1,2},{2,3},{3,4},{4,5},{5,6},{6,7},{8,9},{9,10},{10,11},{11... | collective-permute-start | bytes 147464 | tf_op jit(solution)/shard_map/while/body/eval_jaxpr/ppermute | solution.py:18
  76.9 6.0 %collective-permute-start.1 = (f32[1,96,128]{2,1,0:T(8,128)S(1)}, f32[1,96,128]{2,1,0:T(8,128)S(1)}, u32[]{:S(2)}, u32[]{:S(2)}) collective-permute-start(f32[1,96,128]{2,1,0:T(8,128)S(1)} %get-tuple-element.527), channel_id=1, source_target_pairs={{1,0},{2,1},{3,2},{4,3},{5,4},{6,5},{7,6},{9,8},{10,9},{11,10},{12... | collective-permute-start | bytes 147464 | tf_op jit(solution)/shard_map/while/body/eval_jaxpr/ppermute | solution.py:20
  83.0 8.6 %copy-start.1 = (f32[2,192,256]{2,1,0:T(8,128)S(1)}, f32[2,192,256]{2,1,0:T(8,128)}, u32[]{:S(2)}) copy-start(f32[2,192,256]{2,1,0:T(8,128)} %param.10) | copy-start | bytes 1179652
  83.6 22.0 %copy-start.2 = (f32[192,256]{1,0:T(8,128)}, f32[192,256]{1,0:T(8,128)S(1)}, u32[]{:S(2)}) copy-start(f32[192,256]{1,0:T(8,128)S(1)} %copy.10) | copy-start | bytes 589828
  83.6 8.0 %collective-permute-start.8 = (f32[2,192,256]{2,1,0:T(8,128)S(1)}, f32[2,192,256]{2,1,0:T(8,128)S(1)}, u32[]{:S(2)}, u32[]{:S(2)}) collective-permute-start(f32[2,192,256]{2,1,0:T(8,128)S(1)} %broadcast_in_dim.139), channel_id=1, source_target_pairs={{0,8},{1,9},{2,10},{3,11},{4,12},{5,13},{6,14},{7,15},{16,24},{17,... | collective-permute-start | bytes 1179656 | tf_op jit(solution)/shard_map/ppermute | solution.py:30
  85.0 67.2 %collective-permute-start.10 = (f32[2,192,256]{2,1,0:T(8,128)S(1)}, f32[2,192,256]{2,1,0:T(8,128)S(1)}, u32[]{:S(2)}, u32[]{:S(2)}) collective-permute-start(f32[2,192,256]{2,1,0:T(8,128)S(1)} %copy-done), channel_id=1, source_target_pairs={{1,0},{2,1},{3,2},{4,3},{5,4},{6,5},{7,6},{9,8},{10,9},{11,10},{12... | collective-permute-start | bytes 1179656 | tf_op jit(solution)/shard_map/ppermute | solution.py:20
  86.3 66.6 %collective-permute-start.9 = (f32[2,192,256]{2,1,0:T(8,128)S(1)}, f32[2,192,256]{2,1,0:T(8,128)}, u32[]{:S(2)}, u32[]{:S(2)}) collective-permute-start(f32[2,192,256]{2,1,0:T(8,128)S(1)} %copy-done), channel_id=1, source_target_pairs={{0,1},{1,2},{2,3},{3,4},{4,5},{5,6},{6,7},{8,9},{9,10},{10,11},{11... | collective-permute-start | bytes 1179656 | tf_op jit(solution)/shard_map/ppermute | solution.py:18
  111.9 5.5 %collective-permute-start.4 = (f32[1,96,128]{2,1,0:T(8,128)S(1)}, f32[1,96,128]{2,1,0:T(8,128)S(1)}, u32[]{:S(2)}, u32[]{:S(2)}) collective-permute-start(f32[1,96,128]{2,1,0:T(8,128)S(1)} %get-tuple-element.563), channel_id=1, source_target_pairs={{0,1},{1,2},{2,3},{3,4},{4,5},{5,6},{6,7},{8,9},{9,10},{10,11},{11... | collective-permute-start | bytes 147464 | tf_op jit(solution)/shard_map/while/body/eval_jaxpr/ppermute | solution.py:18
  115.6 6.0 %collective-permute-start.5 = (f32[1,96,128]{2,1,0:T(8,128)S(1)}, f32[1,96,128]{2,1,0:T(8,128)S(1)}, u32[]{:S(2)}, u32[]{:S(2)}) collective-permute-start(f32[1,96,128]{2,1,0:T(8,128)S(1)} %get-tuple-element.563), channel_id=1, source_target_pairs={{1,0},{2,1},{3,2},{4,3},{5,4},{6,5},{7,6},{9,8},{10,9},{11,10},{12... | collective-permute-start | bytes 147464 | tf_op jit(solution)/shard_map/while/body/eval_jaxpr/ppermute | solution.py:20
  121.7 5.2 %collective-permute-start.4 = (f32[1,96,128]{2,1,0:T(8,128)S(1)}, f32[1,96,128]{2,1,0:T(8,128)S(1)}, u32[]{:S(2)}, u32[]{:S(2)}) collective-permute-start(f32[1,96,128]{2,1,0:T(8,128)S(1)} %get-tuple-element.563), channel_id=1, source_target_pairs={{0,1},{1,2},{2,3},{3,4},{4,5},{5,6},{6,7},{8,9},{9,10},{10,11},{11... | collective-permute-start | bytes 147464 | tf_op jit(solution)/shard_map/while/body/eval_jaxpr/ppermute | solution.py:18
  125.2 6.0 %collective-permute-start.5 = (f32[1,96,128]{2,1,0:T(8,128)S(1)}, f32[1,96,128]{2,1,0:T(8,128)S(1)}, u32[]{:S(2)}, u32[]{:S(2)}) collective-permute-start(f32[1,96,128]{2,1,0:T(8,128)S(1)} %get-tuple-element.563), channel_id=1, source_target_pairs={{1,0},{2,1},{3,2},{4,3},{5,4},{6,5},{7,6},{9,8},{10,9},{11,10},{12... | collective-permute-start | bytes 147464 | tf_op jit(solution)/shard_map/while/body/eval_jaxpr/ppermute | solution.py:20
  131.3 6.4 %collective-permute-start.4 = (f32[1,96,128]{2,1,0:T(8,128)S(1)}, f32[1,96,128]{2,1,0:T(8,128)S(1)}, u32[]{:S(2)}, u32[]{:S(2)}) collective-permute-start(f32[1,96,128]{2,1,0:T(8,128)S(1)} %get-tuple-element.563), channel_id=1, source_target_pairs={{0,1},{1,2},{2,3},{3,4},{4,5},{5,6},{6,7},{8,9},{9,10},{10,11},{11... | collective-permute-start | bytes 147464 | tf_op jit(solution)/shard_map/while/body/eval_jaxpr/ppermute | solution.py:18
  136.0 6.0 %collective-permute-start.5 = (f32[1,96,128]{2,1,0:T(8,128)S(1)}, f32[1,96,128]{2,1,0:T(8,128)S(1)}, u32[]{:S(2)}, u32[]{:S(2)}) collective-permute-start(f32[1,96,128]{2,1,0:T(8,128)S(1)} %get-tuple-element.563), channel_id=1, source_target_pairs={{1,0},{2,1},{3,2},{4,3},{5,4},{6,5},{7,6},{9,8},{10,9},{11,10},{12... | collective-permute-start | bytes 147464 | tf_op jit(solution)/shard_map/while/body/eval_jaxpr/ppermute | solution.py:20
  142.1 4.7 %collective-permute-start.4 = (f32[1,96,128]{2,1,0:T(8,128)S(1)}, f32[1,96,128]{2,1,0:T(8,128)S(1)}, u32[]{:S(2)}, u32[]{:S(2)}) collective-permute-start(f32[1,96,128]{2,1,0:T(8,128)S(1)} %get-tuple-element.563), channel_id=1, source_target_pairs={{0,1},{1,2},{2,3},{3,4},{4,5},{5,6},{6,7},{8,9},{9,10},{10,11},{11... | collective-permute-start | bytes 147464 | tf_op jit(solution)/shard_map/while/body/eval_jaxpr/ppermute | solution.py:18
  145.0 6.5 %collective-permute-start.5 = (f32[1,96,128]{2,1,0:T(8,128)S(1)}, f32[1,96,128]{2,1,0:T(8,128)S(1)}, u32[]{:S(2)}, u32[]{:S(2)}) collective-permute-start(f32[1,96,128]{2,1,0:T(8,128)S(1)} %get-tuple-element.563), channel_id=1, source_target_pairs={{1,0},{2,1},{3,2},{4,3},{5,4},{6,5},{7,6},{9,8},{10,9},{11,10},{12... | collective-permute-start | bytes 147464 | tf_op jit(solution)/shard_map/while/body/eval_jaxpr/ppermute | solution.py:20
  152.2 0.7 copy-start.3
  154.1 9.2 %collective-permute-start.2 = (f32[2,192,256]{2,1,0:T(8,128)S(1)}, f32[2,192,256]{2,1,0:T(8,128)S(1)}, u32[]{:S(2)}, u32[]{:S(2)}) collective-permute-start(f32[2,192,256]{2,1,0:T(8,128)S(1)} %get-tuple-element.544), channel_id=1, source_target_pairs={{0,1},{1,2},{2,3},{3,4},{4,5},{5,6},{6,7},{8,9},{9,10},{10,11},{11... | collective-permute-start | bytes 1179656 | tf_op jit(solution)/shard_map/while/body/eval_jaxpr/ppermute | solution.py:18
  157.6 11.8 %collective-permute-start.3 = (f32[2,192,256]{2,1,0:T(8,128)S(1)}, f32[2,192,256]{2,1,0:T(8,128)S(1)}, u32[]{:S(2)}, u32[]{:S(2)}) collective-permute-start(f32[2,192,256]{2,1,0:T(8,128)S(1)} %get-tuple-element.544), channel_id=1, source_target_pairs={{1,0},{2,1},{3,2},{4,3},{5,4},{6,5},{7,6},{9,8},{10,9},{11,10},{12... | collective-permute-start | bytes 1179656 | tf_op jit(solution)/shard_map/while/body/eval_jaxpr/ppermute | solution.py:20
  171.7 11.5 %collective-permute-start.2 = (f32[2,192,256]{2,1,0:T(8,128)S(1)}, f32[2,192,256]{2,1,0:T(8,128)S(1)}, u32[]{:S(2)}, u32[]{:S(2)}) collective-permute-start(f32[2,192,256]{2,1,0:T(8,128)S(1)} %get-tuple-element.544), channel_id=1, source_target_pairs={{0,1},{1,2},{2,3},{3,4},{4,5},{5,6},{6,7},{8,9},{9,10},{10,11},{11... | collective-permute-start | bytes 1179656 | tf_op jit(solution)/shard_map/while/body/eval_jaxpr/ppermute | solution.py:18
  177.5 19.2 %collective-permute-start.3 = (f32[2,192,256]{2,1,0:T(8,128)S(1)}, f32[2,192,256]{2,1,0:T(8,128)S(1)}, u32[]{:S(2)}, u32[]{:S(2)}) collective-permute-start(f32[2,192,256]{2,1,0:T(8,128)S(1)} %get-tuple-element.544), channel_id=1, source_target_pairs={{1,0},{2,1},{3,2},{4,3},{5,4},{6,5},{7,6},{9,8},{10,9},{11,10},{12... | collective-permute-start | bytes 1179656 | tf_op jit(solution)/shard_map/while/body/eval_jaxpr/ppermute | solution.py:20
  199.0 12.0 %collective-permute-start.2 = (f32[2,192,256]{2,1,0:T(8,128)S(1)}, f32[2,192,256]{2,1,0:T(8,128)S(1)}, u32[]{:S(2)}, u32[]{:S(2)}) collective-permute-start(f32[2,192,256]{2,1,0:T(8,128)S(1)} %get-tuple-element.544), channel_id=1, source_target_pairs={{0,1},{1,2},{2,3},{3,4},{4,5},{5,6},{6,7},{8,9},{9,10},{10,11},{11... | collective-permute-start | bytes 1179656 | tf_op jit(solution)/shard_map/while/body/eval_jaxpr/ppermute | solution.py:18
  203.5 17.7 %collective-permute-start.3 = (f32[2,192,256]{2,1,0:T(8,128)S(1)}, f32[2,192,256]{2,1,0:T(8,128)S(1)}, u32[]{:S(2)}, u32[]{:S(2)}) collective-permute-start(f32[2,192,256]{2,1,0:T(8,128)S(1)} %get-tuple-element.544), channel_id=1, source_target_pairs={{1,0},{2,1},{3,2},{4,3},{5,4},{6,5},{7,6},{9,8},{10,9},{11,10},{12... | collective-permute-start | bytes 1179656 | tf_op jit(solution)/shard_map/while/body/eval_jaxpr/ppermute | solution.py:20
  223.5 11.9 %collective-permute-start.2 = (f32[2,192,256]{2,1,0:T(8,128)S(1)}, f32[2,192,256]{2,1,0:T(8,128)S(1)}, u32[]{:S(2)}, u32[]{:S(2)}) collective-permute-start(f32[2,192,256]{2,1,0:T(8,128)S(1)} %get-tuple-element.544), channel_id=1, source_target_pairs={{0,1},{1,2},{2,3},{3,4},{4,5},{5,6},{6,7},{8,9},{9,10},{10,11},{11... | collective-permute-start | bytes 1179656 | tf_op jit(solution)/shard_map/while/body/eval_jaxpr/ppermute | solution.py:18
  228.1 17.7 %collective-permute-start.3 = (f32[2,192,256]{2,1,0:T(8,128)S(1)}, f32[2,192,256]{2,1,0:T(8,128)S(1)}, u32[]{:S(2)}, u32[]{:S(2)}) collective-permute-start(f32[2,192,256]{2,1,0:T(8,128)S(1)} %get-tuple-element.544), channel_id=1, source_target_pairs={{1,0},{2,1},{3,2},{4,3},{5,4},{6,5},{7,6},{9,8},{10,9},{11,10},{12... | collective-permute-start | bytes 1179656 | tf_op jit(solution)/shard_map/while/body/eval_jaxpr/ppermute | solution.py:20
  248.1 11.9 %collective-permute-start.2 = (f32[2,192,256]{2,1,0:T(8,128)S(1)}, f32[2,192,256]{2,1,0:T(8,128)S(1)}, u32[]{:S(2)}, u32[]{:S(2)}) collective-permute-start(f32[2,192,256]{2,1,0:T(8,128)S(1)} %get-tuple-element.544), channel_id=1, source_target_pairs={{0,1},{1,2},{2,3},{3,4},{4,5},{5,6},{6,7},{8,9},{9,10},{10,11},{11... | collective-permute-start | bytes 1179656 | tf_op jit(solution)/shard_map/while/body/eval_jaxpr/ppermute | solution.py:18
  252.6 17.7 %collective-permute-start.3 = (f32[2,192,256]{2,1,0:T(8,128)S(1)}, f32[2,192,256]{2,1,0:T(8,128)S(1)}, u32[]{:S(2)}, u32[]{:S(2)}) collective-permute-start(f32[2,192,256]{2,1,0:T(8,128)S(1)} %get-tuple-element.544), channel_id=1, source_target_pairs={{1,0},{2,1},{3,2},{4,3},{5,4},{6,5},{7,6},{9,8},{10,9},{11,10},{12... | collective-permute-start | bytes 1179656 | tf_op jit(solution)/shard_map/while/body/eval_jaxpr/ppermute | solution.py:20
  272.6 11.9 %collective-permute-start.2 = (f32[2,192,256]{2,1,0:T(8,128)S(1)}, f32[2,192,256]{2,1,0:T(8,128)S(1)}, u32[]{:S(2)}, u32[]{:S(2)}) collective-permute-start(f32[2,192,256]{2,1,0:T(8,128)S(1)} %get-tuple-element.544), channel_id=1, source_target_pairs={{0,1},{1,2},{2,3},{3,4},{4,5},{5,6},{6,7},{8,9},{9,10},{10,11},{11... | collective-permute-start | bytes 1179656 | tf_op jit(solution)/shard_map/while/body/eval_jaxpr/ppermute | solution.py:18
  277.2 17.7 %collective-permute-start.3 = (f32[2,192,256]{2,1,0:T(8,128)S(1)}, f32[2,192,256]{2,1,0:T(8,128)S(1)}, u32[]{:S(2)}, u32[]{:S(2)}) collective-permute-start(f32[2,192,256]{2,1,0:T(8,128)S(1)} %get-tuple-element.544), channel_id=1, source_target_pairs={{1,0},{2,1},{3,2},{4,3},{5,4},{6,5},{7,6},{9,8},{10,9},{11,10},{12... | collective-permute-start | bytes 1179656 | tf_op jit(solution)/shard_map/while/body/eval_jaxpr/ppermute | solution.py:20
  297.1 11.9 %collective-permute-start.2 = (f32[2,192,256]{2,1,0:T(8,128)S(1)}, f32[2,192,256]{2,1,0:T(8,128)S(1)}, u32[]{:S(2)}, u32[]{:S(2)}) collective-permute-start(f32[2,192,256]{2,1,0:T(8,128)S(1)} %get-tuple-element.544), channel_id=1, source_target_pairs={{0,1},{1,2},{2,3},{3,4},{4,5},{5,6},{6,7},{8,9},{9,10},{10,11},{11... | collective-permute-start | bytes 1179656 | tf_op jit(solution)/shard_map/while/body/eval_jaxpr/ppermute | solution.py:18
  301.7 17.7 %collective-permute-start.3 = (f32[2,192,256]{2,1,0:T(8,128)S(1)}, f32[2,192,256]{2,1,0:T(8,128)S(1)}, u32[]{:S(2)}, u32[]{:S(2)}) collective-permute-start(f32[2,192,256]{2,1,0:T(8,128)S(1)} %get-tuple-element.544), channel_id=1, source_target_pairs={{1,0},{2,1},{3,2},{4,3},{5,4},{6,5},{7,6},{9,8},{10,9},{11,10},{12... | collective-permute-start | bytes 1179656 | tf_op jit(solution)/shard_map/while/body/eval_jaxpr/ppermute | solution.py:20
  321.7 9.8 %collective-permute-start.2 = (f32[2,192,256]{2,1,0:T(8,128)S(1)}, f32[2,192,256]{2,1,0:T(8,128)S(1)}, u32[]{:S(2)}, u32[]{:S(2)}) collective-permute-start(f32[2,192,256]{2,1,0:T(8,128)S(1)} %get-tuple-element.544), channel_id=1, source_target_pairs={{0,1},{1,2},{2,3},{3,4},{4,5},{5,6},{6,7},{8,9},{9,10},{10,11},{11... | collective-permute-start | bytes 1179656 | tf_op jit(solution)/shard_map/while/body/eval_jaxpr/ppermute | solution.py:18
  326.2 14.4 %collective-permute-start.3 = (f32[2,192,256]{2,1,0:T(8,128)S(1)}, f32[2,192,256]{2,1,0:T(8,128)S(1)}, u32[]{:S(2)}, u32[]{:S(2)}) collective-permute-start(f32[2,192,256]{2,1,0:T(8,128)S(1)} %get-tuple-element.544), channel_id=1, source_target_pairs={{1,0},{2,1},{3,2},{4,3},{5,4},{6,5},{7,6},{9,8},{10,9},{11,10},{12... | collective-permute-start | bytes 1179656 | tf_op jit(solution)/shard_map/while/body/eval_jaxpr/ppermute | solution.py:20
  343.9 2.6 collective-permute-start.11
  366.8 6.6 %collective-permute-start.6 = (f32[1,96,128]{2,1,0:T(8,128)S(1)}, f32[1,96,128]{2,1,0:T(8,128)S(1)}, u32[]{:S(2)}, u32[]{:S(2)}) collective-permute-start(f32[1,96,128]{2,1,0:T(8,128)S(1)} %get-tuple-element.578), channel_id=1, source_target_pairs={{0,1},{1,2},{2,3},{3,4},{4,5},{5,6},{6,7},{8,9},{9,10},{10,11},{11... | collective-permute-start | bytes 147464 | tf_op jit(solution)/shard_map/while/body/eval_jaxpr/ppermute | solution.py:18
  371.7 6.3 %collective-permute-start.7 = (f32[1,96,128]{2,1,0:T(8,128)S(1)}, f32[1,96,128]{2,1,0:T(8,128)S(1)}, u32[]{:S(2)}, u32[]{:S(2)}) collective-permute-start(f32[1,96,128]{2,1,0:T(8,128)S(1)} %get-tuple-element.578), channel_id=1, source_target_pairs={{1,0},{2,1},{3,2},{4,3},{5,4},{6,5},{7,6},{9,8},{10,9},{11,10},{12... | collective-permute-start | bytes 147464 | tf_op jit(solution)/shard_map/while/body/eval_jaxpr/ppermute | solution.py:20
  378.1 6.6 %collective-permute-start.6 = (f32[1,96,128]{2,1,0:T(8,128)S(1)}, f32[1,96,128]{2,1,0:T(8,128)S(1)}, u32[]{:S(2)}, u32[]{:S(2)}) collective-permute-start(f32[1,96,128]{2,1,0:T(8,128)S(1)} %get-tuple-element.578), channel_id=1, source_target_pairs={{0,1},{1,2},{2,3},{3,4},{4,5},{5,6},{6,7},{8,9},{9,10},{10,11},{11... | collective-permute-start | bytes 147464 | tf_op jit(solution)/shard_map/while/body/eval_jaxpr/ppermute | solution.py:18
  382.9 6.0 %collective-permute-start.7 = (f32[1,96,128]{2,1,0:T(8,128)S(1)}, f32[1,96,128]{2,1,0:T(8,128)S(1)}, u32[]{:S(2)}, u32[]{:S(2)}) collective-permute-start(f32[1,96,128]{2,1,0:T(8,128)S(1)} %get-tuple-element.578), channel_id=1, source_target_pairs={{1,0},{2,1},{3,2},{4,3},{5,4},{6,5},{7,6},{9,8},{10,9},{11,10},{12... | collective-permute-start | bytes 147464 | tf_op jit(solution)/shard_map/while/body/eval_jaxpr/ppermute | solution.py:20
  389.0 4.8 %collective-permute-start.6 = (f32[1,96,128]{2,1,0:T(8,128)S(1)}, f32[1,96,128]{2,1,0:T(8,128)S(1)}, u32[]{:S(2)}, u32[]{:S(2)}) collective-permute-start(f32[1,96,128]{2,1,0:T(8,128)S(1)} %get-tuple-element.578), channel_id=1, source_target_pairs={{0,1},{1,2},{2,3},{3,4},{4,5},{5,6},{6,7},{8,9},{9,10},{10,11},{11... | collective-permute-start | bytes 147464 | tf_op jit(solution)/shard_map/while/body/eval_jaxpr/ppermute | solution.py:18
  391.8 6.0 %collective-permute-start.7 = (f32[1,96,128]{2,1,0:T(8,128)S(1)}, f32[1,96,128]{2,1,0:T(8,128)S(1)}, u32[]{:S(2)}, u32[]{:S(2)}) collective-permute-start(f32[1,96,128]{2,1,0:T(8,128)S(1)} %get-tuple-element.578), channel_id=1, source_target_pairs={{1,0},{2,1},{3,2},{4,3},{5,4},{6,5},{7,6},{9,8},{10,9},{11,10},{12... | collective-permute-start | bytes 147464 | tf_op jit(solution)/shard_map/while/body/eval_jaxpr/ppermute | solution.py:20
  397.9 4.8 %collective-permute-start.6 = (f32[1,96,128]{2,1,0:T(8,128)S(1)}, f32[1,96,128]{2,1,0:T(8,128)S(1)}, u32[]{:S(2)}, u32[]{:S(2)}) collective-permute-start(f32[1,96,128]{2,1,0:T(8,128)S(1)} %get-tuple-element.578), channel_id=1, source_target_pairs={{0,1},{1,2},{2,3},{3,4},{4,5},{5,6},{6,7},{8,9},{9,10},{10,11},{11... | collective-permute-start | bytes 147464 | tf_op jit(solution)/shard_map/while/body/eval_jaxpr/ppermute | solution.py:18
  401.0 6.0 %collective-permute-start.7 = (f32[1,96,128]{2,1,0:T(8,128)S(1)}, f32[1,96,128]{2,1,0:T(8,128)S(1)}, u32[]{:S(2)}, u32[]{:S(2)}) collective-permute-start(f32[1,96,128]{2,1,0:T(8,128)S(1)} %get-tuple-element.578), channel_id=1, source_target_pairs={{1,0},{2,1},{3,2},{4,3},{5,4},{6,5},{7,6},{9,8},{10,9},{11,10},{12... | collective-permute-start | bytes 147464 | tf_op jit(solution)/shard_map/while/body/eval_jaxpr/ppermute | solution.py:20
where the time goes:
time: 410 us; the launch traced here: 408 us
  waiting for transfers between devices  178 us (43%)
  starting transfers between devices  119 us (29%)
  local copies, waits for them, and re-layouts  68.7 us (17%)
  other arithmetic  40.8 us (10%)
    ppermute x21, waiting for transfers between devices, with_halo(): lax.ppermute(head, axis, [((i + 1) % count, i) for i in range(ends)])  130 us
    ppermute x21, starting transfers between devices, with_halo(): lax.ppermute(tail, axis, [(i, (i + 1) % count) for i in range(ends)])  89.1 us
    reduce_sum x4, local copies, waits for them, and re-layouts, restrict(): field.reshape(depth // 2, 2, rows // 2, 2, cols // 2, 2)  55.7 us
    ppermute x21, waiting for transfers between devices, with_halo(): lax.ppermute(tail, axis, [(i, (i + 1) % count) for i in range(ends)])  46.7 us
    ppermute x21, starting transfers between devices, with_halo(): lax.ppermute(head, axis, [((i + 1) % count, i) for i in range(ends)])  27.1 us
    reduce_sum x8, other arithmetic, restrict(): field.reshape(depth // 2, 2, rows // 2, 2, cols // 2, 2)  26.3 us
    select_n x28, other arithmetic, block_turn(): padded = jnp.where(inside[:, None, None], updated, 0.0)  11.3 us
  transfers between devices with their start and end apart: 44, of which 41 were waited for; matrix products, arithmetic and copies ran while one was open for 6% of the time, Pallas kernels for 0%

commit v1 on v0

--- a/solution.py
+++ b/solution.py
@@ -1,6 +1,10 @@
+import functools
+
 import jax
 import jax.numpy as jnp
 from jax import lax
+from jax.experimental import pallas as pl
+from jax.experimental.pallas import tpu as pltpu
 from jax.sharding import PartitionSpec as P
 
 FSTEPS = 16
@@ -134,7 +138,369 @@
     return result[None]
 
 
+F_CONST = (0.5, 0.1, 1.0)
+C_CONST = (2.0, 0.025, 0.5)
+HIGH = lax.Precision.HIGHEST
+OWN = 32
+EDGE = 16
+LANES = 128
+PAD = 8
+TURNS = (0, 4, 8, 12, 16, 40)
+
+
+def weights(step_len, diffusion, upwind_scale):
+    lead = step_len * diffusion
+    lag = step_len * upwind_scale
+    centre = (1.0 - 6.0 * lead - 0.35 * lag) / lead
+    lows = tuple((lead + lag * part) / lead for part in (0.13, 0.12, 0.10))
+    return lead, centre, step_len / lead, lows
+
+
+def iota(shape, dim):
+    return lax.broadcasted_iota(jnp.int32, shape, dim)
+
+
+def lanes_in(rows, first, last):
+    lane = iota((rows, LANES), 1) & 63
+    return (lane >= first) & (lane < last)
+
+
+def roll(x, by):
+    by = by % LANES
+    return x if by == 0 else pltpu.roll(x, by, 1)
+
+
+def dot(a, b):
+    return lax.dot_general(a, b, (((1,), (0,)), ((), ())), precision=HIGH, preferred_element_type=jnp.float32)
+
+
+def spread_matrix(scale):
+    coarse, fine = iota((LANES, LANES), 0), iota((LANES, LANES), 1)
+    hit = ((coarse >> 6) == (fine >> 6)) & ((coarse & 63) == 4 + ((fine & 63) >> 1))
+    return jnp.where(hit, jnp.float32(scale), 0.0)
+
+
+def gather_matrix(first, last, scale):
+    fine, coarse = iota((LANES, LANES), 0), iota((LANES, LANES), 1)
+    hit = ((coarse >> 6) == (fine >> 6)) & ((coarse & 63) == 4 + ((fine & 63) >> 1))
+    hit = hit & ((fine & 63) >= first) & ((fine & 63) < last)
+    return jnp.where(hit, jnp.float32(scale), 0.0)
+
+
+def fill_ends(field, rows):
+    for z in range(field.shape[0]):
+        field[z, PAD - 1 : PAD, :] = roll(field[z, PAD + rows - 1 : PAD + rows, :], 64)
+        field[z, PAD + rows : PAD + rows + 1, :] = roll(field[z, PAD : PAD + 1, :], 64)
+
+
+def one_step(src, dst, keep, rows, lows, chunk):
+    planes = src.shape[0] - 2
+    low_z, low_x, low_y = lows
+    for first in range(0, rows, chunk):
+        below = None
+        here = src[1, PAD + first : PAD + first + chunk, :]
+        for z in range(planes):
+            above = None
+            if z + 1 < planes:
+                above = src[z + 2, PAD + first : PAD + first + chunk, :]
+            x_low = src[z + 1, PAD + first - 1 : PAD + first - 1 + chunk, :]
+            x_high = src[z + 1, PAD + first + 1 : PAD + first + 1 + chunk, :]
+            out = keep[z, first : first + chunk, :] * here + x_high + roll(here, -1)
+            out = out + low_x * x_low + low_y * roll(here, 1)
+            if above is not None:
+                out = out + above
+            if below is not None:
+                out = out + low_z * below
+            dst[z + 1, PAD + first : PAD + first + chunk, :] = out
+            if first == 0:
+                dst[z + 1, PAD + rows : PAD + rows + 1, :] = roll(out[0:1], 64)
+            if first + chunk == rows:
+                dst[z + 1, PAD - 1 : PAD, :] = roll(out[chunk - 1 : chunk], 64)
+            below, here = here, above
+
+
+def pack_kernel(tm_ref, initial, reaction, out, sums):
+    tm = tm_ref[0]
+    count = out.shape[0]
+    half = initial.shape[1] // 2
+    coarse_half = half // 2
+    part = coarse_half // 2
+    step = 32
+    lane = iota((step, LANES), 1)
+    for z in range(2):
+        for first in range(0, half, step):
+            tiles = []
+            for base in (0, half):
+                rows = slice(base + first, base + first + step)
+                tiles.append(
+                    [
+                        jnp.where(tm == 0, initial[z, rows, t * LANES : (t + 1) * LANES], reaction[z, rows, t * LANES : (t + 1) * LANES])
+                        for t in range(2)
+                    ]
+                )
+            turned = [roll(t, 64) for t in tiles[1]]
+            for s in range(count):
+                start = (OWN * s - EDGE) % 256
+                tile, off = start // LANES, start % LANES
+                if off + 64 <= LANES:
+                    a = tiles[0][tile]
+                else:
+                    a = jnp.where(lane >= off, tiles[0][tile], tiles[0][1 - tile])
+                if off >= 64:
+                    b = turned[1 - tile] if off + 64 >= LANES else turned[tile]
+                    b = jnp.where((lane >= off - 64) & (lane < 64), turned[tile], turned[1 - tile])
+                else:
+                    b = turned[tile]
+                in_a = ((lane - off) & (LANES - 1)) < 64
+                out[s, z * half + first : z * half + first + step, :] = roll(jnp.where(in_a, a, b), -off)
+
+    to_coarse = jnp.where((iota((2 * LANES, LANES), 0) >> 1) == iota((2 * LANES, LANES), 1), jnp.float32(0.125), 0.0)
+    lane = iota((part, LANES), 1)
+    for t in range(2):
+
+        @pl.when(tm == t)
+        def _(t=t):
+            def small(field):
+                whole = None
+                for c in range(2):
+                    cols = slice(c * LANES, (c + 1) * LANES)
+                    for h in range(2):
+                        rows = slice(h * half + 2 * part * t, h * half + 2 * part * t + 2 * part)
+                        sums[c, 2 * part * h : 2 * part * (h + 1), :] = field[0, rows, cols] + field[1, rows, cols]
+                for c in range(2):
+                    total = sums[c, pl.ds(0, 2 * part, 2), :] + sums[c, pl.ds(1, 2 * part, 2), :]
+                    piece = dot(total, to_coarse[c * LANES : (c + 1) * LANES])
+                    whole = piece if whole is None else whole + piece
+                return whole[:part], whole[part:]
+
+            fields, rates = small(initial), small(reaction)
+            for s in range(count):
+                halves = []
+                for h in range(2):
+                    at = 64 * h
+                    own = roll(fields[h], 12 - 16 * s + at)
+                    left = roll(rates[h], 52 - 16 * s + at)
+                    right = roll(rates[h], 20 - 16 * s + at)
+                    here = lane & 63
+                    piece = jnp.where(here < 40, own, jnp.where(here < 44, left, jnp.where(here < 48, right, 0.0)))
+                    halves.append(piece)
+                out[s, 2 * half : 2 * half + part, :] = jnp.where(lane < 64, halves[0], halves[1])
+
+
+def march_kernel(tm_ref, mine, other, field_out, change_out, fine_a, fine_b, fine_keep, small_a, small_b, small_keep, first_guess, second_guess):
+    tm = tm_ref[0]
+    planes = fine_keep.shape[0]
+    half = fine_keep.shape[1]
+    rows = small_keep.shape[1]
+    part = rows // 2
+    count = planes // 2
+    lead, centre, slope, lows = weights(*F_CONST)
+    small_lead, small_centre, small_slope, small_lows = weights(*C_CONST)
+    small_scale = small_lead**CSTEPS
+    scale = lead**FSTEPS
+
+    for field in (fine_a, fine_b):
+        for z in (0, planes + 1):
+            field[z] = jnp.zeros(field.shape[1:], jnp.float32)
+    for field in (small_a, small_b):
+        for z in (0, count + 1):
+            field[z] = jnp.zeros(field.shape[1:], jnp.float32)
+
+    to_coarse = gather_matrix(0, 64, 0.125)
+    left, right = lanes_in(rows, 0, 4), lanes_in(rows, 36, 40)
+    for k in range(count):
+        for z in range(2):
+            at = slice(z * half, (z + 1) * half)
+            fine_keep[2 * k + z] = jnp.where(tm == 0, other[k, at, :], mine[k, at, :])
+        total = fine_keep[2 * k, pl.ds(0, rows, 2), :] + fine_keep[2 * k, pl.ds(1, rows, 2), :]
+        total = total + (fine_keep[2 * k + 1, pl.ds(0, rows, 2), :] + fine_keep[2 * k + 1, pl.ds(1, rows, 2), :])
+        at = slice(2 * half, 2 * half + part)
+        small_a[k + 1, PAD : PAD + part, :] = jnp.where(tm == 0, mine[k, at, :], other[k, at, :])
+        small_a[k + 1, PAD + part : PAD + rows, :] = jnp.where(tm == 0, other[k, at, :], mine[k, at, :])
+        window = small_a[k + 1, PAD : PAD + rows, :]
+        rate = jnp.where(left, roll(window, -40), jnp.where(right, roll(window, -8), dot(total, to_coarse)))
+        small_keep[k] = small_centre - small_slope * rate
+        for z in range(2):
+            fine_keep[2 * k + z] = centre - slope * fine_keep[2 * k + z]
+    fill_ends(small_a, rows)
+
+    def coarse_run():
+        for _ in range(CSTEPS // 2):
+            one_step(small_a, small_b, small_keep, rows, small_lows, 24)
+            one_step(small_b, small_a, small_keep, rows, small_lows, 24)
+
+    coarse_run()
+    spread = spread_matrix(small_scale)
+    for k in range(count):
+        guess = dot(small_a[k + 1, PAD : PAD + rows, :], spread)
+        first_guess[k] = guess
+        for z in range(2):
+
+            @pl.when(tm == 0)
+            def _(k=k, z=z):
+                fine_a[2 * k + z + 1, PAD : PAD + half, :] = mine[k, z * half : (z + 1) * half, :]
+
+            @pl.when(tm != 0)
+            def _(k=k, z=z, guess=guess):
+                fine_a[2 * k + z + 1, pl.ds(PAD, rows, 2), :] = guess
+                fine_a[2 * k + z + 1, pl.ds(PAD + 1, rows, 2), :] = guess
+
+    @pl.when(tm != 0)
+    def _():
+        coarse_run()
+        spread = spread_matrix(small_scale * small_scale)
+        for k in range(count):
+            second_guess[k] = dot(small_a[k + 1, PAD : PAD + rows, :], spread)
+
+    fill_ends(fine_a, half)
+
+    def turn(_, carry):
+        one_step(fine_a, fine_b, fine_keep, half, lows, 24)
+        one_step(fine_b, fine_a, fine_keep, half, lows, 24)
+        return carry
+
+    lax.fori_loop(0, FSTEPS // 2, turn, 0)
+
+    keep_first = lanes_in(rows, 16, 48)
+    for k in range(count):
+        add = jnp.where(tm == 0, first_guess[k], 0.0)
+        less = jnp.where(tm == 0, first_guess[k], second_guess[k])
+        for odd in range(2):
+            value = []
+            for z in range(2):
+                fine = fine_a[2 * k + z + 1, pl.ds(PAD + odd, rows, 2), :] * jnp.float32(scale)
+                value.append((add + fine) - less)
+            field_out[k, pl.ds(odd, rows, 2), :] = jnp.where(keep_first, value[0], roll(value[1], 32))
+
+    @pl.when(tm == 0)
+    def _():
+        to_own = gather_matrix(16, 48, 0.125)
+        for k in range(count):
+            total = None
+            for z in range(2):
+                for odd in range(2):
+                    fine = fine_a[2 * k + z + 1, pl.ds(PAD + odd, rows, 2), :] * jnp.float32(scale)
+                    fine = (first_guess[k] + fine) - first_guess[k]
+                    total = fine if total is None else total + fine
+            small_a[k + 1, PAD : PAD + rows, :] = dot(total, to_own)
+        fill_ends(small_a, rows)
+        coarse_run()
+        for k in range(count):
+            change_out[k] = small_a[k + 1, PAD : PAD + rows, :] * jnp.float32(small_scale)
+
+
+def send_kernel(field, guess, out):
+    rows = guess.shape[1]
+    half = 2 * rows
+    spread = spread_matrix(1.0)
+    keep_first = lanes_in(rows, 16, 48)
+    lane = iota((8, LANES), 1)
+    spill = lanes_in(8, 8, 12) | lanes_in(8, 28, 32)
+    for k in range(guess.shape[0]):
+        full = dot(guess[k], spread)
+        both = jnp.where(keep_first, full, roll(full, 32))
+        for odd in range(2):
+            out[k, pl.ds(odd, rows, 2), :] = field[k, pl.ds(odd, rows, 2), :] + both
+        packed = jnp.zeros((8, LANES), jnp.float32)
+        for g, by in enumerate(TURNS):
+            piece = jnp.where(spill, guess[k, 8 * g : 8 * g + 8, :], 0.0)
+            packed = packed + roll(piece, by)
+        out[k, half : half + 8, :] = packed
+
+
+def unpack_kernel(strips, out, spilled):
+    count = strips.shape[0]
+    half = out.shape[1] // 2
+    rows = half // 2
+    lane8 = iota((8, LANES), 1)
+    for h in range(2):
+        for g in range(rows // 8):
+            total = None
+            for s in range(count):
+                piece = roll(strips[s, half : half + 8, :], 16 * s - 4 - (8 + TURNS[g] + 64 * h))
+                offset = (lane8 - (16 * s - 4)) & (LANES - 1)
+                hit = (offset < 4) | ((offset >= 20) & (offset < 24))
+                piece = jnp.where(hit, piece, 0.0)
+                total = piece if total is None else total + piece
+            at = h * rows + 8 * g
+            spilled[pl.ds(2 * at, 8, 2), :] = total
+            spilled[pl.ds(2 * at + 1, 8, 2), :] = total
+    widen = jnp.where((iota((LANES, 2 * LANES), 1) >> 1) == iota((LANES, 2 * LANES), 0), 1.0, 0.0).astype(jnp.float32)
+    step = 32
+    lane = iota((step, LANES), 1)
+    for h in range(2):
+        for first in range(0, half, step):
+            wide = dot(spilled[h * half + first : h * half + first + step, :], widen)
+            for t in range(2):
+                total = [None, None]
+                for j in range(4):
+                    s = 4 * t + j
+                    block = strips[s, first : first + step, :]
+                    for z in range(2):
+                        piece = roll(block, OWN * j - (16 + 64 * h + 32 * z))
+                        total[z] = piece if j == 0 else jnp.where(lane >= OWN * j, piece, total[z])
+                for z in range(2):
+                    out[z, h * half + first : h * half + first + step, t * LANES : (t + 1) * LANES] = (
+                        total[z] + wide[:, t * LANES : (t + 1) * LANES]
+                    )
+
+
+def vmem_call(kernel, out_shapes, scratch, args, scalars=0):
+    specs = [pl.BlockSpec(memory_space=pltpu.SMEM)] * scalars
+    specs += [pl.BlockSpec(memory_space=pltpu.VMEM)] * (len(args) - scalars)
+    shapes = [jax.ShapeDtypeStruct(s, jnp.float32) for s in out_shapes]
+    return pl.pallas_call(
+        kernel,
+        out_shape=shapes,
+        in_specs=specs,
+        out_specs=[pl.BlockSpec(memory_space=pltpu.VMEM)] * len(shapes),
+        scratch_shapes=[pltpu.VMEM(s, jnp.float32) for s in scratch],
+        compiler_params=pltpu.CompilerParams(vmem_limit_bytes=48 * 1024 * 1024),
+    )(*args)
+
+
+def strips_local(initial, reaction):
+    count = lax.axis_size("space")
+    _, nx, _ = initial.shape
+    half, rows = nx // 2, nx // 4
+    planes = 2 * count
+    tm = lax.axis_index("tm").astype(jnp.int32).reshape(1)
+    (blocks,) = vmem_call(pack_kernel, [(count, 2 * half + rows // 2, LANES)], [(2, 2 * rows, LANES)], (tm, initial, reaction), 1)
+    mine = lax.all_to_all(blocks, "space", 0, 0)
+    other = lax.ppermute(mine, "tm", [(0, 1), (1, 0)])
+    fine = (planes + 2, half + 2 * PAD, LANES)
+    small = (count + 2, rows + 2 * PAD, LANES)
+    field, guess = vmem_call(
+        march_kernel,
+        [(count, half, LANES), (count, rows, LANES)],
+        [fine, fine, (planes, half, LANES), small, small, (count, rows, LANES), (count, rows, LANES), (count, rows, LANES)],
+        (tm, mine, other),
+        1,
+    )
+    guess = lax.ppermute(guess, "tm", [(0, 1)])
+    (blocks,) = vmem_call(send_kernel, [(count, half + 8, LANES)], [], (field, guess))
+    strips = lax.all_to_all(blocks, "space", 0, 0)
+    (out,) = vmem_call(unpack_kernel, [(2, nx, 2 * LANES)], [(nx, LANES)], (strips,))
+    return out[None]
+
+
+def fits_strips(mesh, initial):
+    planes = initial.shape[0] // (mesh.shape["groups"] * mesh.shape["space"])
+    return (
+        mesh.shape["space"] == 8
+        and mesh.shape["tm"] == 2
+        and planes == 2
+        and initial.shape[1] == 192
+        and initial.shape[2] == 256
+    )
+
+
 def solution(mesh):
     in_specs = (P(("groups", "space"), None, None), P(("groups", "space"), None, None))
     out_specs = P(("groups", "tm"), "space", None, None)
-    return jax.shard_map(local, mesh=mesh, in_specs=in_specs, out_specs=out_specs, check_vma=False)
+
+    def run(initial, reaction):
+        body = strips_local if fits_strips(mesh, initial) else local
+        return jax.shard_map(body, mesh=mesh, in_specs=in_specs, out_specs=out_specs, check_vma=False)(initial, reaction)
+
+    return run

time: 410 us -> 93.2 us (0.23)
  waiting for transfers between devices: 178 us -> 3.46 us
  starting transfers between devices: 119 us -> 2.08 us
  local copies, waits for them, and re-layouts: 68.7 us -> 1.99 us
  blocking collectives: 0 us -> 45.9 us
  other arithmetic: 40.8 us -> 0 us
  Pallas kernels: 0 us -> 39.6 us
    ppermute x44 -> x2, waiting for transfers between devices: 178 us -> 3.46 us  [the longest x1 2.42 us: strips_local(): other = lax.ppermute(mine, 'tm', [(0, 1), (1, 0)])]
    ppermute x44 -> x2, starting transfers between devices: 119 us -> 2.08 us  [the longest x1 2.08 us: strips_local(): guess = lax.ppermute(guess, 'tm', [(0, 1)])]
    reduce_sum x4 -> x0, local copies, waits for them, and re-layouts: 55.7 us -> none  [restrict(): field.reshape(depth // 2, 2, rows // 2, 2, cols // 2, 2)]
    all_to_all x0 -> x2, blocking collectives: none -> 45.9 us  [the longest x1 29.8 us: strips_local(): mine = lax.all_to_all(blocks, 'space', 0, 0)]
    pallas_call x0 -> x4, Pallas kernels: none -> 39.6 us  [vmem_call(): pl.pallas_call(kernel, out_shape=shapes, in_specs=specs, out_specs=[pl.Bl...]
    reduce_sum x8 -> x0, other arithmetic: 26.3 us -> none  [restrict(): field.reshape(depth // 2, 2, rows // 2, 2, cols // 2, 2)]
    select_n x28 -> x0, other arithmetic: 11.3 us -> none  [block_turn(): padded = jnp.where(inside[:, None, None], updated, 0.0)]
    slice x112 -> x0, local copies, waits for them, and re-layouts: 9.46 us -> none  [the longest x56 7.76 us: stencil(): y_minus = jnp.roll(middle, 1, 2)]
  transfers between devices with their start and end apart: 44 -> 2, of which waited for: 41 -> 2; matrix products, arithmetic and copies ran while one was open for 6% -> 0% of each run, Pallas kernels for 0% -> 0%
where the time goes in v1:
time: 93.2 us; the launch traced here: 93 us
  blocking collectives  45.9 us (49%)
  Pallas kernels  39.6 us (42%)
  waiting for transfers between devices  3.46 us (4%)
  starting transfers between devices  2.08 us (2%)
  local copies, waits for them, and re-layouts  1.99 us (2%)
    pallas_call x4, Pallas kernels, vmem_call(): pl.pallas_call(kernel, out_shape=shapes, in_specs=specs, out_specs=[pl.Bl...  39.6 us
    all_to_all x1, blocking collectives, strips_local(): mine = lax.all_to_all(blocks, 'space', 0, 0)  29.8 us
    all_to_all x1, blocking collectives, strips_local(): strips = lax.all_to_all(blocks, 'space', 0, 0)  16 us
    ppermute x1, waiting for transfers between devices, strips_local(): other = lax.ppermute(mine, 'tm', [(0, 1), (1, 0)])  2.42 us
    ppermute x1, starting transfers between devices, strips_local(): guess = lax.ppermute(guess, 'tm', [(0, 1)])  2.08 us
    unnamed x4, local copies, waits for them, and re-layouts  1.99 us
  transfers between devices with their start and end apart: 2, of which 2 were waited for; matrix products, arithmetic and copies ran while one was open for 0% of the time, Pallas kernels for 0%

profile of v1, /device:TPU:0, one launch (start us, length us, event | category | flops | bytes accessed | tf_op | source)
XLA Modules:
  0.0 93.0 jit_solution(2000338889838546756)
XLA Ops:
  0.0 0.0 copy-start
  0.0 1.0 %copy-done = f32[2,192,256]{2,1,0:T(8,128)S(1)} copy-done((f32[2,192,256]{2,1,0:T(8,128)S(1)}, f32[2,192,256]{2,1,0:T(8,128)}, u32[]{:S(2)}) %copy-start) | copy-done | bytes 393240
  1.0 0.0 copy-start.1
  1.0 1.0 %copy-done.1 = f32[2,192,256]{2,1,0:T(8,128)S(1)} copy-done((f32[2,192,256]{2,1,0:T(8,128)S(1)}, f32[2,192,256]{2,1,0:T(8,128)}, u32[]{:S(2)}) %copy-start.1) | copy-done | bytes 393240
  2.0 1.1 %shard_map.28 = f32[8,216,128]{2,1,0:T(8,128)S(1)} custom-call(s32[1]{0:T(128)} %bitcast.tm_ref, f32[2,192,256]{2,1,0:T(8,128)S(1)} %copy-done, f32[2,192,256]{2,1,0:T(8,128)S(1)} %copy-done.1), custom_call_target="tpu_custom_call" | custom-call | tf_op jit(solution)/shard_map/pallas_call | solution.py:452
  3.1 29.8 %all_to_all.10.mine = f32[8,216,128]{2,1,0:T(8,128)S(1)} all-to-all(f32[8,216,128]{2,1,0:T(8,128)S(1)} %shard_map.28), channel_id=1, replica_groups=mesh['groups'=2,'tm'=2,'space'=8] {'space'}, dimensions={0} | all-to-all | bytes 1769472 | tf_op jit(solution)/shard_map/all_to_all | solution.py:469
  32.9 0.0 collective-permute-start
  32.9 2.4 %collective-permute-done.other = f32[8,216,128]{2,1,0:T(8,128)S(1)} collective-permute-done((f32[8,216,128]{2,1,0:T(8,128)S(1)}, f32[8,216,128]{2,1,0:T(8,128)S(1)}, u32[]{:S(2)}, u32[]{:S(2)}) %collective-permute-start) | collective-permute-done | bytes 884768 | tf_op jit(solution)/shard_map/ppermute | solution.py:470
  35.3 36.5 %shard_map.29 = (f32[8,96,128]{2,1,0:T(8,128)S(1)}, f32[8,48,128]{2,1,0:T(8,128)S(1)}) custom-call(s32[1]{0:T(128)} %bitcast.tm_ref, f32[8,216,128]{2,1,0:T(8,128)S(1)} %all_to_all.10.mine, f32[8,216,128]{2,1,0:T(8,128)S(1)} %collective-permute-done.other), custom_call_target="tpu_custom_call" | custom-call | tf_op jit(solution)/shard_map/pallas_call | solution.py:452
  71.8 2.1 %collective-permute-start.1 = (f32[8,48,128]{2,1,0:T(8,128)S(1)}, f32[8,48,128]{2,1,0:T(8,128)S(1)}, u32[]{:S(2)}, u32[]{:S(2)}) collective-permute-start(f32[8,48,128]{2,1,0:T(8,128)S(1)} %get-tuple-element.8), channel_id=1, source_target_pairs={{0,8},{1,9},{2,10},{3,11},{4,12},{5,13},{6,14},{7,15},{16,24},{17,... | collective-permute-start | bytes 589832 | tf_op jit(solution)/shard_map/ppermute | solution.py:480
  73.9 1.0 %collective-permute-done.1.guess = f32[8,48,128]{2,1,0:T(8,128)S(1)} collective-permute-done((f32[8,48,128]{2,1,0:T(8,128)S(1)}, f32[8,48,128]{2,1,0:T(8,128)S(1)}, u32[]{:S(2)}, u32[]{:S(2)}) %collective-permute-start.1) | collective-permute-done | bytes 196640 | tf_op jit(solution)/shard_map/ppermute | solution.py:480
  75.0 0.6 shard_map.30
  75.6 16.0 %all_to_all.11.strips = f32[8,104,128]{2,1,0:T(8,128)S(1)} all-to-all(f32[8,104,128]{2,1,0:T(8,128)S(1)} %shard_map.30), channel_id=1, replica_groups=mesh['groups'=2,'tm'=2,'space'=8] {'space'}, dimensions={0} | all-to-all | bytes 851968 | tf_op jit(solution)/shard_map/all_to_all | solution.py:482
  91.6 1.4 %shard_map.31 = f32[2,192,256]{2,1,0:T(8,128)} custom-call(f32[8,104,128]{2,1,0:T(8,128)S(1)} %all_to_all.11.strips), custom_call_target="tpu_custom_call" | custom-call | tf_op jit(solution)/shard_map/pallas_call | solution.py:452
Async XLA Ops:
  0.0 1.0 %copy-start = (f32[2,192,256]{2,1,0:T(8,128)S(1)}, f32[2,192,256]{2,1,0:T(8,128)}, u32[]{:S(2)}) copy-start(f32[2,192,256]{2,1,0:T(8,128)} %initial.1) | copy-start | bytes 1179652
  1.0 1.0 %copy-start.1 = (f32[2,192,256]{2,1,0:T(8,128)S(1)}, f32[2,192,256]{2,1,0:T(8,128)}, u32[]{:S(2)}) copy-start(f32[2,192,256]{2,1,0:T(8,128)} %reaction.1) | copy-start | bytes 1179652
  32.9 2.4 %collective-permute-start = (f32[8,216,128]{2,1,0:T(8,128)S(1)}, f32[8,216,128]{2,1,0:T(8,128)S(1)}, u32[]{:S(2)}, u32[]{:S(2)}) collective-permute-start(f32[8,216,128]{2,1,0:T(8,128)S(1)} %all_to_all.10.mine), channel_id=1, source_target_pairs={{0,8},{8,0},{1,9},{9,1},{2,10},{10,2},{3,11},{11,3},{4,12},{12,4},... | collective-permute-start | bytes 2654216 | tf_op jit(solution)/shard_map/ppermute | solution.py:470
  71.8 3.1 %collective-permute-start.1 = (f32[8,48,128]{2,1,0:T(8,128)S(1)}, f32[8,48,128]{2,1,0:T(8,128)S(1)}, u32[]{:S(2)}, u32[]{:S(2)}) collective-permute-start(f32[8,48,128]{2,1,0:T(8,128)S(1)} %get-tuple-element.8), channel_id=1, source_target_pairs={{0,8},{1,9},{2,10},{3,11},{4,12},{5,13},{6,14},{7,15},{16,24},{17,... | collective-permute-start | bytes 589832 | tf_op jit(solution)/shard_map/ppermute | solution.py:480

commit v2 on v0

--- a/solution.py
+++ b/solution.py
@@ -1,6 +1,10 @@
+import functools
+
 import jax
 import jax.numpy as jnp
 from jax import lax
+from jax.experimental import pallas as pl
+from jax.experimental.pallas import tpu as pltpu
 from jax.sharding import PartitionSpec as P
 
 FSTEPS = 16
@@ -134,7 +138,403 @@
     return result[None]
 
 
+F_CONST = (0.5, 0.1, 1.0)
+C_CONST = (2.0, 0.025, 0.5)
+LANES = 128
+PAD = 8
+SPILL_TURNS = (0, 4, 8)
+FINE_CHUNKS = ((0, 16), (32, 16), (16, 16))
+HALF_CHUNKS = ((0, 24), (24, 24))
+QUARTER_CHUNKS = ((0, 24),)
+
+
+def weights(step_len, diffusion, upwind_scale):
+    lead = step_len * diffusion
+    lag = step_len * upwind_scale
+    centre = (1.0 - 6.0 * lead - 0.35 * lag) / lead
+    lows = tuple((lead + lag * part) / lead for part in (0.13, 0.12, 0.10))
+    return lead, centre, step_len / lead, lows
+
+
+def iota(shape, dim):
+    return lax.broadcasted_iota(jnp.int32, shape, dim)
+
+
+def roll(x, by):
+    by = by % LANES
+    return x if by == 0 else pltpu.roll(x, by, 1)
+
+
+def take(x, lanes):
+    return jnp.take_along_axis(x, lanes, axis=1, mode="promise_in_bounds")
+
+
+def inside(index, first, last):
+    return (index >= first) & (index < last)
+
+
+def wrap_rows(field, planes, rows, quarter):
+    height = rows + 2 * PAD
+    for z in range(0, planes, 8):
+        at = (z + 1) * height + PAD
+        field[pl.ds(at - 1, 8, height), :] = roll(field[pl.ds(at + rows - 1, 8, height), :], quarter)
+        field[pl.ds(at + rows, 8, height), :] = roll(field[pl.ds(at, 8, height), :], -quarter)
+
+
+def one_step(src, dst, keep, planes, rows, lows, chunks, quarter):
+    low_z, low_x, low_y = lows
+    height = rows + 2 * PAD
+    several = len(src) == 2
+    for first, size in chunks:
+        below = [None for _ in src]
+        here = [s[height + PAD + first : height + PAD + first + size, :] for s in src]
+        for z in range(planes):
+            at = (z + 1) * height + PAD + first
+            above = [s[at + height : at + height + size, :] if z + 1 < planes else None for s in src]
+            for e, s in enumerate(src):
+                if several:
+                    o = here[1 - e]
+                    y_low, y_high = (roll(o, 1), o) if e == 0 else (o, roll(o, -1))
+                else:
+                    y_low, y_high = roll(here[0], 1), roll(here[0], -1)
+                out = keep[e][z * rows + first : z * rows + first + size, :] * here[e] + s[at + 1 : at + 1 + size, :]
+                out = out + y_high + low_x * s[at - 1 : at - 1 + size, :] + low_y * y_low
+                if above[e] is not None:
+                    out = out + above[e]
+                if below[e] is not None:
+                    out = out + low_z * below[e]
+                dst[e][at : at + size, :] = out
+            below, here = here, above
+    for d in dst:
+        wrap_rows(d, planes, rows, quarter)
+
+
+def pack_kernel(tm_ref, initial_hbm, reaction_hbm, out, initial, reaction, sums, arrived):
+    tm = tm_ref[0]
+    copies = [
+        pltpu.make_async_copy(initial_hbm, initial, arrived.at[0]),
+        pltpu.make_async_copy(reaction_hbm, reaction, arrived.at[1]),
+    ]
+    for copy in copies:
+        copy.start()
+    for copy in copies:
+        copy.wait()
+
+    count = out.shape[0]
+    rows = initial.shape[1] // 4
+    part = rows // 2
+    step = 16
+    lane = iota((step, LANES), 1)
+    low_half = lane < 64
+    even_odd = jnp.where(low_half, 2 * lane, 2 * lane - (LANES - 1))
+    odd_even = jnp.where(low_half, 2 * lane + 1, 2 * lane - LANES)
+
+    def columns(left, right):
+        a, b = take(left, even_odd), take(right, odd_even)
+        return jnp.where(low_half, a, b), roll(jnp.where(low_half, b, a), 64)
+
+    for z in range(2):
+        for first in range(0, rows, step):
+            turned = ([], [])
+            for j in range(4):
+                at = slice(j * rows + first, j * rows + first + step)
+                tiles = [
+                    jnp.where(tm == 0, initial[z, at, t * LANES : (t + 1) * LANES], reaction[z, at, t * LANES : (t + 1) * LANES])
+                    for t in range(2)
+                ]
+                for e, x in enumerate(columns(*tiles)):
+                    turned[e].append(roll(x, 32 * j))
+            for s in range(count):
+                by = 16 * s - 8
+                quarter = ((lane - by) & (LANES - 1)) >> 5
+                for e in range(2):
+                    r = turned[e]
+                    x = jnp.where(quarter == 0, r[0], jnp.where(quarter == 1, r[1], jnp.where(quarter == 2, r[2], r[3])))
+                    at = (2 * z + e) * rows + first
+                    out[s, at : at + step, :] = roll(x, -by)
+
+    lane = iota((part, LANES), 1)
+    here = lane & 63
+    for t in range(2):
+
+        @pl.when(tm == t)
+        def _(t=t):
+            def small(field):
+                parts = []
+                for h in range(2):
+                    for first in range(0, rows, step):
+                        at = slice((2 * h + t) * rows + first, (2 * h + t) * rows + first + step)
+                        tiles = [field[0, at, c * LANES : (c + 1) * LANES] + field[1, at, c * LANES : (c + 1) * LANES] for c in range(2)]
+                        even, odd = columns(*tiles)
+                        sums[first : first + step, :] = (even + odd) * 0.125
+                    parts.append(sums[pl.ds(0, part, 2), :] + sums[pl.ds(1, part, 2), :])
+                return parts
+
+            fields, rates = small(initial), small(reaction)
+            for s in range(count):
+                halves = []
+                for h in range(2):
+                    at = 64 * h
+                    own = roll(fields[h], 12 - 16 * s + at)
+                    left = roll(rates[h], 52 - 16 * s + at)
+                    right = roll(rates[h], 20 - 16 * s + at)
+                    halves.append(jnp.where(here < 40, own, jnp.where(here < 44, left, jnp.where(here < 48, right, 0.0))))
+                out[s, 4 * rows : 4 * rows + part, :] = jnp.where(lane < 64, halves[0], halves[1])
+
+
+def march_kernel(
+    tm_ref, mine, other, field_out, guess_out,
+    even_a, odd_a, even_b, odd_b, even_keep, odd_keep, wide_a, wide_b, wide_keep, small_a, small_b, small_keep, first_guess, second_guess,
+):
+    tm = tm_ref[0]
+    count = mine.shape[0]
+    planes = 2 * count
+    rows = even_keep.shape[0] // planes
+    part = rows // 2
+    height, wide_height, small_height = rows + 2 * PAD, rows + 2 * PAD, part + 2 * PAD
+    lead, centre, slope, lows = weights(*F_CONST)
+    small_lead, small_centre, small_slope, small_lows = weights(*C_CONST)
+    small_scale = jnp.float32(small_lead**CSTEPS)
+    scale = jnp.float32(lead**FSTEPS)
+    fine_a, fine_b, fine_keep = (even_a, odd_a), (even_b, odd_b), (even_keep, odd_keep)
+    lane = iota((part, LANES), 1)
+    even_quarter = ((lane >> 5) & 1) == 0
+
+    in_half = lane & 63
+    for k in range(count):
+        total = None
+        for z in range(2):
+            for e in range(2):
+                at = slice((2 * z + e) * rows, (2 * z + e + 1) * rows)
+                to = slice((2 * k + z) * rows, (2 * k + z + 1) * rows)
+                rate = jnp.where(tm == 0, other[k, at, :], mine[k, at, :])
+                fine_keep[e][to, :] = centre - slope * rate
+                total = rate if total is None else total + rate
+        wide_b[0:rows, :] = total * 0.125
+        rate = wide_b[pl.ds(0, part, 2), :] + wide_b[pl.ds(1, part, 2), :]
+        small_keep[k * part : (k + 1) * part, :] = small_centre - small_slope * rate
+        at = slice(4 * rows, 4 * rows + part)
+        windows = [jnp.where(tm == 0, mine[k, at, :], other[k, at, :]), jnp.where(tm == 0, other[k, at, :], mine[k, at, :])]
+        for n, by in ((0, 4), (1, -28)):
+            to = (k + 1) * wide_height + PAD + n * part
+            wide_a[to : to + part, :] = windows[n]
+            x = jnp.where(in_half < 4, roll(windows[n], -40), jnp.where(inside(in_half, 36, 40), roll(windows[n], -8), roll(rate, by)))
+            wide_keep[k * rows + n * part : k * rows + (n + 1) * part, :] = small_centre - small_slope * x
+    wrap_rows(wide_a, count, rows, 64)
+
+    for _ in range(CSTEPS // 2):
+        one_step((wide_a,), (wide_b,), (wide_keep,), count, rows, small_lows, HALF_CHUNKS, 64)
+        one_step((wide_b,), (wide_a,), (wide_keep,), count, rows, small_lows, HALF_CHUNKS, 64)
+
+    for k in range(count):
+        at = (k + 1) * wide_height + PAD
+        upper, lower = wide_a[at : at + part, :], wide_a[at + part : at + rows, :]
+        guess = jnp.where(even_quarter, roll(upper, -4), roll(lower, 28)) * small_scale
+        first_guess[k * part : (k + 1) * part, :] = guess
+        to = (k + 1) * small_height + PAD
+        small_a[to : to + part, :] = guess
+        for z in range(2):
+            for e in range(2):
+                to = (2 * k + z + 1) * height + PAD
+
+                @pl.when(tm == 0)
+                def _(k=k, z=z, e=e, to=to):
+                    fine_a[e][to : to + rows, :] = mine[k, (2 * z + e) * rows : (2 * z + e + 1) * rows, :]
+
+                @pl.when(tm != 0)
+                def _(e=e, to=to, guess=guess):
+                    fine_a[e][pl.ds(to, part, 2), :] = guess
+                    fine_a[e][pl.ds(to + 1, part, 2), :] = guess
+
+    def coarse_run():
+        wrap_rows(small_a, count, part, 32)
+        for _ in range(CSTEPS // 2):
+            one_step((small_a,), (small_b,), (small_keep,), count, part, small_lows, QUARTER_CHUNKS, 32)
+            one_step((small_b,), (small_a,), (small_keep,), count, part, small_lows, QUARTER_CHUNKS, 32)
+
+    @pl.when(tm != 0)
+    def _():
+        coarse_run()
+        for k in range(count):
+            at = (k + 1) * small_height + PAD
+            second_guess[k * part : (k + 1) * part, :] = small_a[at : at + part, :] * small_scale
+
+    for field in fine_a:
+        wrap_rows(field, planes, rows, 32)
+
+    def turn(_, carry):
+        one_step(fine_a, fine_b, fine_keep, planes, rows, lows, FINE_CHUNKS, 32)
+        one_step(fine_b, fine_a, fine_keep, planes, rows, lows, FINE_CHUNKS, 32)
+        return carry
+
+    lax.fori_loop(0, FSTEPS // 2, turn, 0)
+
+    own = inside(lane & 31, 8, 24)
+    for k in range(count):
+        guess = first_guess[k * part : (k + 1) * part, :]
+        add = jnp.where(tm == 0, guess, 0.0)
+        less = jnp.where(tm == 0, guess, second_guess[k * part : (k + 1) * part, :])
+        total = None
+        for e in range(2):
+            for odd in range(2):
+                value = []
+                for z in range(2):
+                    fine = fine_a[e][pl.ds((2 * k + z + 1) * height + PAD + odd, part, 2), :] * scale
+                    value.append((add + fine) - less)
+                total = value[0] + value[1] if total is None else total + (value[0] + value[1])
+                field_out[k, pl.ds(e * rows + odd, part, 2), :] = jnp.where(own, value[0], roll(value[1], 16))
+        to = (k + 1) * small_height + PAD
+        small_a[to : to + part, :] = jnp.where(own, total * 0.125, 0.0)
+
+    @pl.when(tm == 0)
+    def _():
+        coarse_run()
+        for k in range(count):
+            at = (k + 1) * small_height + PAD
+            guess_out[k] = small_a[at : at + part, :] * small_scale
+
+
+def send_kernel(field, guess, out):
+    part = guess.shape[1]
+    rows = 2 * part
+    in_quarter = iota((part, LANES), 1) & 31
+    own = inside(in_quarter, 8, 24)
+    spill = (inside(in_quarter, 4, 8) | inside(in_quarter, 24, 28))[:8]
+    for k in range(guess.shape[0]):
+        mine = guess[k]
+        both = jnp.where(own, mine, roll(mine, 16))
+        for e in range(2):
+            for odd in range(2):
+                at = pl.ds(e * rows + odd, part, 2)
+                out[k, at, :] = field[k, at, :] + both
+        packed = None
+        for g, by in enumerate(SPILL_TURNS):
+            piece = roll(jnp.where(spill, mine[8 * g : 8 * g + 8], 0.0), by)
+            packed = piece if packed is None else packed + piece
+        out[k, 2 * rows : 2 * rows + 8, :] = packed
+
+
+def unpack_kernel(strips, out, spilled):
+    count = strips.shape[0]
+    rows = out.shape[1] // 4
+    part = rows // 2
+
+    def lined_up(read, first, size):
+        quarter = ((iota((size, LANES), 1) - first) & (LANES - 1)) >> 5
+        for c in range(count):
+            x = [read((c + 2 * j) % count) for j in range(4)]
+            yield jnp.where(quarter == 0, x[0], jnp.where(quarter == 1, x[1], jnp.where(quarter == 2, x[2], x[3])))
+
+    def at_strips(parts, j, hit):
+        total = None
+        for c, x in enumerate(parts):
+            s = (c + 2 * j) % count
+            total = jnp.where(hit[s], x, 0.0 if total is None else total)
+        return total
+
+    lane = iota((8, LANES), 1)
+    hit = []
+    for s in range(count):
+        off = (lane - (16 * s - 4)) & (LANES - 1)
+        hit.append((off < 4) | inside(off, 20, 24))
+    pieces = list(lined_up(lambda s: strips[s, 2 * rows : 2 * rows + 8, :], 4, 8))
+    for g, by in enumerate(SPILL_TURNS):
+        parts = [roll(x, 16 * c - 8 - by) for c, x in enumerate(pieces)]
+        for j in range(4):
+            x = at_strips(parts, j, hit)
+            at = j * rows + 16 * g
+            spilled[pl.ds(at, 8, 2), :] = x
+            spilled[pl.ds(at + 1, 8, 2), :] = x
+
+    step = 16
+    lane = iota((step, LANES), 1)
+    low_half = lane < 64
+    from_first = ((lane & 1) << 6) + (lane >> 1)
+    from_second = from_first ^ 64
+    hit = [inside(lane, 16 * s, 16 * s + 16) for s in range(count)]
+    for first in range(0, rows, step):
+        pieces = [
+            list(lined_up(lambda s, e=e: strips[s, e * rows + first : e * rows + first + step, :], 8, step)) for e in range(2)
+        ]
+        for z in range(2):
+            parts = [[roll(x, 16 * c - 8 - 16 * z) for c, x in enumerate(pieces[e])] for e in range(2)]
+            for j in range(4):
+                at = slice(j * rows + first, j * rows + first + step)
+                more = spilled[at, :]
+                even, odd = (at_strips(parts[e], j, hit) + more for e in range(2))
+                odd = roll(odd, 64)
+                out[z, at, :LANES] = take(jnp.where(low_half, even, odd), from_first)
+                out[z, at, LANES:] = take(jnp.where(low_half, odd, even), from_second)
+
+
+VMEM = pl.BlockSpec(memory_space=pltpu.VMEM)
+SMEM = pl.BlockSpec(memory_space=pltpu.SMEM)
+ANY = pl.BlockSpec(memory_space=pl.ANY)
+
+
+def on_core(kernel, in_specs, out_shapes, scratch, *args):
+    shapes = [jax.ShapeDtypeStruct(s, jnp.float32) for s in out_shapes]
+    return pl.pallas_call(
+        kernel,
+        out_shape=shapes,
+        in_specs=in_specs,
+        out_specs=[VMEM] * len(shapes),
+        scratch_shapes=[pltpu.VMEM(s, jnp.float32) if isinstance(s, tuple) else s for s in scratch],
+        compiler_params=pltpu.CompilerParams(vmem_limit_bytes=48 * 1024 * 1024),
+    )(*args)
+
+
+def strips_local(initial, reaction):
+    count = lax.axis_size("space")
+    _, nx, _ = initial.shape
+    rows = nx // 4
+    part = rows // 2
+    planes = 2 * count
+    tm = lax.axis_index("tm").astype(jnp.int32).reshape(1)
+    (blocks,) = on_core(
+        pack_kernel,
+        [SMEM, ANY, ANY],
+        [(count, 4 * rows + part, LANES)],
+        [initial.shape, reaction.shape, (rows, LANES), pltpu.SemaphoreType.DMA((2,))],
+        tm, initial, reaction,
+    )
+    mine = lax.all_to_all(blocks, "space", 0, 0)
+    other = lax.ppermute(mine, "tm", [(0, 1), (1, 0)])
+    fine = ((planes + 2) * (rows + 2 * PAD), LANES)
+    wide = ((count + 2) * (rows + 2 * PAD), LANES)
+    small = ((count + 2) * (part + 2 * PAD), LANES)
+    small_cells = (count * part, LANES)
+    field, guess = on_core(
+        march_kernel,
+        [SMEM, VMEM, VMEM],
+        [(count, 2 * rows, LANES), (count, part, LANES)],
+        [fine] * 4 + [(planes * rows, LANES)] * 2 + [wide, wide, (count * rows, LANES), small, small] + [small_cells] * 3,
+        tm, mine, other,
+    )
+    guess = lax.ppermute(guess, "tm", [(0, 1)])
+    (blocks,) = on_core(send_kernel, [VMEM, VMEM], [(count, 2 * rows + 8, LANES)], [], field, guess)
+    strips = lax.all_to_all(blocks, "space", 0, 0)
+    (out,) = on_core(unpack_kernel, [VMEM], [initial.shape], [(nx, LANES)], strips)
+    return out[None]
+
+
+def fits_strips(mesh, initial):
+    planes = initial.shape[0] // (mesh.shape["groups"] * mesh.shape["space"])
+    return (
+        mesh.shape["space"] == 8
+        and mesh.shape["tm"] == 2
+        and planes == 2
+        and initial.shape[1] == 192
+        and initial.shape[2] == 2 * LANES
+    )
+
+
 def solution(mesh):
     in_specs = (P(("groups", "space"), None, None), P(("groups", "space"), None, None))
     out_specs = P(("groups", "tm"), "space", None, None)
-    return jax.shard_map(local, mesh=mesh, in_specs=in_specs, out_specs=out_specs, check_vma=False)
+
+    def run(initial, reaction):
+        body = strips_local if fits_strips(mesh, initial) else local
+        return jax.shard_map(body, mesh=mesh, in_specs=in_specs, out_specs=out_specs, check_vma=False)(initial, reaction)
+
+    return run

time: 410 us -> 67 us (0.16)
  waiting for transfers between devices: 178 us -> 3.34 us
  starting transfers between devices: 119 us -> 2.05 us
  local copies, waits for them, and re-layouts: 68.7 us -> 1.99 us
  blocking collectives: 0 us -> 45.9 us
  other arithmetic: 40.8 us -> 0 us
  Pallas kernels: 0 us -> 13.4 us
    ppermute x44 -> x2, waiting for transfers between devices: 178 us -> 3.34 us  [the longest x1 2.42 us: strips_local(): other = lax.ppermute(mine, 'tm', [(0, 1), (1, 0)])]
    ppermute x44 -> x2, starting transfers between devices: 119 us -> 2.05 us  [the longest x1 2.05 us: strips_local(): guess = lax.ppermute(guess, 'tm', [(0, 1)])]
    reduce_sum x4 -> x0, local copies, waits for them, and re-layouts: 55.7 us -> none  [restrict(): field.reshape(depth // 2, 2, rows // 2, 2, cols // 2, 2)]
    all_to_all x0 -> x2, blocking collectives: none -> 45.9 us  [the longest x1 29.8 us: strips_local(): mine = lax.all_to_all(blocks, 'space', 0, 0)]
    reduce_sum x8 -> x0, other arithmetic: 26.3 us -> none  [restrict(): field.reshape(depth // 2, 2, rows // 2, 2, cols // 2, 2)]
    pallas_call x0 -> x4, Pallas kernels: none -> 13.4 us  [on_core(): pl.pallas_call(kernel, out_shape=shapes, in_specs=in_specs, out_specs=[VM...]
    select_n x28 -> x0, other arithmetic: 11.3 us -> none  [block_turn(): padded = jnp.where(inside[:, None, None], updated, 0.0)]
    slice x112 -> x0, local copies, waits for them, and re-layouts: 9.46 us -> none  [the longest x56 7.76 us: stencil(): y_minus = jnp.roll(middle, 1, 2)]
  transfers between devices with their start and end apart: 44 -> 2, of which waited for: 41 -> 2; matrix products, arithmetic and copies ran while one was open for 6% -> 0% of each run, Pallas kernels for 0% -> 0%
where the time goes in v2:
time: 67 us; the launch traced here: 66.7 us
  blocking collectives  45.9 us (69%)
  Pallas kernels  13.4 us (20%)
  waiting for transfers between devices  3.34 us (5%)
  starting transfers between devices  2.05 us (3%)
  local copies, waits for them, and re-layouts  1.99 us (3%)
    all_to_all x1, blocking collectives, strips_local(): mine = lax.all_to_all(blocks, 'space', 0, 0)  29.8 us
    all_to_all x1, blocking collectives, strips_local(): strips = lax.all_to_all(blocks, 'space', 0, 0)  16.1 us
    pallas_call x4, Pallas kernels, on_core(): pl.pallas_call(kernel, out_shape=shapes, in_specs=in_specs, out_specs=[VM...  13.4 us
    ppermute x1, waiting for transfers between devices, strips_local(): other = lax.ppermute(mine, 'tm', [(0, 1), (1, 0)])  2.42 us
    ppermute x1, starting transfers between devices, strips_local(): guess = lax.ppermute(guess, 'tm', [(0, 1)])  2.05 us
    unnamed x4, local copies, waits for them, and re-layouts  1.99 us
  transfers between devices with their start and end apart: 2, of which 2 were waited for; matrix products, arithmetic and copies ran while one was open for 0% of the time, Pallas kernels for 0%

profile of v2, /device:TPU:0, one launch (start us, length us, event | category | flops | bytes accessed | tf_op | source)
XLA Modules:
  0.0 66.7 jit_solution(9578581873729169476)
XLA Ops:
  0.0 0.0 copy-start
  0.0 1.0 %copy-done = f32[2,192,256]{2,1,0:T(8,128)S(1)} copy-done((f32[2,192,256]{2,1,0:T(8,128)S(1)}, f32[2,192,256]{2,1,0:T(8,128)}, u32[]{:S(2)}) %copy-start) | copy-done | bytes 393240
  1.0 0.0 copy-start.1
  1.0 1.0 %copy-done.1 = f32[2,192,256]{2,1,0:T(8,128)S(1)} copy-done((f32[2,192,256]{2,1,0:T(8,128)S(1)}, f32[2,192,256]{2,1,0:T(8,128)}, u32[]{:S(2)}) %copy-start.1) | copy-done | bytes 393240
  2.0 2.8 %shard_map.28 = f32[8,216,128]{2,1,0:T(8,128)S(1)} custom-call(s32[1]{0:T(128)} %bitcast.tm_ref, f32[2,192,256]{2,1,0:T(8,128)S(1)} %copy-done, f32[2,192,256]{2,1,0:T(8,128)S(1)} %copy-done.1), custom_call_target="tpu_custom_call" | custom-call | tf_op jit(solution)/shard_map/pallas_call | solution.py:477
  4.8 29.8 %all_to_all.10.mine = f32[8,216,128]{2,1,0:T(8,128)S(1)} all-to-all(f32[8,216,128]{2,1,0:T(8,128)S(1)} %shard_map.28), channel_id=1, replica_groups=mesh['groups'=2,'tm'=2,'space'=8] {'space'}, dimensions={0} | all-to-all | bytes 1769472 | tf_op jit(solution)/shard_map/all_to_all | solution.py:501
  34.6 0.0 collective-permute-start
  34.6 2.4 %collective-permute-done.other = f32[8,216,128]{2,1,0:T(8,128)S(1)} collective-permute-done((f32[8,216,128]{2,1,0:T(8,128)S(1)}, f32[8,216,128]{2,1,0:T(8,128)S(1)}, u32[]{:S(2)}, u32[]{:S(2)}) %collective-permute-start) | collective-permute-done | bytes 884768 | tf_op jit(solution)/shard_map/ppermute | solution.py:502
  37.0 8.1 %shard_map.29 = (f32[8,96,128]{2,1,0:T(8,128)S(1)}, f32[8,24,128]{2,1,0:T(8,128)S(1)}) custom-call(s32[1]{0:T(128)} %bitcast.tm_ref, f32[8,216,128]{2,1,0:T(8,128)S(1)} %all_to_all.10.mine, f32[8,216,128]{2,1,0:T(8,128)S(1)} %collective-permute-done.other), custom_call_target="tpu_custom_call" | custom-call | tf_op jit(solution)/shard_map/pallas_call | solution.py:477
  45.1 2.0 %collective-permute-start.1 = (f32[8,24,128]{2,1,0:T(8,128)S(1)}, f32[8,24,128]{2,1,0:T(8,128)S(1)}, u32[]{:S(2)}, u32[]{:S(2)}) collective-permute-start(f32[8,24,128]{2,1,0:T(8,128)S(1)} %get-tuple-element.8), channel_id=1, source_target_pairs={{0,8},{1,9},{2,10},{3,11},{4,12},{5,13},{6,14},{7,15},{16,24},{17,... | collective-permute-start | bytes 294920 | tf_op jit(solution)/shard_map/ppermute | solution.py:514
  47.2 0.9 %collective-permute-done.1.guess = f32[8,24,128]{2,1,0:T(8,128)S(1)} collective-permute-done((f32[8,24,128]{2,1,0:T(8,128)S(1)}, f32[8,24,128]{2,1,0:T(8,128)S(1)}, u32[]{:S(2)}, u32[]{:S(2)}) %collective-permute-start.1) | collective-permute-done | bytes 98336 | tf_op jit(solution)/shard_map/ppermute | solution.py:514
  48.1 0.1 shard_map.30
  48.2 16.1 %all_to_all.11.strips = f32[8,104,128]{2,1,0:T(8,128)S(1)} all-to-all(f32[8,104,128]{2,1,0:T(8,128)S(1)} %shard_map.30), channel_id=1, replica_groups=mesh['groups'=2,'tm'=2,'space'=8] {'space'}, dimensions={0} | all-to-all | bytes 851968 | tf_op jit(solution)/shard_map/all_to_all | solution.py:516
  64.3 2.4 %shard_map.31 = f32[2,192,256]{2,1,0:T(8,128)} custom-call(f32[8,104,128]{2,1,0:T(8,128)S(1)} %all_to_all.11.strips), custom_call_target="tpu_custom_call" | custom-call | tf_op jit(solution)/shard_map/pallas_call | solution.py:477
Async XLA Ops:
  0.0 1.0 %copy-start = (f32[2,192,256]{2,1,0:T(8,128)S(1)}, f32[2,192,256]{2,1,0:T(8,128)}, u32[]{:S(2)}) copy-start(f32[2,192,256]{2,1,0:T(8,128)} %initial_hbm.1) | copy-start | bytes 1179652
  1.0 1.0 %copy-start.1 = (f32[2,192,256]{2,1,0:T(8,128)S(1)}, f32[2,192,256]{2,1,0:T(8,128)}, u32[]{:S(2)}) copy-start(f32[2,192,256]{2,1,0:T(8,128)} %reaction_hbm.1) | copy-start | bytes 1179652
  34.6 2.4 %collective-permute-start = (f32[8,216,128]{2,1,0:T(8,128)S(1)}, f32[8,216,128]{2,1,0:T(8,128)S(1)}, u32[]{:S(2)}, u32[]{:S(2)}) collective-permute-start(f32[8,216,128]{2,1,0:T(8,128)S(1)} %all_to_all.10.mine), channel_id=1, source_target_pairs={{0,8},{8,0},{1,9},{9,1},{2,10},{10,2},{3,11},{11,3},{4,12},{12,4},... | collective-permute-start | bytes 2654216 | tf_op jit(solution)/shard_map/ppermute | solution.py:502
  45.1 3.0 %collective-permute-start.1 = (f32[8,24,128]{2,1,0:T(8,128)S(1)}, f32[8,24,128]{2,1,0:T(8,128)S(1)}, u32[]{:S(2)}, u32[]{:S(2)}) collective-permute-start(f32[8,24,128]{2,1,0:T(8,128)S(1)} %get-tuple-element.8), channel_id=1, source_target_pairs={{0,8},{1,9},{2,10},{3,11},{4,12},{5,13},{6,14},{7,15},{16,24},{17,... | collective-permute-start | bytes 294920 | tf_op jit(solution)/shard_map/ppermute | solution.py:514

commit v3 on v2

--- a/solution.py
+++ b/solution.py
@@ -143,6 +143,8 @@
 LANES = 128
 PAD = 8
 SPILL_TURNS = (0, 4, 8)
+EXCHANGES = ((7, 1), (6, 5), (2, 4), (3, 0))
+EDGE_ROWS = 16
 FINE_CHUNKS = ((0, 16), (32, 16), (16, 16))
 HALF_CHUNKS = ((0, 24), (24, 24))
 QUARTER_CHUNKS = ((0, 24),)
@@ -209,87 +211,71 @@
         wrap_rows(d, planes, rows, quarter)
 
 
-def pack_kernel(tm_ref, initial_hbm, reaction_hbm, out, initial, reaction, sums, arrived):
-    tm = tm_ref[0]
-    copies = [
-        pltpu.make_async_copy(initial_hbm, initial, arrived.at[0]),
-        pltpu.make_async_copy(reaction_hbm, reaction, arrived.at[1]),
-    ]
-    for copy in copies:
-        copy.start()
-    for copy in copies:
-        copy.wait()
-
-    count = out.shape[0]
-    rows = initial.shape[1] // 4
+def sent_to(masks):
+    return lax.axis_index("space") ^ jnp.where(lax.axis_index("tm") == 0, masks[0], masks[1])
+
+
+def prepare_kernel(turns, field, turned, edges, sums, coarse):
+    rows = field.shape[1] // 4
     part = rows // 2
-    step = 16
-    lane = iota((step, LANES), 1)
+    lane = iota((rows, LANES), 1)
     low_half = lane < 64
     even_odd = jnp.where(low_half, 2 * lane, 2 * lane - (LANES - 1))
     odd_even = jnp.where(low_half, 2 * lane + 1, 2 * lane - LANES)
-
-    def columns(left, right):
-        a, b = take(left, even_odd), take(right, odd_even)
-        return jnp.where(low_half, a, b), roll(jnp.where(low_half, b, a), 64)
-
     for z in range(2):
-        for first in range(0, rows, step):
-            turned = ([], [])
-            for j in range(4):
-                at = slice(j * rows + first, j * rows + first + step)
-                tiles = [
-                    jnp.where(tm == 0, initial[z, at, t * LANES : (t + 1) * LANES], reaction[z, at, t * LANES : (t + 1) * LANES])
-                    for t in range(2)
-                ]
-                for e, x in enumerate(columns(*tiles)):
-                    turned[e].append(roll(x, 32 * j))
-            for s in range(count):
-                by = 16 * s - 8
-                quarter = ((lane - by) & (LANES - 1)) >> 5
-                for e in range(2):
-                    r = turned[e]
-                    x = jnp.where(quarter == 0, r[0], jnp.where(quarter == 1, r[1], jnp.where(quarter == 2, r[2], r[3])))
-                    at = (2 * z + e) * rows + first
-                    out[s, at : at + step, :] = roll(x, -by)
-
-    lane = iota((part, LANES), 1)
-    here = lane & 63
-    for t in range(2):
-
-        @pl.when(tm == t)
-        def _(t=t):
-            def small(field):
-                parts = []
-                for h in range(2):
-                    for first in range(0, rows, step):
-                        at = slice((2 * h + t) * rows + first, (2 * h + t) * rows + first + step)
-                        tiles = [field[0, at, c * LANES : (c + 1) * LANES] + field[1, at, c * LANES : (c + 1) * LANES] for c in range(2)]
-                        even, odd = columns(*tiles)
-                        sums[first : first + step, :] = (even + odd) * 0.125
-                    parts.append(sums[pl.ds(0, part, 2), :] + sums[pl.ds(1, part, 2), :])
-                return parts
-
-            fields, rates = small(initial), small(reaction)
-            for s in range(count):
-                halves = []
-                for h in range(2):
-                    at = 64 * h
-                    own = roll(fields[h], 12 - 16 * s + at)
-                    left = roll(rates[h], 52 - 16 * s + at)
-                    right = roll(rates[h], 20 - 16 * s + at)
-                    halves.append(jnp.where(here < 40, own, jnp.where(here < 44, left, jnp.where(here < 48, right, 0.0))))
-                out[s, 4 * rows : 4 * rows + part, :] = jnp.where(lane < 64, halves[0], halves[1])
+        for j in range(4):
+            at = slice(j * rows, (j + 1) * rows)
+            left, right = take(field[z, at, :LANES], even_odd), take(field[z, at, LANES:], odd_even)
+            even = jnp.where(low_half, left, right)
+            odd = roll(jnp.where(low_half, right, left), 64)
+            for e, x in enumerate((even, odd)):
+                to = ((2 * z + e) * 4 + j) * rows
+                turned[to : to + rows, :] = roll(x, 32 * j)
+            if z == 0:
+                sums[at, :] = even + odd
+            else:
+                sums[at, :] = (sums[at, :] + (even + odd)) * 0.125
+    for j in range(4):
+        at = j * rows
+        coarse[j * part : (j + 1) * part, :] = sums[pl.ds(at, part, 2), :] + sums[pl.ds(at + 1, part, 2), :]
+    for g in range(2 * rows // EDGE_ROWS):
+        x = coarse[g * EDGE_ROWS : (g + 1) * EDGE_ROWS, :]
+        place = 64 * (g // 3) + 16 * (g % 3)
+        for n, by in enumerate(turns):
+            to = (2 * g + n) * EDGE_ROWS
+            edges[to : to + EDGE_ROWS, :] = roll(x, place + by)
+
+
+def fill_kernel(initial_turned, initial_edges, reaction_turned, reaction_edges, *blocks):
+    rows = initial_turned.shape[0] // 16
+    dests = [sent_to(masks) for masks in EXCHANGES] + [lax.axis_index("space")]
+    for dest, block in zip(dests, blocks):
+        back = (8 - 16 * dest) & (LANES - 1)
+        quarter = ((iota((rows, LANES), 1) + back) & (LANES - 1)) >> 5
+        for n in range(8):
+            turned = (initial_turned, reaction_turned)[n // 4]
+            x = [turned[(4 * (n % 4) + j) * rows : (4 * (n % 4) + j + 1) * rows, :] for j in range(4)]
+            x = jnp.where(quarter == 0, x[0], jnp.where(quarter == 1, x[1], jnp.where(quarter == 2, x[2], x[3])))
+            block[n * rows : (n + 1) * rows, :] = pltpu.roll(x, back, 1)
+        back = (-16 * dest) & (LANES - 1)
+        slot = ((iota((EDGE_ROWS, LANES), 1) + back) & (LANES - 1)) >> 2
+        x = jnp.zeros((EDGE_ROWS, LANES), jnp.float32)
+        for g in range(2 * rows // EDGE_ROWS):
+            for n in range(4):
+                edges = (initial_edges, reaction_edges)[n // 2]
+                at = (2 * g + n % 2) * EDGE_ROWS
+                x = jnp.where(slot == 16 * (g // 3) + 4 * (g % 3) + n, edges[at : at + EDGE_ROWS, :], x)
+        block[8 * rows : 8 * rows + EDGE_ROWS, :] = pltpu.roll(x, back, 1)
 
 
 def march_kernel(
-    tm_ref, mine, other, field_out, guess_out,
-    even_a, odd_a, even_b, odd_b, even_keep, odd_keep, wide_a, wide_b, wide_keep, small_a, small_b, small_keep, first_guess, second_guess,
+    own_block, mine_0, mine_1, mine_2, mine_3, other_0, other_1, other_2, other_3, field_out, guess_out,
+    even_a, odd_a, even_b, odd_b, even_keep, odd_keep, wide_a, wide_b, wide_keep, small_a, small_b, small_keep, first_guess, second_guess, sums,
 ):
-    tm = tm_ref[0]
-    count = mine.shape[0]
-    planes = 2 * count
-    rows = even_keep.shape[0] // planes
+    tm, space = lax.axis_index("tm"), lax.axis_index("space")
+    rows = (own_block.shape[0] - EDGE_ROWS) // 8
+    planes = even_keep.shape[0] // rows
+    count = planes // 2
     part = rows // 2
     height, wide_height, small_height = rows + 2 * PAD, rows + 2 * PAD, part + 2 * PAD
     lead, centre, slope, lows = weights(*F_CONST)
@@ -300,26 +286,48 @@
     lane = iota((part, LANES), 1)
     even_quarter = ((lane >> 5) & 1) == 0
 
-    in_half = lane & 63
-    for k in range(count):
-        total = None
-        for z in range(2):
-            for e in range(2):
-                at = slice((2 * z + e) * rows, (2 * z + e + 1) * rows)
-                to = slice((2 * k + z) * rows, (2 * k + z + 1) * rows)
-                rate = jnp.where(tm == 0, other[k, at, :], mine[k, at, :])
-                fine_keep[e][to, :] = centre - slope * rate
-                total = rate if total is None else total + rate
-        wide_b[0:rows, :] = total * 0.125
-        rate = wide_b[pl.ds(0, part, 2), :] + wide_b[pl.ds(1, part, 2), :]
-        small_keep[k * part : (k + 1) * part, :] = small_centre - small_slope * rate
-        at = slice(4 * rows, 4 * rows + part)
-        windows = [jnp.where(tm == 0, mine[k, at, :], other[k, at, :]), jnp.where(tm == 0, other[k, at, :], mine[k, at, :])]
-        for n, by in ((0, 4), (1, -28)):
-            to = (k + 1) * wide_height + PAD + n * part
-            wide_a[to : to + part, :] = windows[n]
-            x = jnp.where(in_half < 4, roll(windows[n], -40), jnp.where(inside(in_half, 36, 40), roll(windows[n], -8), roll(rate, by)))
-            wide_keep[k * rows + n * part : k * rows + (n + 1) * part, :] = small_centre - small_slope * x
+    def some(index, height, first, size):
+        return pl.ds(pl.multiple_of(index * height + first, 8), size)
+
+    in_half = iota((rows, LANES), 1) & 63
+    left, right = in_half < 4, inside(in_half, 36, 40)
+    blocks = [(own_block, None, space)]
+    for masks, mine, other in zip(EXCHANGES, (mine_0, mine_1, mine_2), (other_0, other_1, other_2)):
+        blocks.append((mine, None, sent_to(masks)))
+        blocks.append((other, None, sent_to(masks[::-1])))
+    blocks.append((mine_3, other_3, space ^ EXCHANGES[3][0]))
+    for number, (block, if_second, k) in enumerate(blocks):
+
+        def read(first, size, block=block, if_second=if_second):
+            if if_second is None:
+                return block[first : first + size, :]
+            return jnp.where(tm == 0, block[first : first + size, :], if_second[first : first + size, :])
+
+        totals = []
+        for n in range(2):
+            total = None
+            for z in range(2):
+                for e in range(2):
+                    x = read((4 * n + 2 * z + e) * rows, rows)
+                    if n == 0:
+                        fine_a[e][some(2 * k + z + 1, height, PAD, rows), :] = x
+                    else:
+                        fine_keep[e][some(2 * k + z, rows, 0, rows), :] = centre - slope * x
+                    total = x if total is None else total + x
+            temp = (2 * number + n) * rows
+            sums[temp : temp + rows, :] = total * 0.125
+            totals.append(temp)
+        edge = read(8 * rows, EDGE_ROWS)
+        small = [sums[pl.ds(temp, part, 2), :] + sums[pl.ds(temp + 1, part, 2), :] for temp in totals]
+        small_keep[some(k, part, 0, part), :] = small_centre - small_slope * small[1]
+        windows = []
+        for n in range(2):
+            inner = jnp.concatenate([roll(small[n], 4), roll(small[n], -28)], 0)
+            lefts = jnp.concatenate([roll(edge, -16 * g - 8 * n) for g in range(rows // EDGE_ROWS)], 0)
+            rights = jnp.concatenate([roll(edge, 32 - 16 * g - 8 * n) for g in range(rows // EDGE_ROWS)], 0)
+            windows.append(jnp.where(left, lefts, jnp.where(right, rights, inner)))
+        wide_a[some(k + 1, wide_height, PAD, rows), :] = windows[0]
+        wide_keep[some(k, rows, 0, rows), :] = small_centre - small_slope * windows[1]
     wrap_rows(wide_a, count, rows, 64)
 
     for _ in range(CSTEPS // 2):
@@ -333,18 +341,6 @@
         first_guess[k * part : (k + 1) * part, :] = guess
         to = (k + 1) * small_height + PAD
         small_a[to : to + part, :] = guess
-        for z in range(2):
-            for e in range(2):
-                to = (2 * k + z + 1) * height + PAD
-
-                @pl.when(tm == 0)
-                def _(k=k, z=z, e=e, to=to):
-                    fine_a[e][to : to + rows, :] = mine[k, (2 * z + e) * rows : (2 * z + e + 1) * rows, :]
-
-                @pl.when(tm != 0)
-                def _(e=e, to=to, guess=guess):
-                    fine_a[e][pl.ds(to, part, 2), :] = guess
-                    fine_a[e][pl.ds(to + 1, part, 2), :] = guess
 
     def coarse_run():
         wrap_rows(small_a, count, part, 32)
@@ -354,6 +350,13 @@
 
     @pl.when(tm != 0)
     def _():
+        for k in range(count):
+            guess = first_guess[k * part : (k + 1) * part, :]
+            for z in range(2):
+                for e in range(2):
+                    to = (2 * k + z + 1) * height + PAD
+                    fine_a[e][pl.ds(to, part, 2), :] = guess
+                    fine_a[e][pl.ds(to + 1, part, 2), :] = guess
         coarse_run()
         for k in range(count):
             at = (k + 1) * small_height + PAD
@@ -394,30 +397,36 @@
             guess_out[k] = small_a[at : at + part, :] * small_scale
 
 
-def send_kernel(field, guess, out):
+def send_kernel(field, guess, *blocks):
+    tm, space = lax.axis_index("tm"), lax.axis_index("space")
     part = guess.shape[1]
     rows = 2 * part
     in_quarter = iota((part, LANES), 1) & 31
     own = inside(in_quarter, 8, 24)
     spill = (inside(in_quarter, 4, 8) | inside(in_quarter, 24, 28))[:8]
-    for k in range(guess.shape[0]):
-        mine = guess[k]
+    for k, block in enumerate(blocks):
+        dest = space ^ k
+        mine = jnp.where(tm == 0, 0.0, guess[dest])
         both = jnp.where(own, mine, roll(mine, 16))
         for e in range(2):
             for odd in range(2):
                 at = pl.ds(e * rows + odd, part, 2)
-                out[k, at, :] = field[k, at, :] + both
+                block[at, :] = field[dest, at, :] + both
         packed = None
         for g, by in enumerate(SPILL_TURNS):
             piece = roll(jnp.where(spill, mine[8 * g : 8 * g + 8], 0.0), by)
             packed = piece if packed is None else packed + piece
-        out[k, 2 * rows : 2 * rows + 8, :] = packed
-
-
-def unpack_kernel(strips, out, spilled):
-    count = strips.shape[0]
+        block[2 * rows : 2 * rows + 8, :] = packed
+
+
+def unpack_kernel(*refs):
+    blocks, (out_hbm, strips, spilled, out, left) = refs[:-5], refs[-5:]
+    count = len(blocks)
     rows = out.shape[1] // 4
     part = rows // 2
+    space = lax.axis_index("space")
+    for k, block in enumerate(blocks):
+        strips[space ^ k] = block[...]
 
     def lined_up(read, first, size):
         quarter = ((iota((size, LANES), 1) - first) & (LANES - 1)) >> 5
@@ -446,42 +455,43 @@
             spilled[pl.ds(at, 8, 2), :] = x
             spilled[pl.ds(at + 1, 8, 2), :] = x
 
-    step = 16
-    lane = iota((step, LANES), 1)
+    lane = iota((rows, LANES), 1)
     low_half = lane < 64
     from_first = ((lane & 1) << 6) + (lane >> 1)
     from_second = from_first ^ 64
     hit = [inside(lane, 16 * s, 16 * s + 16) for s in range(count)]
-    for first in range(0, rows, step):
-        pieces = [
-            list(lined_up(lambda s, e=e: strips[s, e * rows + first : e * rows + first + step, :], 8, step)) for e in range(2)
-        ]
-        for z in range(2):
-            parts = [[roll(x, 16 * c - 8 - 16 * z) for c, x in enumerate(pieces[e])] for e in range(2)]
-            for j in range(4):
-                at = slice(j * rows + first, j * rows + first + step)
-                more = spilled[at, :]
-                even, odd = (at_strips(parts[e], j, hit) + more for e in range(2))
-                odd = roll(odd, 64)
-                out[z, at, :LANES] = take(jnp.where(low_half, even, odd), from_first)
-                out[z, at, LANES:] = take(jnp.where(low_half, odd, even), from_second)
+    copies = []
+    for z in range(2):
+        parts = []
+        for e in range(2):
+            pieces = lined_up(lambda s, e=e: strips[s, e * rows : (e + 1) * rows, :], 8, rows)
+            parts.append([roll(x, 16 * c - 8 - 16 * z) for c, x in enumerate(pieces)])
+        for j in range(4):
+            at = slice(j * rows, (j + 1) * rows)
+            more = spilled[at, :]
+            even, odd = (at_strips(parts[e], j, hit) + more for e in range(2))
+            odd = roll(odd, 64)
+            out[z, at, :LANES] = take(jnp.where(low_half, even, odd), from_first)
+            out[z, at, LANES:] = take(jnp.where(low_half, odd, even), from_second)
+        copies.append(pltpu.make_async_copy(out.at[z], out_hbm.at[z], left.at[z]))
+        copies[-1].start()
+    for copy in copies:
+        copy.wait()
 
 
 VMEM = pl.BlockSpec(memory_space=pltpu.VMEM)
-SMEM = pl.BlockSpec(memory_space=pltpu.SMEM)
-ANY = pl.BlockSpec(memory_space=pl.ANY)
-
-
-def on_core(kernel, in_specs, out_shapes, scratch, *args):
+
+
+def on_core(kernel, inputs, out_shapes, scratch=(), out_spec=VMEM):
     shapes = [jax.ShapeDtypeStruct(s, jnp.float32) for s in out_shapes]
     return pl.pallas_call(
         kernel,
         out_shape=shapes,
-        in_specs=in_specs,
-        out_specs=[VMEM] * len(shapes),
+        in_specs=[VMEM] * len(inputs),
+        out_specs=[out_spec] * len(shapes),
         scratch_shapes=[pltpu.VMEM(s, jnp.float32) if isinstance(s, tuple) else s for s in scratch],
         compiler_params=pltpu.CompilerParams(vmem_limit_bytes=48 * 1024 * 1024),
-    )(*args)
+    )(*inputs)
 
 
 def strips_local(initial, reaction):
@@ -490,31 +500,45 @@
     rows = nx // 4
     part = rows // 2
     planes = 2 * count
-    tm = lax.axis_index("tm").astype(jnp.int32).reshape(1)
-    (blocks,) = on_core(
-        pack_kernel,
-        [SMEM, ANY, ANY],
-        [(count, 4 * rows + part, LANES)],
-        [initial.shape, reaction.shape, (rows, LANES), pltpu.SemaphoreType.DMA((2,))],
-        tm, initial, reaction,
-    )
-    mine = lax.all_to_all(blocks, "space", 0, 0)
-    other = lax.ppermute(mine, "tm", [(0, 1), (1, 0)])
+    block = (8 * rows + EDGE_ROWS, LANES)
+    prepared = []
+    for field, turns in ((initial, (12, -20)), (reaction, (20, -12))):
+        prepared += on_core(
+            functools.partial(prepare_kernel, turns),
+            [field],
+            [(16 * rows, LANES), (4 * rows, LANES)],
+            [(4 * rows, LANES), (2 * rows, LANES)],
+        )
+    *blocks, own_block = on_core(fill_kernel, prepared, [block] * 5)
+    mine, other = [], []
+    for x, masks in zip(blocks, EXCHANGES):
+        pairs = [(t * count + i, t * count + (i ^ masks[t])) for t in range(2) if masks[t] for i in range(count)]
+        mine.append(lax.ppermute(x, ("tm", "space"), pairs))
+        other.append(lax.ppermute(mine[-1], "tm", [(0, 1), (1, 0)]))
     fine = ((planes + 2) * (rows + 2 * PAD), LANES)
     wide = ((count + 2) * (rows + 2 * PAD), LANES)
     small = ((count + 2) * (part + 2 * PAD), LANES)
     small_cells = (count * part, LANES)
     field, guess = on_core(
         march_kernel,
-        [SMEM, VMEM, VMEM],
+        [own_block, *mine, *other],
         [(count, 2 * rows, LANES), (count, part, LANES)],
-        [fine] * 4 + [(planes * rows, LANES)] * 2 + [wide, wide, (count * rows, LANES), small, small] + [small_cells] * 3,
-        tm, mine, other,
+        [fine] * 4
+        + [(planes * rows, LANES)] * 2
+        + [wide, wide, (count * rows, LANES), small, small]
+        + [small_cells] * 3
+        + [(planes * rows, LANES)],
     )
-    guess = lax.ppermute(guess, "tm", [(0, 1)])
-    (blocks,) = on_core(send_kernel, [VMEM, VMEM], [(count, 2 * rows + 8, LANES)], [], field, guess)
-    strips = lax.all_to_all(blocks, "space", 0, 0)
-    (out,) = on_core(unpack_kernel, [VMEM], [initial.shape], [(nx, LANES)], strips)
+    guess = lax.ppermute(guess, "tm", [(0, 1), (1, 0)])
+    own_strip, *strips = on_core(send_kernel, [field, guess], [(2 * rows + 8, LANES)] * count)
+    strips = [lax.ppermute(x, "space", [(i, i ^ k) for i in range(count)]) for k, x in enumerate(strips, 1)]
+    (out,) = on_core(
+        unpack_kernel,
+        [own_strip, *strips],
+        [initial.shape],
+        [(count, 2 * rows + 8, LANES), (nx, LANES), initial.shape, pltpu.SemaphoreType.DMA((2,))],
+        pl.BlockSpec(memory_space=pltpu.HBM),
+    )
     return out[None]
 
 

time: 67 us -> 56.1 us (0.84)
  blocking collectives: 45.9 us -> 0 us
  starting transfers between devices: 2.05 us -> 29.4 us
  waiting for transfers between devices: 3.34 us -> 13.7 us
  Pallas kernels: 13.4 us -> 11.5 us
  local copies, waits for them, and re-layouts: 1.99 us -> 1.25 us
    all_to_all x2 -> x0, blocking collectives: 45.9 us -> none  [the longest x1 29.8 us: strips_local(): mine = lax.all_to_all(blocks, 'space', 0, 0)]
    ppermute x2 -> x16, starting transfers between devices: 2.05 us -> 29.4 us  [the longest x7 12.6 us: strips_local(): lax.ppermute(x, 'space', [(i, i ^ k) for i in range(count)])]
    ppermute x2 -> x16, waiting for transfers between devices: 3.34 us -> 13.7 us  [the longest x4 5.96 us: strips_local(): mine.append(lax.ppermute(x, ('tm', 'space'), pairs))]
    pallas_call x4 -> x6, Pallas kernels: 13.4 us -> 11.5 us  [on_core(): pl.pallas_call(kernel, out_shape=shapes, in_specs=[VMEM] * len(inputs), o...]
    unnamed x4, local copies, waits for them, and re-layouts: 1.99 us -> 1.25 us
  transfers between devices with their start and end apart: 2 -> 16, of which waited for: 2 -> 7; matrix products, arithmetic and copies ran while one was open for 0% -> 0% of each run, Pallas kernels for 0% -> 0%
where the time goes in v3:
time: 56.1 us; the launch traced here: 55.9 us
  starting transfers between devices  29.4 us (52%)
  waiting for transfers between devices  13.7 us (24%)
  Pallas kernels  11.5 us (20%)
  local copies, waits for them, and re-layouts  1.25 us (2%)
    ppermute x7, starting transfers between devices, strips_local(): lax.ppermute(x, 'space', [(i, i ^ k) for i in range(count)])  12.6 us
    pallas_call x6, Pallas kernels, on_core(): pl.pallas_call(kernel, out_shape=shapes, in_specs=[VMEM] * len(inputs), o...  11.5 us
    ppermute x4, starting transfers between devices, strips_local(): mine.append(lax.ppermute(x, ('tm', 'space'), pairs))  10 us
    ppermute x4, starting transfers between devices, strips_local(): other.append(lax.ppermute(mine[-1], 'tm', [(0, 1), (1, 0)]))  6.35 us
    ppermute x4, waiting for transfers between devices, strips_local(): mine.append(lax.ppermute(x, ('tm', 'space'), pairs))  5.96 us
    ppermute x7, waiting for transfers between devices, strips_local(): lax.ppermute(x, 'space', [(i, i ^ k) for i in range(count)])  5.33 us
    ppermute x4, waiting for transfers between devices, strips_local(): other.append(lax.ppermute(mine[-1], 'tm', [(0, 1), (1, 0)]))  1.44 us
    unnamed x4, local copies, waits for them, and re-layouts  1.25 us
  transfers between devices with their start and end apart: 16, of which 7 were waited for; matrix products, arithmetic and copies ran while one was open for 0% of the time, Pallas kernels for 0%

profile of v3, /device:TPU:0, one launch (start us, length us, event | category | flops | bytes accessed | tf_op | source)
XLA Modules:
  0.0 55.9 jit_solution(4090897525332883167)
XLA Ops:
  0.0 0.0 copy-start
  0.0 1.0 %copy-done = f32[2,192,256]{2,1,0:T(8,128)S(1)} copy-done((f32[2,192,256]{2,1,0:T(8,128)S(1)}, f32[2,192,256]{2,1,0:T(8,128)}, u32[]{:S(2)}) %copy-start) | copy-done | bytes 393240
  1.0 0.0 copy-start.1
  1.0 0.7 %shard_map.28 = (f32[768,128]{1,0:T(8,128)S(1)}, f32[192,128]{1,0:T(8,128)S(1)}) custom-call(f32[2,192,256]{2,1,0:T(8,128)S(1)} %copy-done), custom_call_target="tpu_custom_call" | custom-call | tf_op jit(solution)/shard_map/pallas_call | solution.py:487
  1.7 0.3 copy-done.1
  2.0 0.7 %shard_map.29 = (f32[768,128]{1,0:T(8,128)S(1)}, f32[192,128]{1,0:T(8,128)S(1)}) custom-call(f32[2,192,256]{2,1,0:T(8,128)S(1)} %copy-done.1), custom_call_target="tpu_custom_call" | custom-call | tf_op jit(solution)/shard_map/pallas_call | solution.py:487
  2.7 0.4 shard_map.30
  3.1 6.0 %collective-permute-start = (f32[400,128]{1,0:T(8,128)S(1)}, f32[400,128]{1,0:T(8,128)S(1)}, u32[]{:S(2)}, u32[]{:S(2)}) collective-permute-start(f32[400,128]{1,0:T(8,128)S(1)} %get-tuple-element.29), channel_id=1, source_target_pairs={{0,7},{1,6},{2,5},{3,4},{4,3},{5,2},{6,1},{7,0},{8,9},{9,8},{10,11... | collective-permute-start | bytes 614408 | tf_op jit(solution)/shard_map/ppermute | solution.py:516
  9.1 0.2 collective-permute-start.1
  9.4 0.0 collective-permute-start.2
  9.4 3.8 %collective-permute-start.3 = (f32[400,128]{1,0:T(8,128)S(1)}, f32[400,128]{1,0:T(8,128)S(1)}, u32[]{:S(2)}, u32[]{:S(2)}) collective-permute-start(f32[400,128]{1,0:T(8,128)S(1)} %get-tuple-element.32), channel_id=1, source_target_pairs={{0,3},{1,2},{2,1},{3,0},{4,7},{5,6},{6,5},{7,4},{16,19},{17,18},{1... | collective-permute-start | bytes 614408 | tf_op jit(solution)/shard_map/ppermute | solution.py:516
  13.2 1.7 %collective-permute-done.mine_0 = f32[400,128]{1,0:T(8,128)S(1)} collective-permute-done((f32[400,128]{1,0:T(8,128)S(1)}, f32[400,128]{1,0:T(8,128)S(1)}, u32[]{:S(2)}, u32[]{:S(2)}) %collective-permute-start) | collective-permute-done | bytes 204832 | tf_op jit(solution)/shard_map/ppermute | solution.py:516
  14.9 0.0 collective-permute-start.4
  14.9 4.2 %collective-permute-done.1.mine_1 = f32[400,128]{1,0:T(8,128)S(1)} collective-permute-done((f32[400,128]{1,0:T(8,128)S(1)}, f32[400,128]{1,0:T(8,128)S(1)}, u32[]{:S(2)}, u32[]{:S(2)}) %collective-permute-start.1) | collective-permute-done | bytes 204832 | tf_op jit(solution)/shard_map/ppermute | solution.py:516
  19.1 3.9 %collective-permute-start.5 = (f32[400,128]{1,0:T(8,128)S(1)}, f32[400,128]{1,0:T(8,128)S(1)}, u32[]{:S(2)}, u32[]{:S(2)}) collective-permute-start(f32[400,128]{1,0:T(8,128)S(1)} %collective-permute-done.1.mine_1), channel_id=1, source_target_pairs={{0,8},{8,0},{1,9},{9,1},{2,10},{10,2},{3,11},{11,3},{4,12},{12,4},... | collective-permute-start | bytes 614408 | tf_op jit(solution)/shard_map/ppermute | solution.py:517
  23.0 0.0 collective-permute-done.2.mine_2
  23.0 2.5 %collective-permute-start.6 = (f32[400,128]{1,0:T(8,128)S(1)}, f32[400,128]{1,0:T(8,128)S(1)}, u32[]{:S(2)}, u32[]{:S(2)}) collective-permute-start(f32[400,128]{1,0:T(8,128)S(1)} %collective-permute-done.2.mine_2), channel_id=1, source_target_pairs={{0,8},{8,0},{1,9},{9,1},{2,10},{10,2},{3,11},{11,3},{4,12},{12,4},... | collective-permute-start | bytes 614408 | tf_op jit(solution)/shard_map/ppermute | solution.py:517
  25.5 0.0 collective-permute-done.3.mine_3
  25.5 0.0 collective-permute-start.7
  25.5 0.0 collective-permute-done.4.other_0
  25.5 0.0 collective-permute-done.5.other_1
  25.5 1.1 %collective-permute-done.6.other_2 = f32[400,128]{1,0:T(8,128)S(1)} collective-permute-done((f32[400,128]{1,0:T(8,128)S(1)}, f32[400,128]{1,0:T(8,128)S(1)}, u32[]{:S(2)}, u32[]{:S(2)}) %collective-permute-start.6) | collective-permute-done | bytes 204832 | tf_op jit(solution)/shard_map/ppermute | solution.py:517
  26.5 0.4 collective-permute-done.7.other_3
  26.9 7.7 %shard_map.31 = (f32[8,96,128]{2,1,0:T(8,128)S(1)}, f32[8,24,128]{2,1,0:T(8,128)S(1)}) custom-call(f32[400,128]{1,0:T(8,128)S(1)} %get-tuple-element.28.own_block, f32[400,128]{1,0:T(8,128)S(1)} %collective-permute-done.mine_0, f32[400,128]{1,0:T(8,128)S(1)} %collective-permute-done.1.mine_1, f32[400,128]{1,0:T(8,128)S(1)} %collective-permute-done.2.mine_2, ...), custom_call_target="tpu_custom_call" | custom-call | tf_op jit(solution)/shard_map/pallas_call | solution.py:487
  34.7 0.4 collective-permute-start.8
  35.0 1.0 %collective-permute-done.8.guess = f32[8,24,128]{2,1,0:T(8,128)S(1)} collective-permute-done((f32[8,24,128]{2,1,0:T(8,128)S(1)}, f32[8,24,128]{2,1,0:T(8,128)S(1)}, u32[]{:S(2)}, u32[]{:S(2)}) %collective-permute-start.8) | collective-permute-done | bytes 98336 | tf_op jit(solution)/shard_map/ppermute | solution.py:532
  36.0 0.1 shard_map.32
  36.1 2.6 %collective-permute-start.9 = (f32[104,128]{1,0:T(8,128)S(1)}, f32[104,128]{1,0:T(8,128)S(1)}, u32[]{:S(2)}, u32[]{:S(2)}) collective-permute-start(f32[104,128]{1,0:T(8,128)S(1)} %get-tuple-element.36), channel_id=1, source_target_pairs={{0,1},{1,0},{2,3},{3,2},{4,5},{5,4},{6,7},{7,6},{8,9},{9,8},{10,11... | collective-permute-start | bytes 159752 | tf_op jit(solution)/shard_map/ppermute | solution.py:534
  38.7 1.4 %collective-permute-start.10 = (f32[104,128]{1,0:T(8,128)S(1)}, f32[104,128]{1,0:T(8,128)S(1)}, u32[]{:S(2)}, u32[]{:S(2)}) collective-permute-start(f32[104,128]{1,0:T(8,128)S(1)} %get-tuple-element.37), channel_id=1, source_target_pairs={{0,2},{1,3},{2,0},{3,1},{4,6},{5,7},{6,4},{7,5},{8,10},{9,11},{10,... | collective-permute-start | bytes 159752 | tf_op jit(solution)/shard_map/ppermute | solution.py:534
  40.0 0.2 collective-permute-start.11
  40.2 3.8 %collective-permute-start.12 = (f32[104,128]{1,0:T(8,128)S(1)}, f32[104,128]{1,0:T(8,128)S(1)}, u32[]{:S(2)}, u32[]{:S(2)}) collective-permute-start(f32[104,128]{1,0:T(8,128)S(1)} %get-tuple-element.39), channel_id=1, source_target_pairs={{0,4},{1,5},{2,6},{3,7},{4,0},{5,1},{6,2},{7,3},{8,12},{9,13},{10,... | collective-permute-start | bytes 159752 | tf_op jit(solution)/shard_map/ppermute | solution.py:534
  44.0 0.5 collective-permute-start.13
  44.5 0.0 collective-permute-done.9.refs_1_
  44.5 2.6 %collective-permute-start.14 = (f32[104,128]{1,0:T(8,128)S(1)}, f32[104,128]{1,0:T(8,128)S(1)}, u32[]{:S(2)}, u32[]{:S(2)}) collective-permute-start(f32[104,128]{1,0:T(8,128)S(1)} %get-tuple-element.41), channel_id=1, source_target_pairs={{0,6},{1,7},{2,4},{3,5},{4,2},{5,3},{6,0},{7,1},{8,14},{9,15},{10,... | collective-permute-start | bytes 159752 | tf_op jit(solution)/shard_map/ppermute | solution.py:534
  47.1 0.0 collective-permute-done.10.refs_2_
  47.1 1.6 %collective-permute-start.15 = (f32[104,128]{1,0:T(8,128)S(1)}, f32[104,128]{1,0:T(8,128)S(1)}, u32[]{:S(2)}, u32[]{:S(2)}) collective-permute-start(f32[104,128]{1,0:T(8,128)S(1)} %get-tuple-element.42), channel_id=1, source_target_pairs={{0,7},{1,6},{2,5},{3,4},{4,3},{5,2},{6,1},{7,0},{8,15},{9,14},{10,... | collective-permute-start | bytes 159752 | tf_op jit(solution)/shard_map/ppermute | solution.py:534
  48.7 0.0 collective-permute-done.11.refs_3_
  48.7 0.0 collective-permute-done.12.refs_4_
  48.7 3.5 %collective-permute-done.13.refs_5_ = f32[104,128]{1,0:T(8,128)S(1)} collective-permute-done((f32[104,128]{1,0:T(8,128)S(1)}, f32[104,128]{1,0:T(8,128)S(1)}, u32[]{:S(2)}, u32[]{:S(2)}) %collective-permute-start.13) | collective-permute-done | bytes 53280 | tf_op jit(solution)/shard_map/ppermute | solution.py:534
  52.3 0.0 collective-permute-done.14.refs_6_
  52.3 1.8 %collective-permute-done.15.refs_7_ = f32[104,128]{1,0:T(8,128)S(1)} collective-permute-done((f32[104,128]{1,0:T(8,128)S(1)}, f32[104,128]{1,0:T(8,128)S(1)}, u32[]{:S(2)}, u32[]{:S(2)}) %collective-permute-start.15) | collective-permute-done | bytes 53280 | tf_op jit(solution)/shard_map/ppermute | solution.py:534
  54.1 1.8 %shard_map.33 = f32[2,192,256]{2,1,0:T(8,128)} custom-call(f32[104,128]{1,0:T(8,128)S(1)} %get-tuple-element.35.refs_0_, f32[104,128]{1,0:T(8,128)S(1)} %collective-permute-done.9.refs_1_, f32[104,128]{1,0:T(8,128)S(1)} %collective-permute-done.10.refs_2_, f32[104,128]{1,0:T(8,128)S(1)} %collective-permute-done.11.refs_3_, ...), custom_call_target="tpu_custom_call" | custom-call | tf_op jit(solution)/shard_map/pallas_call | solution.py:487
Async XLA Ops:
  0.0 1.0 %copy-start = (f32[2,192,256]{2,1,0:T(8,128)S(1)}, f32[2,192,256]{2,1,0:T(8,128)}, u32[]{:S(2)}) copy-start(f32[2,192,256]{2,1,0:T(8,128)} %field.2) | copy-start | bytes 1179652
  1.0 1.0 %copy-start.1 = (f32[2,192,256]{2,1,0:T(8,128)S(1)}, f32[2,192,256]{2,1,0:T(8,128)}, u32[]{:S(2)}) copy-start(f32[2,192,256]{2,1,0:T(8,128)} %field.3) | copy-start | bytes 1179652
  3.1 11.8 %collective-permute-start = (f32[400,128]{1,0:T(8,128)S(1)}, f32[400,128]{1,0:T(8,128)S(1)}, u32[]{:S(2)}, u32[]{:S(2)}) collective-permute-start(f32[400,128]{1,0:T(8,128)S(1)} %get-tuple-element.29), channel_id=1, source_target_pairs={{0,7},{1,6},{2,5},{3,4},{4,3},{5,2},{6,1},{7,0},{8,9},{9,8},{10,11... | collective-permute-start | bytes 614408 | tf_op jit(solution)/shard_map/ppermute | solution.py:516
  9.1 10.0 %collective-permute-start.1 = (f32[400,128]{1,0:T(8,128)S(1)}, f32[400,128]{1,0:T(8,128)S(1)}, u32[]{:S(2)}, u32[]{:S(2)}) collective-permute-start(f32[400,128]{1,0:T(8,128)S(1)} %get-tuple-element.30), channel_id=1, source_target_pairs={{0,6},{1,7},{2,4},{3,5},{4,2},{5,3},{6,0},{7,1},{8,13},{9,12},{10,... | collective-permute-start | bytes 614408 | tf_op jit(solution)/shard_map/ppermute | solution.py:516
  9.4 13.6 %collective-permute-start.2 = (f32[400,128]{1,0:T(8,128)S(1)}, f32[400,128]{1,0:T(8,128)S(1)}, u32[]{:S(2)}, u32[]{:S(2)}) collective-permute-start(f32[400,128]{1,0:T(8,128)S(1)} %get-tuple-element.31), channel_id=1, source_target_pairs={{0,2},{1,3},{2,0},{3,1},{4,6},{5,7},{6,4},{7,5},{8,12},{9,13},{10,... | collective-permute-start | bytes 614408 | tf_op jit(solution)/shard_map/ppermute | solution.py:516
  9.4 16.1 %collective-permute-start.3 = (f32[400,128]{1,0:T(8,128)S(1)}, f32[400,128]{1,0:T(8,128)S(1)}, u32[]{:S(2)}, u32[]{:S(2)}) collective-permute-start(f32[400,128]{1,0:T(8,128)S(1)} %get-tuple-element.32), channel_id=1, source_target_pairs={{0,3},{1,2},{2,1},{3,0},{4,7},{5,6},{6,5},{7,4},{16,19},{17,18},{1... | collective-permute-start | bytes 614408 | tf_op jit(solution)/shard_map/ppermute | solution.py:516
  14.9 10.6 %collective-permute-start.4 = (f32[400,128]{1,0:T(8,128)S(1)}, f32[400,128]{1,0:T(8,128)S(1)}, u32[]{:S(2)}, u32[]{:S(2)}) collective-permute-start(f32[400,128]{1,0:T(8,128)S(1)} %collective-permute-done.mine_0), channel_id=1, source_target_pairs={{0,8},{8,0},{1,9},{9,1},{2,10},{10,2},{3,11},{11,3},{4,12},{12,4},... | collective-permute-start | bytes 614408 | tf_op jit(solution)/shard_map/ppermute | solution.py:517
  19.1 6.4 %collective-permute-start.5 = (f32[400,128]{1,0:T(8,128)S(1)}, f32[400,128]{1,0:T(8,128)S(1)}, u32[]{:S(2)}, u32[]{:S(2)}) collective-permute-start(f32[400,128]{1,0:T(8,128)S(1)} %collective-permute-done.1.mine_1), channel_id=1, source_target_pairs={{0,8},{8,0},{1,9},{9,1},{2,10},{10,2},{3,11},{11,3},{4,12},{12,4},... | collective-permute-start | bytes 614408 | tf_op jit(solution)/shard_map/ppermute | solution.py:517
  23.0 3.5 %collective-permute-start.6 = (f32[400,128]{1,0:T(8,128)S(1)}, f32[400,128]{1,0:T(8,128)S(1)}, u32[]{:S(2)}, u32[]{:S(2)}) collective-permute-start(f32[400,128]{1,0:T(8,128)S(1)} %collective-permute-done.2.mine_2), channel_id=1, source_target_pairs={{0,8},{8,0},{1,9},{9,1},{2,10},{10,2},{3,11},{11,3},{4,12},{12,4},... | collective-permute-start | bytes 614408 | tf_op jit(solution)/shard_map/ppermute | solution.py:517
  25.5 1.5 %collective-permute-start.7 = (f32[400,128]{1,0:T(8,128)S(1)}, f32[400,128]{1,0:T(8,128)S(1)}, u32[]{:S(2)}, u32[]{:S(2)}) collective-permute-start(f32[400,128]{1,0:T(8,128)S(1)} %collective-permute-done.3.mine_3), channel_id=1, source_target_pairs={{0,8},{8,0},{1,9},{9,1},{2,10},{10,2},{3,11},{11,3},{4,12},{12,4},... | collective-permute-start | bytes 614408 | tf_op jit(solution)/shard_map/ppermute | solution.py:517
  34.7 1.3 %collective-permute-start.8 = (f32[8,24,128]{2,1,0:T(8,128)S(1)}, f32[8,24,128]{2,1,0:T(8,128)S(1)}, u32[]{:S(2)}, u32[]{:S(2)}) collective-permute-start(f32[8,24,128]{2,1,0:T(8,128)S(1)} %get-tuple-element.34), channel_id=1, source_target_pairs={{0,8},{8,0},{1,9},{9,1},{2,10},{10,2},{3,11},{11,3},{4,12},{12,4},... | collective-permute-start | bytes 294920 | tf_op jit(solution)/shard_map/ppermute | solution.py:532
  36.1 8.4 %collective-permute-start.9 = (f32[104,128]{1,0:T(8,128)S(1)}, f32[104,128]{1,0:T(8,128)S(1)}, u32[]{:S(2)}, u32[]{:S(2)}) collective-permute-start(f32[104,128]{1,0:T(8,128)S(1)} %get-tuple-element.36), channel_id=1, source_target_pairs={{0,1},{1,0},{2,3},{3,2},{4,5},{5,4},{6,7},{7,6},{8,9},{9,8},{10,11... | collective-permute-start | bytes 159752 | tf_op jit(solution)/shard_map/ppermute | solution.py:534
  38.7 8.5 %collective-permute-start.10 = (f32[104,128]{1,0:T(8,128)S(1)}, f32[104,128]{1,0:T(8,128)S(1)}, u32[]{:S(2)}, u32[]{:S(2)}) collective-permute-start(f32[104,128]{1,0:T(8,128)S(1)} %get-tuple-element.37), channel_id=1, source_target_pairs={{0,2},{1,3},{2,0},{3,1},{4,6},{5,7},{6,4},{7,5},{8,10},{9,11},{10,... | collective-permute-start | bytes 159752 | tf_op jit(solution)/shard_map/ppermute | solution.py:534
  40.0 8.7 %collective-permute-start.11 = (f32[104,128]{1,0:T(8,128)S(1)}, f32[104,128]{1,0:T(8,128)S(1)}, u32[]{:S(2)}, u32[]{:S(2)}) collective-permute-start(f32[104,128]{1,0:T(8,128)S(1)} %get-tuple-element.38), channel_id=1, source_target_pairs={{0,3},{1,2},{2,1},{3,0},{4,7},{5,6},{6,5},{7,4},{8,11},{9,10},{10,... | collective-permute-start | bytes 159752 | tf_op jit(solution)/shard_map/ppermute | solution.py:534
  40.2 8.5 %collective-permute-start.12 = (f32[104,128]{1,0:T(8,128)S(1)}, f32[104,128]{1,0:T(8,128)S(1)}, u32[]{:S(2)}, u32[]{:S(2)}) collective-permute-start(f32[104,128]{1,0:T(8,128)S(1)} %get-tuple-element.39), channel_id=1, source_target_pairs={{0,4},{1,5},{2,6},{3,7},{4,0},{5,1},{6,2},{7,3},{8,12},{9,13},{10,... | collective-permute-start | bytes 159752 | tf_op jit(solution)/shard_map/ppermute | solution.py:534
  44.0 8.3 %collective-permute-start.13 = (f32[104,128]{1,0:T(8,128)S(1)}, f32[104,128]{1,0:T(8,128)S(1)}, u32[]{:S(2)}, u32[]{:S(2)}) collective-permute-start(f32[104,128]{1,0:T(8,128)S(1)} %get-tuple-element.40), channel_id=1, source_target_pairs={{0,5},{1,4},{2,7},{3,6},{4,1},{5,0},{6,3},{7,2},{8,13},{9,12},{10,... | collective-permute-start | bytes 159752 | tf_op jit(solution)/shard_map/ppermute | solution.py:534
  44.5 7.7 %collective-permute-start.14 = (f32[104,128]{1,0:T(8,128)S(1)}, f32[104,128]{1,0:T(8,128)S(1)}, u32[]{:S(2)}, u32[]{:S(2)}) collective-permute-start(f32[104,128]{1,0:T(8,128)S(1)} %get-tuple-element.41), channel_id=1, source_target_pairs={{0,6},{1,7},{2,4},{3,5},{4,2},{5,3},{6,0},{7,1},{8,14},{9,15},{10,... | collective-permute-start | bytes 159752 | tf_op jit(solution)/shard_map/ppermute | solution.py:534
  47.1 6.9 %collective-permute-start.15 = (f32[104,128]{1,0:T(8,128)S(1)}, f32[104,128]{1,0:T(8,128)S(1)}, u32[]{:S(2)}, u32[]{:S(2)}) collective-permute-start(f32[104,128]{1,0:T(8,128)S(1)} %get-tuple-element.42), channel_id=1, source_target_pairs={{0,7},{1,6},{2,5},{3,4},{4,3},{5,2},{6,1},{7,0},{8,15},{9,14},{10,... | collective-permute-start | bytes 159752 | tf_op jit(solution)/shard_map/ppermute | solution.py:534

commit v4 on v3

--- a/solution.py
+++ b/solution.py
@@ -143,7 +143,8 @@
 LANES = 128
 PAD = 8
 SPILL_TURNS = (0, 4, 8)
-EXCHANGES = ((7, 1), (6, 5), (2, 4), (3, 0))
+WAY_IN = ((1, 2), (3, 4), (5, 6), (7, 0))
+WAY_OUT = ((4, 5), (6, 7), (1, 2), (3, 0))
 EDGE_ROWS = 16
 FINE_CHUNKS = ((0, 16), (32, 16), (16, 16))
 HALF_CHUNKS = ((0, 24), (24, 24))
@@ -248,7 +249,7 @@
 
 def fill_kernel(initial_turned, initial_edges, reaction_turned, reaction_edges, *blocks):
     rows = initial_turned.shape[0] // 16
-    dests = [sent_to(masks) for masks in EXCHANGES] + [lax.axis_index("space")]
+    dests = [sent_to(masks) for masks in WAY_IN] + [lax.axis_index("space")]
     for dest, block in zip(dests, blocks):
         back = (8 - 16 * dest) & (LANES - 1)
         quarter = ((iota((rows, LANES), 1) + back) & (LANES - 1)) >> 5
@@ -269,7 +270,7 @@
 
 
 def march_kernel(
-    own_block, mine_0, mine_1, mine_2, mine_3, other_0, other_1, other_2, other_3, field_out, guess_out,
+    own_block, mine_0, mine_1, mine_2, mine_3, other_0, other_1, other_2, other_3, strip,
     even_a, odd_a, even_b, odd_b, even_keep, odd_keep, wide_a, wide_b, wide_keep, small_a, small_b, small_keep, first_guess, second_guess, sums,
 ):
     tm, space = lax.axis_index("tm"), lax.axis_index("space")
@@ -292,10 +293,10 @@
     in_half = iota((rows, LANES), 1) & 63
     left, right = in_half < 4, inside(in_half, 36, 40)
     blocks = [(own_block, None, space)]
-    for masks, mine, other in zip(EXCHANGES, (mine_0, mine_1, mine_2), (other_0, other_1, other_2)):
+    for masks, mine, other in zip(WAY_IN, (mine_0, mine_1, mine_2), (other_0, other_1, other_2)):
         blocks.append((mine, None, sent_to(masks)))
         blocks.append((other, None, sent_to(masks[::-1])))
-    blocks.append((mine_3, other_3, space ^ EXCHANGES[3][0]))
+    blocks.append((mine_3, other_3, space ^ WAY_IN[3][0]))
     for number, (block, if_second, k) in enumerate(blocks):
 
         def read(first, size, block=block, if_second=if_second):
@@ -385,7 +386,7 @@
                     fine = fine_a[e][pl.ds((2 * k + z + 1) * height + PAD + odd, part, 2), :] * scale
                     value.append((add + fine) - less)
                 total = value[0] + value[1] if total is None else total + (value[0] + value[1])
-                field_out[k, pl.ds(e * rows + odd, part, 2), :] = jnp.where(own, value[0], roll(value[1], 16))
+                strip[k, pl.ds(e * rows + odd, part, 2), :] = jnp.where(own, value[0], roll(value[1], 16))
         to = (k + 1) * small_height + PAD
         small_a[to : to + part, :] = jnp.where(own, total * 0.125, 0.0)
 
@@ -394,39 +395,49 @@
         coarse_run()
         for k in range(count):
             at = (k + 1) * small_height + PAD
-            guess_out[k] = small_a[at : at + part, :] * small_scale
-
-
-def send_kernel(field, guess, *blocks):
-    tm, space = lax.axis_index("tm"), lax.axis_index("space")
-    part = guess.shape[1]
+            strip[k, 2 * rows :, :] = small_a[at : at + part, :] * small_scale
+
+
+def send_kernel(mine, other, *blocks):
+    tm = lax.axis_index("tm")
+    part = mine.shape[1] // 5
     rows = 2 * part
     in_quarter = iota((part, LANES), 1) & 31
     own = inside(in_quarter, 8, 24)
     spill = (inside(in_quarter, 4, 8) | inside(in_quarter, 24, 28))[:8]
-    for k, block in enumerate(blocks):
-        dest = space ^ k
-        mine = jnp.where(tm == 0, 0.0, guess[dest])
-        both = jnp.where(own, mine, roll(mine, 16))
+    dests = [sent_to(masks) for masks in WAY_OUT] + [lax.axis_index("space")]
+    for dest, block in zip(dests, blocks):
+        guess = jnp.where(tm == 0, mine[dest, 2 * rows :, :], other[dest, 2 * rows :, :])
+        both = jnp.where(own, guess, roll(guess, 16))
+        block[: 2 * rows, :] = jnp.where(tm == 0, mine[dest, : 2 * rows, :], other[dest, : 2 * rows, :])
         for e in range(2):
             for odd in range(2):
                 at = pl.ds(e * rows + odd, part, 2)
-                block[at, :] = field[dest, at, :] + both
+                to = pl.ds((2 + e) * rows + odd, part, 2)
+                block[to, :] = jnp.where(tm == 0, other[dest, at, :], mine[dest, at, :]) + both
         packed = None
         for g, by in enumerate(SPILL_TURNS):
-            piece = roll(jnp.where(spill, mine[8 * g : 8 * g + 8], 0.0), by)
+            piece = roll(jnp.where(spill, guess[8 * g : 8 * g + 8], 0.0), by)
             packed = piece if packed is None else packed + piece
-        block[2 * rows : 2 * rows + 8, :] = packed
-
-
-def unpack_kernel(*refs):
-    blocks, (out_hbm, strips, spilled, out, left) = refs[:-5], refs[-5:]
-    count = len(blocks)
+        block[4 * rows : 4 * rows + 8, :] = packed
+
+
+def unpack_kernel(own_block, mine_0, mine_1, mine_2, mine_3, other_0, other_1, other_2, other_3, out_hbm, strips, spilled, out, left):
+    tm, space = lax.axis_index("tm"), lax.axis_index("space")
+    count = strips.shape[0]
     rows = out.shape[1] // 4
     part = rows // 2
-    space = lax.axis_index("space")
-    for k, block in enumerate(blocks):
-        strips[space ^ k] = block[...]
+    blocks = [(own_block, None, space)]
+    for masks, mine, other in zip(WAY_OUT, (mine_0, mine_1, mine_2), (other_0, other_1, other_2)):
+        blocks.append((mine, None, sent_to(masks)))
+        blocks.append((other, None, sent_to(masks[::-1])))
+    blocks.append((mine_3, other_3, space ^ WAY_OUT[3][0]))
+    for block, if_second, k in blocks:
+        slabs = [block[: 2 * rows, :], block[2 * rows :, :]]
+        if if_second is not None:
+            slabs = [jnp.where(tm == 0, x, y) for x, y in zip(slabs, (if_second[: 2 * rows, :], if_second[2 * rows :, :]))]
+        strips[k, : 2 * rows, :] = jnp.where(tm == 0, slabs[0], slabs[1][: 2 * rows])
+        strips[k, 2 * rows :, :] = jnp.where(tm == 0, 0.0, slabs[1][2 * rows :])
 
     def lined_up(read, first, size):
         quarter = ((iota((size, LANES), 1) - first) & (LANES - 1)) >> 5
@@ -494,6 +505,19 @@
     )(*inputs)
 
 
+def swapped(x):
+    return lax.ppermute(x, "tm", [(0, 1), (1, 0)])
+
+
+def exchanged(blocks, way):
+    count = lax.axis_size("space")
+    mine = []
+    for block, masks in zip(blocks, way):
+        pairs = [(t * count + i, t * count + (i ^ masks[t])) for t in range(2) if masks[t] for i in range(count)]
+        mine.append(lax.ppermute(block, ("tm", "space"), pairs))
+    return mine, [swapped(x) for x in mine]
+
+
 def strips_local(initial, reaction):
     count = lax.axis_size("space")
     _, nx, _ = initial.shape
@@ -510,31 +534,26 @@
             [(4 * rows, LANES), (2 * rows, LANES)],
         )
     *blocks, own_block = on_core(fill_kernel, prepared, [block] * 5)
-    mine, other = [], []
-    for x, masks in zip(blocks, EXCHANGES):
-        pairs = [(t * count + i, t * count + (i ^ masks[t])) for t in range(2) if masks[t] for i in range(count)]
-        mine.append(lax.ppermute(x, ("tm", "space"), pairs))
-        other.append(lax.ppermute(mine[-1], "tm", [(0, 1), (1, 0)]))
+    mine, other = exchanged(blocks, WAY_IN)
     fine = ((planes + 2) * (rows + 2 * PAD), LANES)
     wide = ((count + 2) * (rows + 2 * PAD), LANES)
     small = ((count + 2) * (part + 2 * PAD), LANES)
     small_cells = (count * part, LANES)
-    field, guess = on_core(
+    (strip,) = on_core(
         march_kernel,
         [own_block, *mine, *other],
-        [(count, 2 * rows, LANES), (count, part, LANES)],
+        [(count, 5 * part, LANES)],
         [fine] * 4
         + [(planes * rows, LANES)] * 2
         + [wide, wide, (count * rows, LANES), small, small]
         + [small_cells] * 3
         + [(planes * rows, LANES)],
     )
-    guess = lax.ppermute(guess, "tm", [(0, 1), (1, 0)])
-    own_strip, *strips = on_core(send_kernel, [field, guess], [(2 * rows + 8, LANES)] * count)
-    strips = [lax.ppermute(x, "space", [(i, i ^ k) for i in range(count)]) for k, x in enumerate(strips, 1)]
+    *blocks, own_block = on_core(send_kernel, [strip, swapped(strip)], [(4 * rows + 8, LANES)] * 5)
+    mine, other = exchanged(blocks, WAY_OUT)
     (out,) = on_core(
         unpack_kernel,
-        [own_strip, *strips],
+        [own_block, *mine, *other],
         [initial.shape],
         [(count, 2 * rows + 8, LANES), (nx, LANES), initial.shape, pltpu.SemaphoreType.DMA((2,))],
         pl.BlockSpec(memory_space=pltpu.HBM),

time: 56.1 us -> 53.3 us (0.950)
  starting transfers between devices: 29.4 us -> 19.7 us
  waiting for transfers between devices: 13.7 us -> 20.6 us
    ppermute x16 -> x17, starting transfers between devices: 29.4 us -> 19.7 us  [the longest x8 17.5 us: exchanged(): mine.append(lax.ppermute(block, ('tm', 'space'), pairs))]
    ppermute x16 -> x17, waiting for transfers between devices: 13.7 us -> 20.6 us  [the longest x8 16.5 us: exchanged(): mine.append(lax.ppermute(block, ('tm', 'space'), pairs))]
  transfers between devices with their start and end apart: 16 -> 17, of which waited for: 7 -> 9; matrix products, arithmetic and copies ran while one was open for 0% -> 0% of each run, Pallas kernels for 0% -> 0%
where the time goes in v4:
time: 53.3 us; the launch traced here: 53 us
  waiting for transfers between devices  20.6 us (39%)
  starting transfers between devices  19.7 us (37%)
  Pallas kernels  11.5 us (22%)
  local copies, waits for them, and re-layouts  1.25 us (2%)
    ppermute x8, starting transfers between devices, exchanged(): mine.append(lax.ppermute(block, ('tm', 'space'), pairs))  17.5 us
    ppermute x8, waiting for transfers between devices, exchanged(): mine.append(lax.ppermute(block, ('tm', 'space'), pairs))  16.5 us
    pallas_call x6, Pallas kernels, on_core(): pl.pallas_call(kernel, out_shape=shapes, in_specs=[VMEM] * len(inputs), o...  11.5 us
    ppermute x9, waiting for transfers between devices, swapped(): return lax.ppermute(x, 'tm', [(0, 1), (1, 0)])  4.11 us
    ppermute x9, starting transfers between devices, swapped(): return lax.ppermute(x, 'tm', [(0, 1), (1, 0)])  2.11 us
    unnamed x4, local copies, waits for them, and re-layouts  1.25 us
  transfers between devices with their start and end apart: 17, of which 9 were waited for; matrix products, arithmetic and copies ran while one was open for 0% of the time, Pallas kernels for 0%

profile of v4, /device:TPU:0, one launch (start us, length us, event | category | flops | bytes accessed | tf_op | source)
XLA Modules:
  0.0 53.0 jit_solution(1086047034182682042)
XLA Ops:
  0.0 0.0 copy-start
  0.0 1.0 %copy-done = f32[2,192,256]{2,1,0:T(8,128)S(1)} copy-done((f32[2,192,256]{2,1,0:T(8,128)S(1)}, f32[2,192,256]{2,1,0:T(8,128)}, u32[]{:S(2)}) %copy-start) | copy-done | bytes 393240
  1.0 0.0 copy-start.1
  1.0 0.7 %shard_map.28 = (f32[768,128]{1,0:T(8,128)S(1)}, f32[192,128]{1,0:T(8,128)S(1)}) custom-call(f32[2,192,256]{2,1,0:T(8,128)S(1)} %copy-done), custom_call_target="tpu_custom_call" | custom-call | tf_op jit(solution)/shard_map/pallas_call | solution.py:498
  1.7 0.3 copy-done.1
  2.0 0.7 %shard_map.29 = (f32[768,128]{1,0:T(8,128)S(1)}, f32[192,128]{1,0:T(8,128)S(1)}) custom-call(f32[2,192,256]{2,1,0:T(8,128)S(1)} %copy-done.1), custom_call_target="tpu_custom_call" | custom-call | tf_op jit(solution)/shard_map/pallas_call | solution.py:498
  2.7 0.4 shard_map.30
  3.1 3.0 %collective-permute-start = (f32[400,128]{1,0:T(8,128)S(1)}, f32[400,128]{1,0:T(8,128)S(1)}, u32[]{:S(2)}, u32[]{:S(2)}) collective-permute-start(f32[400,128]{1,0:T(8,128)S(1)} %get-tuple-element.24), channel_id=1, source_target_pairs={{0,1},{1,0},{2,3},{3,2},{4,5},{5,4},{6,7},{7,6},{8,10},{9,11},{10,... | collective-permute-start | bytes 614408 | tf_op jit(solution)/shard_map/ppermute | solution.py:517
  6.1 1.5 %collective-permute-start.1 = (f32[400,128]{1,0:T(8,128)S(1)}, f32[400,128]{1,0:T(8,128)S(1)}, u32[]{:S(2)}, u32[]{:S(2)}) collective-permute-start(f32[400,128]{1,0:T(8,128)S(1)} %get-tuple-element.25), channel_id=1, source_target_pairs={{0,3},{1,2},{2,1},{3,0},{4,7},{5,6},{6,5},{7,4},{8,12},{9,13},{10,... | collective-permute-start | bytes 614408 | tf_op jit(solution)/shard_map/ppermute | solution.py:517
  7.7 3.5 %collective-permute-start.2 = (f32[400,128]{1,0:T(8,128)S(1)}, f32[400,128]{1,0:T(8,128)S(1)}, u32[]{:S(2)}, u32[]{:S(2)}) collective-permute-start(f32[400,128]{1,0:T(8,128)S(1)} %get-tuple-element.26), channel_id=1, source_target_pairs={{0,5},{1,4},{2,7},{3,6},{4,1},{5,0},{6,3},{7,2},{8,14},{9,15},{10,... | collective-permute-start | bytes 614408 | tf_op jit(solution)/shard_map/ppermute | solution.py:517
  11.2 1.9 %collective-permute-start.3 = (f32[400,128]{1,0:T(8,128)S(1)}, f32[400,128]{1,0:T(8,128)S(1)}, u32[]{:S(2)}, u32[]{:S(2)}) collective-permute-start(f32[400,128]{1,0:T(8,128)S(1)} %get-tuple-element.27), channel_id=1, source_target_pairs={{0,7},{1,6},{2,5},{3,4},{4,3},{5,2},{6,1},{7,0},{16,23},{17,22},{1... | collective-permute-start | bytes 614408 | tf_op jit(solution)/shard_map/ppermute | solution.py:517
  13.1 0.0 collective-permute-done.mine_0
  13.1 0.1 collective-permute-start.4
  13.2 1.8 %collective-permute-done.1.mine_1 = f32[400,128]{1,0:T(8,128)S(1)} collective-permute-done((f32[400,128]{1,0:T(8,128)S(1)}, f32[400,128]{1,0:T(8,128)S(1)}, u32[]{:S(2)}, u32[]{:S(2)}) %collective-permute-start.1) | collective-permute-done | bytes 204832 | tf_op jit(solution)/shard_map/ppermute | solution.py:517
  15.0 0.0 collective-permute-start.5
  15.0 10.5 %collective-permute-done.2.mine_2 = f32[400,128]{1,0:T(8,128)S(1)} collective-permute-done((f32[400,128]{1,0:T(8,128)S(1)}, f32[400,128]{1,0:T(8,128)S(1)}, u32[]{:S(2)}, u32[]{:S(2)}) %collective-permute-start.2) | collective-permute-done | bytes 204832 | tf_op jit(solution)/shard_map/ppermute | solution.py:517
  25.5 0.0 collective-permute-start.6
  25.5 0.0 collective-permute-done.3.mine_3
  25.6 0.5 collective-permute-start.7
  26.1 0.0 collective-permute-done.4.other_0
  26.1 0.0 collective-permute-done.5.other_1
  26.1 0.9 %collective-permute-done.6.other_2 = f32[400,128]{1,0:T(8,128)S(1)} collective-permute-done((f32[400,128]{1,0:T(8,128)S(1)}, f32[400,128]{1,0:T(8,128)S(1)}, u32[]{:S(2)}, u32[]{:S(2)}) %collective-permute-start.6) | collective-permute-done | bytes 204832 | tf_op jit(solution)/shard_map/ppermute | solution.py:509
  27.0 0.3 collective-permute-done.7.other_3
  27.3 7.7 %shard_map.31.mine = f32[8,120,128]{2,1,0:T(8,128)S(1)} custom-call(f32[400,128]{1,0:T(8,128)S(1)} %get-tuple-element.23.own_block, f32[400,128]{1,0:T(8,128)S(1)} %collective-permute-done.mine_0, f32[400,128]{1,0:T(8,128)S(1)} %collective-permute-done.1.mine_1, f32[400,128]{1,0:T(8,128)S(1)} %collective-permute-done.2.mine_2, ...), custom_call_target="tpu_custom_call" | custom-call | tf_op jit(solution)/shard_map/pallas_call | solution.py:498
  35.0 0.3 collective-permute-start.8
  35.3 1.6 %collective-permute-done.8.other = f32[8,120,128]{2,1,0:T(8,128)S(1)} collective-permute-done((f32[8,120,128]{2,1,0:T(8,128)S(1)}, f32[8,120,128]{2,1,0:T(8,128)S(1)}, u32[]{:S(2)}, u32[]{:S(2)}) %collective-permute-start.8) | collective-permute-done | bytes 491552 | tf_op jit(solution)/shard_map/ppermute | solution.py:509
  36.9 0.1 shard_map.32
  37.0 3.6 %collective-permute-start.9 = (f32[200,128]{1,0:T(8,128)S(1)}, f32[200,128]{1,0:T(8,128)S(1)}, u32[]{:S(2)}, u32[]{:S(2)}) collective-permute-start(f32[200,128]{1,0:T(8,128)S(1)} %get-tuple-element.29), channel_id=1, source_target_pairs={{0,4},{1,5},{2,6},{3,7},{4,0},{5,1},{6,2},{7,3},{8,13},{9,12},{10,... | collective-permute-start | bytes 307208 | tf_op jit(solution)/shard_map/ppermute | solution.py:517
  40.6 1.3 %collective-permute-start.10 = (f32[200,128]{1,0:T(8,128)S(1)}, f32[200,128]{1,0:T(8,128)S(1)}, u32[]{:S(2)}, u32[]{:S(2)}) collective-permute-start(f32[200,128]{1,0:T(8,128)S(1)} %get-tuple-element.30), channel_id=1, source_target_pairs={{0,6},{1,7},{2,4},{3,5},{4,2},{5,3},{6,0},{7,1},{8,15},{9,14},{10,... | collective-permute-start | bytes 307208 | tf_op jit(solution)/shard_map/ppermute | solution.py:517
  41.9 0.6 %collective-permute-start.11 = (f32[200,128]{1,0:T(8,128)S(1)}, f32[200,128]{1,0:T(8,128)S(1)}, u32[]{:S(2)}, u32[]{:S(2)}) collective-permute-start(f32[200,128]{1,0:T(8,128)S(1)} %get-tuple-element.31), channel_id=1, source_target_pairs={{0,1},{1,0},{2,3},{3,2},{4,5},{5,4},{6,7},{7,6},{8,10},{9,11},{10,... | collective-permute-start | bytes 307208 | tf_op jit(solution)/shard_map/ppermute | solution.py:517
  42.5 2.1 %collective-permute-start.12 = (f32[200,128]{1,0:T(8,128)S(1)}, f32[200,128]{1,0:T(8,128)S(1)}, u32[]{:S(2)}, u32[]{:S(2)}) collective-permute-start(f32[200,128]{1,0:T(8,128)S(1)} %get-tuple-element.32), channel_id=1, source_target_pairs={{0,3},{1,2},{2,1},{3,0},{4,7},{5,6},{6,5},{7,4},{16,19},{17,18},{1... | collective-permute-start | bytes 307208 | tf_op jit(solution)/shard_map/ppermute | solution.py:517
  44.6 4.0 %collective-permute-done.9.mine_0 = f32[200,128]{1,0:T(8,128)S(1)} collective-permute-done((f32[200,128]{1,0:T(8,128)S(1)}, f32[200,128]{1,0:T(8,128)S(1)}, u32[]{:S(2)}, u32[]{:S(2)}) %collective-permute-start.9) | collective-permute-done | bytes 102432 | tf_op jit(solution)/shard_map/ppermute | solution.py:517
  48.7 0.0 collective-permute-start.13
  48.7 0.0 collective-permute-done.10.mine_1
  48.7 0.5 collective-permute-start.14
  49.2 0.0 collective-permute-done.11.mine_2
  49.2 0.7 %collective-permute-start.15 = (f32[200,128]{1,0:T(8,128)S(1)}, f32[200,128]{1,0:T(8,128)S(1)}, u32[]{:S(2)}, u32[]{:S(2)}) collective-permute-start(f32[200,128]{1,0:T(8,128)S(1)} %collective-permute-done.11.mine_2), channel_id=1, source_target_pairs={{0,8},{8,0},{1,9},{9,1},{2,10},{10,2},{3,11},{11,3},{4,12},{12,4},... | collective-permute-start | bytes 307208 | tf_op jit(solution)/shard_map/ppermute | solution.py:509
  49.9 0.0 collective-permute-done.12.mine_3
  49.9 0.0 collective-permute-start.16
  49.9 0.0 collective-permute-done.13.other_0
  50.0 0.2 collective-permute-done.14.other_1
  50.1 0.7 %collective-permute-done.15.other_2 = f32[200,128]{1,0:T(8,128)S(1)} collective-permute-done((f32[200,128]{1,0:T(8,128)S(1)}, f32[200,128]{1,0:T(8,128)S(1)}, u32[]{:S(2)}, u32[]{:S(2)}) %collective-permute-start.15) | collective-permute-done | bytes 102432 | tf_op jit(solution)/shard_map/ppermute | solution.py:509
  50.8 0.4 collective-permute-done.16.other_3
  51.2 1.8 %shard_map.33 = f32[2,192,256]{2,1,0:T(8,128)} custom-call(f32[200,128]{1,0:T(8,128)S(1)} %get-tuple-element.28.own_block, f32[200,128]{1,0:T(8,128)S(1)} %collective-permute-done.9.mine_0, f32[200,128]{1,0:T(8,128)S(1)} %collective-permute-done.10.mine_1, f32[200,128]{1,0:T(8,128)S(1)} %collective-permute-done.11.mine_2, ...), custom_call_target="tpu_custom_call" | custom-call | tf_op jit(solution)/shard_map/pallas_call | solution.py:498
Async XLA Ops:
  0.0 1.0 %copy-start = (f32[2,192,256]{2,1,0:T(8,128)S(1)}, f32[2,192,256]{2,1,0:T(8,128)}, u32[]{:S(2)}) copy-start(f32[2,192,256]{2,1,0:T(8,128)} %field.2) | copy-start | bytes 1179652
  1.0 1.0 %copy-start.1 = (f32[2,192,256]{2,1,0:T(8,128)S(1)}, f32[2,192,256]{2,1,0:T(8,128)}, u32[]{:S(2)}) copy-start(f32[2,192,256]{2,1,0:T(8,128)} %field.3) | copy-start | bytes 1179652
  3.1 10.0 %collective-permute-start = (f32[400,128]{1,0:T(8,128)S(1)}, f32[400,128]{1,0:T(8,128)S(1)}, u32[]{:S(2)}, u32[]{:S(2)}) collective-permute-start(f32[400,128]{1,0:T(8,128)S(1)} %get-tuple-element.24), channel_id=1, source_target_pairs={{0,1},{1,0},{2,3},{3,2},{4,5},{5,4},{6,7},{7,6},{8,10},{9,11},{10,... | collective-permute-start | bytes 614408 | tf_op jit(solution)/shard_map/ppermute | solution.py:517
  6.1 8.9 %collective-permute-start.1 = (f32[400,128]{1,0:T(8,128)S(1)}, f32[400,128]{1,0:T(8,128)S(1)}, u32[]{:S(2)}, u32[]{:S(2)}) collective-permute-start(f32[400,128]{1,0:T(8,128)S(1)} %get-tuple-element.25), channel_id=1, source_target_pairs={{0,3},{1,2},{2,1},{3,0},{4,7},{5,6},{6,5},{7,4},{8,12},{9,13},{10,... | collective-permute-start | bytes 614408 | tf_op jit(solution)/shard_map/ppermute | solution.py:517
  7.7 17.9 %collective-permute-start.2 = (f32[400,128]{1,0:T(8,128)S(1)}, f32[400,128]{1,0:T(8,128)S(1)}, u32[]{:S(2)}, u32[]{:S(2)}) collective-permute-start(f32[400,128]{1,0:T(8,128)S(1)} %get-tuple-element.26), channel_id=1, source_target_pairs={{0,5},{1,4},{2,7},{3,6},{4,1},{5,0},{6,3},{7,2},{8,14},{9,15},{10,... | collective-permute-start | bytes 614408 | tf_op jit(solution)/shard_map/ppermute | solution.py:517
  11.2 14.4 %collective-permute-start.3 = (f32[400,128]{1,0:T(8,128)S(1)}, f32[400,128]{1,0:T(8,128)S(1)}, u32[]{:S(2)}, u32[]{:S(2)}) collective-permute-start(f32[400,128]{1,0:T(8,128)S(1)} %get-tuple-element.27), channel_id=1, source_target_pairs={{0,7},{1,6},{2,5},{3,4},{4,3},{5,2},{6,1},{7,0},{16,23},{17,22},{1... | collective-permute-start | bytes 614408 | tf_op jit(solution)/shard_map/ppermute | solution.py:517
  13.1 13.0 %collective-permute-start.4 = (f32[400,128]{1,0:T(8,128)S(1)}, f32[400,128]{1,0:T(8,128)S(1)}, u32[]{:S(2)}, u32[]{:S(2)}) collective-permute-start(f32[400,128]{1,0:T(8,128)S(1)} %collective-permute-done.mine_0), channel_id=1, source_target_pairs={{0,8},{8,0},{1,9},{9,1},{2,10},{10,2},{3,11},{11,3},{4,12},{12,4},... | collective-permute-start | bytes 614408 | tf_op jit(solution)/shard_map/ppermute | solution.py:509
  15.0 11.0 %collective-permute-start.5 = (f32[400,128]{1,0:T(8,128)S(1)}, f32[400,128]{1,0:T(8,128)S(1)}, u32[]{:S(2)}, u32[]{:S(2)}) collective-permute-start(f32[400,128]{1,0:T(8,128)S(1)} %collective-permute-done.1.mine_1), channel_id=1, source_target_pairs={{0,8},{8,0},{1,9},{9,1},{2,10},{10,2},{3,11},{11,3},{4,12},{12,4},... | collective-permute-start | bytes 614408 | tf_op jit(solution)/shard_map/ppermute | solution.py:509
  25.5 1.5 %collective-permute-start.6 = (f32[400,128]{1,0:T(8,128)S(1)}, f32[400,128]{1,0:T(8,128)S(1)}, u32[]{:S(2)}, u32[]{:S(2)}) collective-permute-start(f32[400,128]{1,0:T(8,128)S(1)} %collective-permute-done.2.mine_2), channel_id=1, source_target_pairs={{0,8},{8,0},{1,9},{9,1},{2,10},{10,2},{3,11},{11,3},{4,12},{12,4},... | collective-permute-start | bytes 614408 | tf_op jit(solution)/shard_map/ppermute | solution.py:509
  25.6 1.7 %collective-permute-start.7 = (f32[400,128]{1,0:T(8,128)S(1)}, f32[400,128]{1,0:T(8,128)S(1)}, u32[]{:S(2)}, u32[]{:S(2)}) collective-permute-start(f32[400,128]{1,0:T(8,128)S(1)} %collective-permute-done.3.mine_3), channel_id=1, source_target_pairs={{0,8},{8,0},{1,9},{9,1},{2,10},{10,2},{3,11},{11,3},{4,12},{12,4},... | collective-permute-start | bytes 614408 | tf_op jit(solution)/shard_map/ppermute | solution.py:509
  35.0 1.9 %collective-permute-start.8 = (f32[8,120,128]{2,1,0:T(8,128)S(1)}, f32[8,120,128]{2,1,0:T(8,128)S(1)}, u32[]{:S(2)}, u32[]{:S(2)}) collective-permute-start(f32[8,120,128]{2,1,0:T(8,128)S(1)} %shard_map.31.mine), channel_id=1, source_target_pairs={{0,8},{8,0},{1,9},{9,1},{2,10},{10,2},{3,11},{11,3},{4,12},{12,4},... | collective-permute-start | bytes 1474568 | tf_op jit(solution)/shard_map/ppermute | solution.py:509
  37.0 11.6 %collective-permute-start.9 = (f32[200,128]{1,0:T(8,128)S(1)}, f32[200,128]{1,0:T(8,128)S(1)}, u32[]{:S(2)}, u32[]{:S(2)}) collective-permute-start(f32[200,128]{1,0:T(8,128)S(1)} %get-tuple-element.29), channel_id=1, source_target_pairs={{0,4},{1,5},{2,6},{3,7},{4,0},{5,1},{6,2},{7,3},{8,13},{9,12},{10,... | collective-permute-start | bytes 307208 | tf_op jit(solution)/shard_map/ppermute | solution.py:517
  40.6 8.1 %collective-permute-start.10 = (f32[200,128]{1,0:T(8,128)S(1)}, f32[200,128]{1,0:T(8,128)S(1)}, u32[]{:S(2)}, u32[]{:S(2)}) collective-permute-start(f32[200,128]{1,0:T(8,128)S(1)} %get-tuple-element.30), channel_id=1, source_target_pairs={{0,6},{1,7},{2,4},{3,5},{4,2},{5,3},{6,0},{7,1},{8,15},{9,14},{10,... | collective-permute-start | bytes 307208 | tf_op jit(solution)/shard_map/ppermute | solution.py:517
  41.9 7.2 %collective-permute-start.11 = (f32[200,128]{1,0:T(8,128)S(1)}, f32[200,128]{1,0:T(8,128)S(1)}, u32[]{:S(2)}, u32[]{:S(2)}) collective-permute-start(f32[200,128]{1,0:T(8,128)S(1)} %get-tuple-element.31), channel_id=1, source_target_pairs={{0,1},{1,0},{2,3},{3,2},{4,5},{5,4},{6,7},{7,6},{8,10},{9,11},{10,... | collective-permute-start | bytes 307208 | tf_op jit(solution)/shard_map/ppermute | solution.py:517
  42.5 7.4 %collective-permute-start.12 = (f32[200,128]{1,0:T(8,128)S(1)}, f32[200,128]{1,0:T(8,128)S(1)}, u32[]{:S(2)}, u32[]{:S(2)}) collective-permute-start(f32[200,128]{1,0:T(8,128)S(1)} %get-tuple-element.32), channel_id=1, source_target_pairs={{0,3},{1,2},{2,1},{3,0},{4,7},{5,6},{6,5},{7,4},{16,19},{17,18},{1... | collective-permute-start | bytes 307208 | tf_op jit(solution)/shard_map/ppermute | solution.py:517
  48.7 1.3 %collective-permute-start.13 = (f32[200,128]{1,0:T(8,128)S(1)}, f32[200,128]{1,0:T(8,128)S(1)}, u32[]{:S(2)}, u32[]{:S(2)}) collective-permute-start(f32[200,128]{1,0:T(8,128)S(1)} %collective-permute-done.9.mine_0), channel_id=1, source_target_pairs={{0,8},{8,0},{1,9},{9,1},{2,10},{10,2},{3,11},{11,3},{4,12},{12,4},... | collective-permute-start | bytes 307208 | tf_op jit(solution)/shard_map/ppermute | solution.py:509
  48.7 1.5 %collective-permute-start.14 = (f32[200,128]{1,0:T(8,128)S(1)}, f32[200,128]{1,0:T(8,128)S(1)}, u32[]{:S(2)}, u32[]{:S(2)}) collective-permute-start(f32[200,128]{1,0:T(8,128)S(1)} %collective-permute-done.10.mine_1), channel_id=1, source_target_pairs={{0,8},{8,0},{1,9},{9,1},{2,10},{10,2},{3,11},{11,3},{4,12},{12,4},... | collective-permute-start | bytes 307208 | tf_op jit(solution)/shard_map/ppermute | solution.py:509
  49.2 1.7 %collective-permute-start.15 = (f32[200,128]{1,0:T(8,128)S(1)}, f32[200,128]{1,0:T(8,128)S(1)}, u32[]{:S(2)}, u32[]{:S(2)}) collective-permute-start(f32[200,128]{1,0:T(8,128)S(1)} %collective-permute-done.11.mine_2), channel_id=1, source_target_pairs={{0,8},{8,0},{1,9},{9,1},{2,10},{10,2},{3,11},{11,3},{4,12},{12,4},... | collective-permute-start | bytes 307208 | tf_op jit(solution)/shard_map/ppermute | solution.py:509
  49.9 1.3 %collective-permute-start.16 = (f32[200,128]{1,0:T(8,128)S(1)}, f32[200,128]{1,0:T(8,128)S(1)}, u32[]{:S(2)}, u32[]{:S(2)}) collective-permute-start(f32[200,128]{1,0:T(8,128)S(1)} %collective-permute-done.12.mine_3), channel_id=1, source_target_pairs={{0,8},{8,0},{1,9},{9,1},{2,10},{10,2},{3,11},{11,3},{4,12},{12,4},... | collective-permute-start | bytes 307208 | tf_op jit(solution)/shard_map/ppermute | solution.py:509

commit v5 on v4

--- a/solution.py
+++ b/solution.py
@@ -143,11 +143,11 @@
 LANES = 128
 PAD = 8
 SPILL_TURNS = (0, 4, 8)
-WAY_IN = ((1, 2), (3, 4), (5, 6), (7, 0))
+WAY_IN = ((1, 4), (5, 2), (3, 6), (7, 0))
 WAY_OUT = ((4, 5), (6, 7), (1, 2), (3, 0))
 EDGE_ROWS = 16
 FINE_CHUNKS = ((0, 16), (32, 16), (16, 16))
-HALF_CHUNKS = ((0, 24), (24, 24))
+HALF_CHUNKS = ((0, 16), (32, 16), (16, 16))
 QUARTER_CHUNKS = ((0, 24),)
 
 
@@ -214,6 +214,10 @@
 
 def sent_to(masks):
     return lax.axis_index("space") ^ jnp.where(lax.axis_index("tm") == 0, masks[0], masks[1])
+
+
+def served(way, other_core=False):
+    return [sent_to(masks[::-1] if other_core else masks) for masks in way] + [lax.axis_index("space")]
 
 
 def prepare_kernel(turns, field, turned, edges, sums, coarse):
@@ -249,8 +253,7 @@
 
 def fill_kernel(initial_turned, initial_edges, reaction_turned, reaction_edges, *blocks):
     rows = initial_turned.shape[0] // 16
-    dests = [sent_to(masks) for masks in WAY_IN] + [lax.axis_index("space")]
-    for dest, block in zip(dests, blocks):
+    for dest, block in zip(served(WAY_IN), blocks):
         back = (8 - 16 * dest) & (LANES - 1)
         quarter = ((iota((rows, LANES), 1) + back) & (LANES - 1)) >> 5
         for n in range(8):
@@ -270,8 +273,8 @@
 
 
 def march_kernel(
-    own_block, mine_0, mine_1, mine_2, mine_3, other_0, other_1, other_2, other_3, strip,
-    even_a, odd_a, even_b, odd_b, even_keep, odd_keep, wide_a, wide_b, wide_keep, small_a, small_b, small_keep, first_guess, second_guess, sums,
+    own_block, mine_0, mine_1, mine_2, mine_3, other_0, other_1, other_2, other_3, strip, given,
+    even_a, odd_a, even_b, odd_b, even_keep, odd_keep, wide_a, wide_b, wide_keep, small_a, small_b, small_keep, second_guess, sums,
 ):
     tm, space = lax.axis_index("tm"), lax.axis_index("space")
     rows = (own_block.shape[0] - EDGE_ROWS) // 8
@@ -329,20 +332,6 @@
             windows.append(jnp.where(left, lefts, jnp.where(right, rights, inner)))
         wide_a[some(k + 1, wide_height, PAD, rows), :] = windows[0]
         wide_keep[some(k, rows, 0, rows), :] = small_centre - small_slope * windows[1]
-    wrap_rows(wide_a, count, rows, 64)
-
-    for _ in range(CSTEPS // 2):
-        one_step((wide_a,), (wide_b,), (wide_keep,), count, rows, small_lows, HALF_CHUNKS, 64)
-        one_step((wide_b,), (wide_a,), (wide_keep,), count, rows, small_lows, HALF_CHUNKS, 64)
-
-    for k in range(count):
-        at = (k + 1) * wide_height + PAD
-        upper, lower = wide_a[at : at + part, :], wide_a[at + part : at + rows, :]
-        guess = jnp.where(even_quarter, roll(upper, -4), roll(lower, 28)) * small_scale
-        first_guess[k * part : (k + 1) * part, :] = guess
-        to = (k + 1) * small_height + PAD
-        small_a[to : to + part, :] = guess
-
     def coarse_run():
         wrap_rows(small_a, count, part, 32)
         for _ in range(CSTEPS // 2):
@@ -351,8 +340,17 @@
 
     @pl.when(tm != 0)
     def _():
+        wrap_rows(wide_a, count, rows, 64)
+        for _ in range(CSTEPS // 2):
+            one_step((wide_a,), (wide_b,), (wide_keep,), count, rows, small_lows, HALF_CHUNKS, 64)
+            one_step((wide_b,), (wide_a,), (wide_keep,), count, rows, small_lows, HALF_CHUNKS, 64)
         for k in range(count):
-            guess = first_guess[k * part : (k + 1) * part, :]
+            at = (k + 1) * wide_height + PAD
+            upper, lower = wide_a[at : at + part, :], wide_a[at + part : at + rows, :]
+            guess = jnp.where(even_quarter, roll(upper, -4), roll(lower, 28)) * small_scale
+            strip[k, 2 * rows :, :] = guess
+            to = (k + 1) * small_height + PAD
+            small_a[to : to + part, :] = guess
             for z in range(2):
                 for e in range(2):
                     to = (2 * k + z + 1) * height + PAD
@@ -375,16 +373,11 @@
 
     own = inside(lane & 31, 8, 24)
     for k in range(count):
-        guess = first_guess[k * part : (k + 1) * part, :]
-        add = jnp.where(tm == 0, guess, 0.0)
-        less = jnp.where(tm == 0, guess, second_guess[k * part : (k + 1) * part, :])
+        less = jnp.where(tm == 0, 0.0, second_guess[k * part : (k + 1) * part, :])
         total = None
         for e in range(2):
             for odd in range(2):
-                value = []
-                for z in range(2):
-                    fine = fine_a[e][pl.ds((2 * k + z + 1) * height + PAD + odd, part, 2), :] * scale
-                    value.append((add + fine) - less)
+                value = [fine_a[e][pl.ds((2 * k + z + 1) * height + PAD + odd, part, 2), :] * scale - less for z in range(2)]
                 total = value[0] + value[1] if total is None else total + (value[0] + value[1])
                 strip[k, pl.ds(e * rows + odd, part, 2), :] = jnp.where(own, value[0], roll(value[1], 16))
         to = (k + 1) * small_height + PAD
@@ -396,6 +389,9 @@
         for k in range(count):
             at = (k + 1) * small_height + PAD
             strip[k, 2 * rows :, :] = small_a[at : at + part, :] * small_scale
+
+    for n, dest in enumerate(served(WAY_OUT, True)):
+        given[n] = strip[dest]
 
 
 def send_kernel(mine, other, *blocks):
@@ -405,24 +401,25 @@
     in_quarter = iota((part, LANES), 1) & 31
     own = inside(in_quarter, 8, 24)
     spill = (inside(in_quarter, 4, 8) | inside(in_quarter, 24, 28))[:8]
-    dests = [sent_to(masks) for masks in WAY_OUT] + [lax.axis_index("space")]
-    for dest, block in zip(dests, blocks):
-        guess = jnp.where(tm == 0, mine[dest, 2 * rows :, :], other[dest, 2 * rows :, :])
-        both = jnp.where(own, guess, roll(guess, 16))
-        block[: 2 * rows, :] = jnp.where(tm == 0, mine[dest, : 2 * rows, :], other[dest, : 2 * rows, :])
+    for n, (dest, block) in enumerate(zip(served(WAY_OUT), blocks)):
+        kept, came = mine[dest, 2 * rows :, :], other[n, 2 * rows :, :]
+        change, first = jnp.where(tm == 0, kept, came), jnp.where(tm == 0, came, kept)
+        h = [jnp.where(own, x, roll(x, 16)) for x in (first, change)]
         for e in range(2):
             for odd in range(2):
                 at = pl.ds(e * rows + odd, part, 2)
                 to = pl.ds((2 + e) * rows + odd, part, 2)
-                block[to, :] = jnp.where(tm == 0, other[dest, at, :], mine[dest, at, :]) + both
+                kept, came = mine[dest, at, :], other[n, at, :]
+                block[at, :] = (h[0] + jnp.where(tm == 0, kept, came)) - h[0]
+                block[to, :] = h[1] + jnp.where(tm == 0, came, kept)
         packed = None
         for g, by in enumerate(SPILL_TURNS):
-            piece = roll(jnp.where(spill, guess[8 * g : 8 * g + 8], 0.0), by)
+            piece = roll(jnp.where(spill, change[8 * g : 8 * g + 8], 0.0), by)
             packed = piece if packed is None else packed + piece
         block[4 * rows : 4 * rows + 8, :] = packed
 
 
-def unpack_kernel(own_block, mine_0, mine_1, mine_2, mine_3, other_0, other_1, other_2, other_3, out_hbm, strips, spilled, out, left):
+def unpack_kernel(own_block, mine_0, mine_1, mine_2, mine_3, other_0, other_1, other_2, other_3, out_hbm, strips, spilled, halves, out, left):
     tm, space = lax.axis_index("tm"), lax.axis_index("space")
     count = strips.shape[0]
     rows = out.shape[1] // 4
@@ -471,16 +468,19 @@
     from_first = ((lane & 1) << 6) + (lane >> 1)
     from_second = from_first ^ 64
     hit = [inside(lane, 16 * s, 16 * s + 16) for s in range(count)]
+    for e in range(2):
+        pieces = list(lined_up(lambda s, e=e: strips[s, e * rows : (e + 1) * rows, :], 8, rows))
+        for z in range(2):
+            parts = [roll(x, 16 * c - 8 - 16 * z) for c, x in enumerate(pieces)]
+            for j in range(4):
+                to = ((2 * z + e) * 4 + j) * rows
+                halves[to : to + rows, :] = at_strips(parts, j, hit)
     copies = []
     for z in range(2):
-        parts = []
-        for e in range(2):
-            pieces = lined_up(lambda s, e=e: strips[s, e * rows : (e + 1) * rows, :], 8, rows)
-            parts.append([roll(x, 16 * c - 8 - 16 * z) for c, x in enumerate(pieces)])
         for j in range(4):
             at = slice(j * rows, (j + 1) * rows)
             more = spilled[at, :]
-            even, odd = (at_strips(parts[e], j, hit) + more for e in range(2))
+            even, odd = (halves[((2 * z + e) * 4 + j) * rows : ((2 * z + e) * 4 + j + 1) * rows, :] + more for e in range(2))
             odd = roll(odd, 64)
             out[z, at, :LANES] = take(jnp.where(low_half, even, odd), from_first)
             out[z, at, LANES:] = take(jnp.where(low_half, odd, even), from_second)
@@ -539,23 +539,23 @@
     wide = ((count + 2) * (rows + 2 * PAD), LANES)
     small = ((count + 2) * (part + 2 * PAD), LANES)
     small_cells = (count * part, LANES)
-    (strip,) = on_core(
+    strip, given = on_core(
         march_kernel,
         [own_block, *mine, *other],
-        [(count, 5 * part, LANES)],
+        [(count, 5 * part, LANES), (len(WAY_OUT) + 1, 5 * part, LANES)],
         [fine] * 4
         + [(planes * rows, LANES)] * 2
         + [wide, wide, (count * rows, LANES), small, small]
-        + [small_cells] * 3
+        + [small_cells] * 2
         + [(planes * rows, LANES)],
     )
-    *blocks, own_block = on_core(send_kernel, [strip, swapped(strip)], [(4 * rows + 8, LANES)] * 5)
+    *blocks, own_block = on_core(send_kernel, [strip, swapped(given)], [(4 * rows + 8, LANES)] * 5)
     mine, other = exchanged(blocks, WAY_OUT)
     (out,) = on_core(
         unpack_kernel,
         [own_block, *mine, *other],
         [initial.shape],
-        [(count, 2 * rows + 8, LANES), (nx, LANES), initial.shape, pltpu.SemaphoreType.DMA((2,))],
+        [(count, 2 * rows + 8, LANES), (nx, LANES), (16 * rows, LANES), initial.shape, pltpu.SemaphoreType.DMA((2,))],
         pl.BlockSpec(memory_space=pltpu.HBM),
     )
     return out[None]

time: 53.3 us -> 52.7 us (0.989)
  starting transfers between devices: 19.7 us -> 24.1 us
  waiting for transfers between devices: 20.6 us -> 16.3 us
  Pallas kernels: 11.5 us -> 10.7 us
    ppermute x8, waiting for transfers between devices: 16.5 us -> 12.3 us  [exchanged(): mine.append(lax.ppermute(block, ('tm', 'space'), pairs))]
    ppermute x9, starting transfers between devices: 2.11 us -> 4.97 us  [swapped(): return lax.ppermute(x, 'tm', [(0, 1), (1, 0)])]
    ppermute x8, starting transfers between devices: 17.5 us -> 19.2 us  [exchanged(): mine.append(lax.ppermute(block, ('tm', 'space'), pairs))]
    pallas_call x6, Pallas kernels: 11.5 us -> 10.7 us  [on_core(): pl.pallas_call(kernel, out_shape=shapes, in_specs=[VMEM] * len(inputs), o...]
  transfers between devices with their start and end apart: 17 -> 17, of which waited for: 9 -> 8; matrix products, arithmetic and copies ran while one was open for 0% -> 0% of each run, Pallas kernels for 0% -> 0%
where the time goes in v5:
time: 52.7 us; the launch traced here: 52.4 us
  starting transfers between devices  24.1 us (46%)
  waiting for transfers between devices  16.3 us (31%)
  Pallas kernels  10.7 us (20%)
  local copies, waits for them, and re-layouts  1.25 us (2%)
    ppermute x8, starting transfers between devices, exchanged(): mine.append(lax.ppermute(block, ('tm', 'space'), pairs))  19.2 us
    ppermute x8, waiting for transfers between devices, exchanged(): mine.append(lax.ppermute(block, ('tm', 'space'), pairs))  12.3 us
    pallas_call x6, Pallas kernels, on_core(): pl.pallas_call(kernel, out_shape=shapes, in_specs=[VMEM] * len(inputs), o...  10.7 us
    ppermute x9, starting transfers between devices, swapped(): return lax.ppermute(x, 'tm', [(0, 1), (1, 0)])  4.97 us
    ppermute x9, waiting for transfers between devices, swapped(): return lax.ppermute(x, 'tm', [(0, 1), (1, 0)])  3.97 us
    unnamed x4, local copies, waits for them, and re-layouts  1.25 us
  transfers between devices with their start and end apart: 17, of which 8 were waited for; matrix products, arithmetic and copies ran while one was open for 0% of the time, Pallas kernels for 0%

profile of v5, /device:TPU:0, one launch (start us, length us, event | category | flops | bytes accessed | tf_op | source)
XLA Modules:
  0.0 52.4 jit_solution(14095486544126522390)
XLA Ops:
  0.0 0.0 copy-start
  0.0 1.0 %copy-done = f32[2,192,256]{2,1,0:T(8,128)S(1)} copy-done((f32[2,192,256]{2,1,0:T(8,128)S(1)}, f32[2,192,256]{2,1,0:T(8,128)}, u32[]{:S(2)}) %copy-start) | copy-done | bytes 393240
  1.0 0.0 copy-start.1
  1.0 0.7 %shard_map.28 = (f32[768,128]{1,0:T(8,128)S(1)}, f32[192,128]{1,0:T(8,128)S(1)}) custom-call(f32[2,192,256]{2,1,0:T(8,128)S(1)} %copy-done), custom_call_target="tpu_custom_call" | custom-call | tf_op jit(solution)/shard_map/pallas_call | solution.py:498
  1.7 0.3 copy-done.1
  2.0 0.7 %shard_map.29 = (f32[768,128]{1,0:T(8,128)S(1)}, f32[192,128]{1,0:T(8,128)S(1)}) custom-call(f32[2,192,256]{2,1,0:T(8,128)S(1)} %copy-done.1), custom_call_target="tpu_custom_call" | custom-call | tf_op jit(solution)/shard_map/pallas_call | solution.py:498
  2.7 0.4 shard_map.30
  3.1 3.0 %collective-permute-start = (f32[400,128]{1,0:T(8,128)S(1)}, f32[400,128]{1,0:T(8,128)S(1)}, u32[]{:S(2)}, u32[]{:S(2)}) collective-permute-start(f32[400,128]{1,0:T(8,128)S(1)} %get-tuple-element.26), channel_id=1, source_target_pairs={{0,1},{1,0},{2,3},{3,2},{4,5},{5,4},{6,7},{7,6},{8,12},{9,13},{10,... | collective-permute-start | bytes 614408 | tf_op jit(solution)/shard_map/ppermute | solution.py:517
  6.1 2.6 %collective-permute-start.1 = (f32[400,128]{1,0:T(8,128)S(1)}, f32[400,128]{1,0:T(8,128)S(1)}, u32[]{:S(2)}, u32[]{:S(2)}) collective-permute-start(f32[400,128]{1,0:T(8,128)S(1)} %get-tuple-element.27), channel_id=1, source_target_pairs={{0,5},{1,4},{2,7},{3,6},{4,1},{5,0},{6,3},{7,2},{8,10},{9,11},{10,... | collective-permute-start | bytes 614408 | tf_op jit(solution)/shard_map/ppermute | solution.py:517
  8.7 2.5 %collective-permute-start.2 = (f32[400,128]{1,0:T(8,128)S(1)}, f32[400,128]{1,0:T(8,128)S(1)}, u32[]{:S(2)}, u32[]{:S(2)}) collective-permute-start(f32[400,128]{1,0:T(8,128)S(1)} %get-tuple-element.28), channel_id=1, source_target_pairs={{0,3},{1,2},{2,1},{3,0},{4,7},{5,6},{6,5},{7,4},{8,14},{9,15},{10,... | collective-permute-start | bytes 614408 | tf_op jit(solution)/shard_map/ppermute | solution.py:517
  11.2 1.9 %collective-permute-start.3 = (f32[400,128]{1,0:T(8,128)S(1)}, f32[400,128]{1,0:T(8,128)S(1)}, u32[]{:S(2)}, u32[]{:S(2)}) collective-permute-start(f32[400,128]{1,0:T(8,128)S(1)} %get-tuple-element.29), channel_id=1, source_target_pairs={{0,7},{1,6},{2,5},{3,4},{4,3},{5,2},{6,1},{7,0},{16,23},{17,22},{1... | collective-permute-start | bytes 614408 | tf_op jit(solution)/shard_map/ppermute | solution.py:517
  13.1 0.0 collective-permute-done.mine_0
  13.1 1.9 %collective-permute-start.4 = (f32[400,128]{1,0:T(8,128)S(1)}, f32[400,128]{1,0:T(8,128)S(1)}, u32[]{:S(2)}, u32[]{:S(2)}) collective-permute-start(f32[400,128]{1,0:T(8,128)S(1)} %collective-permute-done.mine_0), channel_id=1, source_target_pairs={{0,8},{8,0},{1,9},{9,1},{2,10},{10,2},{3,11},{11,3},{4,12},{12,4},... | collective-permute-start | bytes 614408 | tf_op jit(solution)/shard_map/ppermute | solution.py:509
  15.0 8.2 %collective-permute-done.1.mine_1 = f32[400,128]{1,0:T(8,128)S(1)} collective-permute-done((f32[400,128]{1,0:T(8,128)S(1)}, f32[400,128]{1,0:T(8,128)S(1)}, u32[]{:S(2)}, u32[]{:S(2)}) %collective-permute-start.1) | collective-permute-done | bytes 204832 | tf_op jit(solution)/shard_map/ppermute | solution.py:517
  23.2 0.0 collective-permute-start.5
  23.2 0.0 collective-permute-done.2.mine_2
  23.2 0.5 collective-permute-start.6
  23.7 0.0 collective-permute-done.3.mine_3
  23.7 0.1 collective-permute-start.7
  23.8 0.0 collective-permute-done.4.other_0
  23.8 0.9 %collective-permute-done.5.other_1 = f32[400,128]{1,0:T(8,128)S(1)} collective-permute-done((f32[400,128]{1,0:T(8,128)S(1)}, f32[400,128]{1,0:T(8,128)S(1)}, u32[]{:S(2)}, u32[]{:S(2)}) %collective-permute-start.5) | collective-permute-done | bytes 204832 | tf_op jit(solution)/shard_map/ppermute | solution.py:509
  24.7 0.3 collective-permute-done.6.other_2
  25.0 0.3 collective-permute-done.7.other_3
  25.3 6.9 %shard_map.31 = (f32[8,120,128]{2,1,0:T(8,128)S(1)}, f32[5,120,128]{2,1,0:T(8,128)S(1)}) custom-call(f32[400,128]{1,0:T(8,128)S(1)} %get-tuple-element.25.own_block, f32[400,128]{1,0:T(8,128)S(1)} %collective-permute-done.mine_0, f32[400,128]{1,0:T(8,128)S(1)} %collective-permute-done.1.mine_1, f32[400,128]{1,0:T(8,128)S(1)} %collective-permute-done.2.mine_2, ...), custom_call_target="tpu_custom_call" | custom-call | tf_op jit(solution)/shard_map/pallas_call | solution.py:498
  32.2 1.0 %collective-permute-start.8 = (f32[5,120,128]{2,1,0:T(8,128)S(1)}, f32[5,120,128]{2,1,0:T(8,128)S(1)}, u32[]{:S(2)}, u32[]{:S(2)}) collective-permute-start(f32[5,120,128]{2,1,0:T(8,128)S(1)} %get-tuple-element.31), channel_id=1, source_target_pairs={{0,8},{8,0},{1,9},{9,1},{2,10},{10,2},{3,11},{11,3},{4,12},{12,4},... | collective-permute-start | bytes 921608 | tf_op jit(solution)/shard_map/ppermute | solution.py:509
  33.2 1.2 %collective-permute-done.8.other = f32[5,120,128]{2,1,0:T(8,128)S(1)} collective-permute-done((f32[5,120,128]{2,1,0:T(8,128)S(1)}, f32[5,120,128]{2,1,0:T(8,128)S(1)}, u32[]{:S(2)}, u32[]{:S(2)}) %collective-permute-start.8) | collective-permute-done | bytes 307232 | tf_op jit(solution)/shard_map/ppermute | solution.py:509
  34.4 0.1 shard_map.32
  34.5 5.2 %collective-permute-start.9 = (f32[200,128]{1,0:T(8,128)S(1)}, f32[200,128]{1,0:T(8,128)S(1)}, u32[]{:S(2)}, u32[]{:S(2)}) collective-permute-start(f32[200,128]{1,0:T(8,128)S(1)} %get-tuple-element.33), channel_id=1, source_target_pairs={{0,4},{1,5},{2,6},{3,7},{4,0},{5,1},{6,2},{7,3},{8,13},{9,12},{10,... | collective-permute-start | bytes 307208 | tf_op jit(solution)/shard_map/ppermute | solution.py:517
  39.7 0.3 collective-permute-start.10
  40.1 0.7 %collective-permute-start.11 = (f32[200,128]{1,0:T(8,128)S(1)}, f32[200,128]{1,0:T(8,128)S(1)}, u32[]{:S(2)}, u32[]{:S(2)}) collective-permute-start(f32[200,128]{1,0:T(8,128)S(1)} %get-tuple-element.35), channel_id=1, source_target_pairs={{0,1},{1,0},{2,3},{3,2},{4,5},{5,4},{6,7},{7,6},{8,10},{9,11},{10,... | collective-permute-start | bytes 307208 | tf_op jit(solution)/shard_map/ppermute | solution.py:517
  40.7 3.0 %collective-permute-start.12 = (f32[200,128]{1,0:T(8,128)S(1)}, f32[200,128]{1,0:T(8,128)S(1)}, u32[]{:S(2)}, u32[]{:S(2)}) collective-permute-start(f32[200,128]{1,0:T(8,128)S(1)} %get-tuple-element.36), channel_id=1, source_target_pairs={{0,3},{1,2},{2,1},{3,0},{4,7},{5,6},{6,5},{7,4},{16,19},{17,18},{1... | collective-permute-start | bytes 307208 | tf_op jit(solution)/shard_map/ppermute | solution.py:517
  43.7 4.1 %collective-permute-done.9.mine_0 = f32[200,128]{1,0:T(8,128)S(1)} collective-permute-done((f32[200,128]{1,0:T(8,128)S(1)}, f32[200,128]{1,0:T(8,128)S(1)}, u32[]{:S(2)}, u32[]{:S(2)}) %collective-permute-start.9) | collective-permute-done | bytes 102432 | tf_op jit(solution)/shard_map/ppermute | solution.py:517
  47.8 0.0 collective-permute-start.13
  47.8 0.0 collective-permute-done.10.mine_1
  47.8 0.5 collective-permute-start.14
  48.4 0.0 collective-permute-done.11.mine_2
  48.4 1.0 %collective-permute-start.15 = (f32[200,128]{1,0:T(8,128)S(1)}, f32[200,128]{1,0:T(8,128)S(1)}, u32[]{:S(2)}, u32[]{:S(2)}) collective-permute-start(f32[200,128]{1,0:T(8,128)S(1)} %collective-permute-done.11.mine_2), channel_id=1, source_target_pairs={{0,8},{8,0},{1,9},{9,1},{2,10},{10,2},{3,11},{11,3},{4,12},{12,4},... | collective-permute-start | bytes 307208 | tf_op jit(solution)/shard_map/ppermute | solution.py:509
  49.4 0.0 collective-permute-done.12.mine_3
  49.4 0.0 collective-permute-start.16
  49.4 0.0 collective-permute-done.13.other_0
  49.4 0.0 collective-permute-done.14.other_1
  49.4 0.9 %collective-permute-done.15.other_2 = f32[200,128]{1,0:T(8,128)S(1)} collective-permute-done((f32[200,128]{1,0:T(8,128)S(1)}, f32[200,128]{1,0:T(8,128)S(1)}, u32[]{:S(2)}, u32[]{:S(2)}) %collective-permute-start.15) | collective-permute-done | bytes 102432 | tf_op jit(solution)/shard_map/ppermute | solution.py:509
  50.3 0.4 collective-permute-done.16.other_3
  50.7 1.8 %shard_map.33 = f32[2,192,256]{2,1,0:T(8,128)} custom-call(f32[200,128]{1,0:T(8,128)S(1)} %get-tuple-element.32.own_block, f32[200,128]{1,0:T(8,128)S(1)} %collective-permute-done.9.mine_0, f32[200,128]{1,0:T(8,128)S(1)} %collective-permute-done.10.mine_1, f32[200,128]{1,0:T(8,128)S(1)} %collective-permute-done.11.mine_2, ...), custom_call_target="tpu_custom_call" | custom-call | tf_op jit(solution)/shard_map/pallas_call | solution.py:498
Async XLA Ops:
  0.0 1.0 %copy-start = (f32[2,192,256]{2,1,0:T(8,128)S(1)}, f32[2,192,256]{2,1,0:T(8,128)}, u32[]{:S(2)}) copy-start(f32[2,192,256]{2,1,0:T(8,128)} %field.2) | copy-start | bytes 1179652
  1.0 1.0 %copy-start.1 = (f32[2,192,256]{2,1,0:T(8,128)S(1)}, f32[2,192,256]{2,1,0:T(8,128)}, u32[]{:S(2)}) copy-start(f32[2,192,256]{2,1,0:T(8,128)} %field.3) | copy-start | bytes 1179652
  3.1 10.0 %collective-permute-start = (f32[400,128]{1,0:T(8,128)S(1)}, f32[400,128]{1,0:T(8,128)S(1)}, u32[]{:S(2)}, u32[]{:S(2)}) collective-permute-start(f32[400,128]{1,0:T(8,128)S(1)} %get-tuple-element.26), channel_id=1, source_target_pairs={{0,1},{1,0},{2,3},{3,2},{4,5},{5,4},{6,7},{7,6},{8,12},{9,13},{10,... | collective-permute-start | bytes 614408 | tf_op jit(solution)/shard_map/ppermute | solution.py:517
  6.1 17.1 %collective-permute-start.1 = (f32[400,128]{1,0:T(8,128)S(1)}, f32[400,128]{1,0:T(8,128)S(1)}, u32[]{:S(2)}, u32[]{:S(2)}) collective-permute-start(f32[400,128]{1,0:T(8,128)S(1)} %get-tuple-element.27), channel_id=1, source_target_pairs={{0,5},{1,4},{2,7},{3,6},{4,1},{5,0},{6,3},{7,2},{8,10},{9,11},{10,... | collective-permute-start | bytes 614408 | tf_op jit(solution)/shard_map/ppermute | solution.py:517
  8.7 14.5 %collective-permute-start.2 = (f32[400,128]{1,0:T(8,128)S(1)}, f32[400,128]{1,0:T(8,128)S(1)}, u32[]{:S(2)}, u32[]{:S(2)}) collective-permute-start(f32[400,128]{1,0:T(8,128)S(1)} %get-tuple-element.28), channel_id=1, source_target_pairs={{0,3},{1,2},{2,1},{3,0},{4,7},{5,6},{6,5},{7,4},{8,14},{9,15},{10,... | collective-permute-start | bytes 614408 | tf_op jit(solution)/shard_map/ppermute | solution.py:517
  11.2 12.6 %collective-permute-start.3 = (f32[400,128]{1,0:T(8,128)S(1)}, f32[400,128]{1,0:T(8,128)S(1)}, u32[]{:S(2)}, u32[]{:S(2)}) collective-permute-start(f32[400,128]{1,0:T(8,128)S(1)} %get-tuple-element.29), channel_id=1, source_target_pairs={{0,7},{1,6},{2,5},{3,4},{4,3},{5,2},{6,1},{7,0},{16,23},{17,22},{1... | collective-permute-start | bytes 614408 | tf_op jit(solution)/shard_map/ppermute | solution.py:517
  13.1 10.7 %collective-permute-start.4 = (f32[400,128]{1,0:T(8,128)S(1)}, f32[400,128]{1,0:T(8,128)S(1)}, u32[]{:S(2)}, u32[]{:S(2)}) collective-permute-start(f32[400,128]{1,0:T(8,128)S(1)} %collective-permute-done.mine_0), channel_id=1, source_target_pairs={{0,8},{8,0},{1,9},{9,1},{2,10},{10,2},{3,11},{11,3},{4,12},{12,4},... | collective-permute-start | bytes 614408 | tf_op jit(solution)/shard_map/ppermute | solution.py:509
  23.2 1.5 %collective-permute-start.5 = (f32[400,128]{1,0:T(8,128)S(1)}, f32[400,128]{1,0:T(8,128)S(1)}, u32[]{:S(2)}, u32[]{:S(2)}) collective-permute-start(f32[400,128]{1,0:T(8,128)S(1)} %collective-permute-done.1.mine_1), channel_id=1, source_target_pairs={{0,8},{8,0},{1,9},{9,1},{2,10},{10,2},{3,11},{11,3},{4,12},{12,4},... | collective-permute-start | bytes 614408 | tf_op jit(solution)/shard_map/ppermute | solution.py:509
  23.2 1.7 %collective-permute-start.6 = (f32[400,128]{1,0:T(8,128)S(1)}, f32[400,128]{1,0:T(8,128)S(1)}, u32[]{:S(2)}, u32[]{:S(2)}) collective-permute-start(f32[400,128]{1,0:T(8,128)S(1)} %collective-permute-done.2.mine_2), channel_id=1, source_target_pairs={{0,8},{8,0},{1,9},{9,1},{2,10},{10,2},{3,11},{11,3},{4,12},{12,4},... | collective-permute-start | bytes 614408 | tf_op jit(solution)/shard_map/ppermute | solution.py:509
  23.7 1.5 %collective-permute-start.7 = (f32[400,128]{1,0:T(8,128)S(1)}, f32[400,128]{1,0:T(8,128)S(1)}, u32[]{:S(2)}, u32[]{:S(2)}) collective-permute-start(f32[400,128]{1,0:T(8,128)S(1)} %collective-permute-done.3.mine_3), channel_id=1, source_target_pairs={{0,8},{8,0},{1,9},{9,1},{2,10},{10,2},{3,11},{11,3},{4,12},{12,4},... | collective-permute-start | bytes 614408 | tf_op jit(solution)/shard_map/ppermute | solution.py:509
  32.2 2.2 %collective-permute-start.8 = (f32[5,120,128]{2,1,0:T(8,128)S(1)}, f32[5,120,128]{2,1,0:T(8,128)S(1)}, u32[]{:S(2)}, u32[]{:S(2)}) collective-permute-start(f32[5,120,128]{2,1,0:T(8,128)S(1)} %get-tuple-element.31), channel_id=1, source_target_pairs={{0,8},{8,0},{1,9},{9,1},{2,10},{10,2},{3,11},{11,3},{4,12},{12,4},... | collective-permute-start | bytes 921608 | tf_op jit(solution)/shard_map/ppermute | solution.py:509
  34.5 13.3 %collective-permute-start.9 = (f32[200,128]{1,0:T(8,128)S(1)}, f32[200,128]{1,0:T(8,128)S(1)}, u32[]{:S(2)}, u32[]{:S(2)}) collective-permute-start(f32[200,128]{1,0:T(8,128)S(1)} %get-tuple-element.33), channel_id=1, source_target_pairs={{0,4},{1,5},{2,6},{3,7},{4,0},{5,1},{6,2},{7,3},{8,13},{9,12},{10,... | collective-permute-start | bytes 307208 | tf_op jit(solution)/shard_map/ppermute | solution.py:517
  39.7 8.1 %collective-permute-start.10 = (f32[200,128]{1,0:T(8,128)S(1)}, f32[200,128]{1,0:T(8,128)S(1)}, u32[]{:S(2)}, u32[]{:S(2)}) collective-permute-start(f32[200,128]{1,0:T(8,128)S(1)} %get-tuple-element.34), channel_id=1, source_target_pairs={{0,6},{1,7},{2,4},{3,5},{4,2},{5,3},{6,0},{7,1},{8,15},{9,14},{10,... | collective-permute-start | bytes 307208 | tf_op jit(solution)/shard_map/ppermute | solution.py:517
  40.1 8.3 %collective-permute-start.11 = (f32[200,128]{1,0:T(8,128)S(1)}, f32[200,128]{1,0:T(8,128)S(1)}, u32[]{:S(2)}, u32[]{:S(2)}) collective-permute-start(f32[200,128]{1,0:T(8,128)S(1)} %get-tuple-element.35), channel_id=1, source_target_pairs={{0,1},{1,0},{2,3},{3,2},{4,5},{5,4},{6,7},{7,6},{8,10},{9,11},{10,... | collective-permute-start | bytes 307208 | tf_op jit(solution)/shard_map/ppermute | solution.py:517
  40.7 8.6 %collective-permute-start.12 = (f32[200,128]{1,0:T(8,128)S(1)}, f32[200,128]{1,0:T(8,128)S(1)}, u32[]{:S(2)}, u32[]{:S(2)}) collective-permute-start(f32[200,128]{1,0:T(8,128)S(1)} %get-tuple-element.36), channel_id=1, source_target_pairs={{0,3},{1,2},{2,1},{3,0},{4,7},{5,6},{6,5},{7,4},{16,19},{17,18},{1... | collective-permute-start | bytes 307208 | tf_op jit(solution)/shard_map/ppermute | solution.py:517
  47.8 1.5 %collective-permute-start.13 = (f32[200,128]{1,0:T(8,128)S(1)}, f32[200,128]{1,0:T(8,128)S(1)}, u32[]{:S(2)}, u32[]{:S(2)}) collective-permute-start(f32[200,128]{1,0:T(8,128)S(1)} %collective-permute-done.9.mine_0), channel_id=1, source_target_pairs={{0,8},{8,0},{1,9},{9,1},{2,10},{10,2},{3,11},{11,3},{4,12},{12,4},... | collective-permute-start | bytes 307208 | tf_op jit(solution)/shard_map/ppermute | solution.py:509
  47.8 1.5 %collective-permute-start.14 = (f32[200,128]{1,0:T(8,128)S(1)}, f32[200,128]{1,0:T(8,128)S(1)}, u32[]{:S(2)}, u32[]{:S(2)}) collective-permute-start(f32[200,128]{1,0:T(8,128)S(1)} %collective-permute-done.10.mine_1), channel_id=1, source_target_pairs={{0,8},{8,0},{1,9},{9,1},{2,10},{10,2},{3,11},{11,3},{4,12},{12,4},... | collective-permute-start | bytes 307208 | tf_op jit(solution)/shard_map/ppermute | solution.py:509
  48.4 2.0 %collective-permute-start.15 = (f32[200,128]{1,0:T(8,128)S(1)}, f32[200,128]{1,0:T(8,128)S(1)}, u32[]{:S(2)}, u32[]{:S(2)}) collective-permute-start(f32[200,128]{1,0:T(8,128)S(1)} %collective-permute-done.11.mine_2), channel_id=1, source_target_pairs={{0,8},{8,0},{1,9},{9,1},{2,10},{10,2},{3,11},{11,3},{4,12},{12,4},... | collective-permute-start | bytes 307208 | tf_op jit(solution)/shard_map/ppermute | solution.py:509
  49.4 1.3 %collective-permute-start.16 = (f32[200,128]{1,0:T(8,128)S(1)}, f32[200,128]{1,0:T(8,128)S(1)}, u32[]{:S(2)}, u32[]{:S(2)}) collective-permute-start(f32[200,128]{1,0:T(8,128)S(1)} %collective-permute-done.12.mine_3), channel_id=1, source_target_pairs={{0,8},{8,0},{1,9},{9,1},{2,10},{10,2},{3,11},{11,3},{4,12},{12,4},... | collective-permute-start | bytes 307208 | tf_op jit(solution)/shard_map/ppermute | solution.py:509

commit v6 on v5

--- a/solution.py
+++ b/solution.py
@@ -220,7 +220,7 @@
     return [sent_to(masks[::-1] if other_core else masks) for masks in way] + [lax.axis_index("space")]
 
 
-def prepare_kernel(turns, field, turned, edges, sums, coarse):
+def prepare_kernel(turns, field, turned, edges, split, sums, coarse):
     rows = field.shape[1] // 4
     part = rows // 2
     lane = iota((rows, LANES), 1)
@@ -230,19 +230,26 @@
     for z in range(2):
         for j in range(4):
             at = slice(j * rows, (j + 1) * rows)
-            left, right = take(field[z, at, :LANES], even_odd), take(field[z, at, LANES:], odd_even)
-            even = jnp.where(low_half, left, right)
-            odd = roll(jnp.where(low_half, right, left), 64)
+            for n, (x, lanes) in enumerate(((field[z, at, :LANES], even_odd), (field[z, at, LANES:], odd_even))):
+                to = ((2 * z + n) * 4 + j) * rows
+                split[to : to + rows, :] = take(x, lanes)
+    for z in range(2):
+        for j in range(4):
+            at = slice(j * rows, (j + 1) * rows)
+            left, right = (split[((2 * z + n) * 4 + j) * rows : ((2 * z + n) * 4 + j + 1) * rows, :] for n in range(2))
+            even = roll(jnp.where(low_half, left, right), 32 * j)
+            odd = roll(jnp.where(low_half, right, left), 32 * j + 64)
             for e, x in enumerate((even, odd)):
                 to = ((2 * z + e) * 4 + j) * rows
-                turned[to : to + rows, :] = roll(x, 32 * j)
+                turned[to : to + rows, :] = x
             if z == 0:
                 sums[at, :] = even + odd
             else:
                 sums[at, :] = (sums[at, :] + (even + odd)) * 0.125
     for j in range(4):
         at = j * rows
-        coarse[j * part : (j + 1) * part, :] = sums[pl.ds(at, part, 2), :] + sums[pl.ds(at + 1, part, 2), :]
+        x = sums[pl.ds(at, part, 2), :] + sums[pl.ds(at + 1, part, 2), :]
+        coarse[j * part : (j + 1) * part, :] = roll(x, -32 * j)
     for g in range(2 * rows // EDGE_ROWS):
         x = coarse[g * EDGE_ROWS : (g + 1) * EDGE_ROWS, :]
         place = 64 * (g // 3) + 16 * (g % 3)
@@ -419,7 +426,7 @@
         block[4 * rows : 4 * rows + 8, :] = packed
 
 
-def unpack_kernel(own_block, mine_0, mine_1, mine_2, mine_3, other_0, other_1, other_2, other_3, out_hbm, strips, spilled, halves, out, left):
+def unpack_kernel(own_block, mine_0, mine_1, mine_2, mine_3, other_0, other_1, other_2, other_3, out_hbm, strips, spilled, turned, halves, out, left):
     tm, space = lax.axis_index("tm"), lax.axis_index("space")
     count = strips.shape[0]
     rows = out.shape[1] // 4
@@ -467,21 +474,23 @@
     low_half = lane < 64
     from_first = ((lane & 1) << 6) + (lane >> 1)
     from_second = from_first ^ 64
-    hit = [inside(lane, 16 * s, 16 * s + 16) for s in range(count)]
+    hit = [[inside((lane + 64 * e) & (LANES - 1), 16 * s, 16 * s + 16) for s in range(count)] for e in range(2)]
     for e in range(2):
         pieces = list(lined_up(lambda s, e=e: strips[s, e * rows : (e + 1) * rows, :], 8, rows))
         for z in range(2):
-            parts = [roll(x, 16 * c - 8 - 16 * z) for c, x in enumerate(pieces)]
+            parts = [roll(x, 16 * c - 8 - 16 * z + 64 * e) for c, x in enumerate(pieces)]
             for j in range(4):
                 to = ((2 * z + e) * 4 + j) * rows
-                halves[to : to + rows, :] = at_strips(parts, j, hit)
+                halves[to : to + rows, :] = at_strips(parts, j, hit[e])
+    for j in range(4):
+        at = slice(j * rows, (j + 1) * rows)
+        turned[at, :] = roll(spilled[at, :], 64)
     copies = []
     for z in range(2):
         for j in range(4):
             at = slice(j * rows, (j + 1) * rows)
-            more = spilled[at, :]
-            even, odd = (halves[((2 * z + e) * 4 + j) * rows : ((2 * z + e) * 4 + j + 1) * rows, :] + more for e in range(2))
-            odd = roll(odd, 64)
+            even, odd = (halves[((2 * z + e) * 4 + j) * rows : ((2 * z + e) * 4 + j + 1) * rows, :] for e in range(2))
+            even, odd = even + spilled[at, :], odd + turned[at, :]
             out[z, at, :LANES] = take(jnp.where(low_half, even, odd), from_first)
             out[z, at, LANES:] = take(jnp.where(low_half, odd, even), from_second)
         copies.append(pltpu.make_async_copy(out.at[z], out_hbm.at[z], left.at[z]))
@@ -531,7 +540,7 @@
             functools.partial(prepare_kernel, turns),
             [field],
             [(16 * rows, LANES), (4 * rows, LANES)],
-            [(4 * rows, LANES), (2 * rows, LANES)],
+            [(16 * rows, LANES), (4 * rows, LANES), (2 * rows, LANES)],
         )
     *blocks, own_block = on_core(fill_kernel, prepared, [block] * 5)
     mine, other = exchanged(blocks, WAY_IN)
@@ -555,7 +564,7 @@
         unpack_kernel,
         [own_block, *mine, *other],
         [initial.shape],
-        [(count, 2 * rows + 8, LANES), (nx, LANES), (16 * rows, LANES), initial.shape, pltpu.SemaphoreType.DMA((2,))],
+        [(count, 2 * rows + 8, LANES), (nx, LANES), (nx, LANES), (16 * rows, LANES), initial.shape, pltpu.SemaphoreType.DMA((2,))],
         pl.BlockSpec(memory_space=pltpu.HBM),
     )
     return out[None]

time: 52.7 us -> 51.9 us (0.985)
  Pallas kernels: 10.7 us -> 9.6 us
    pallas_call x6, Pallas kernels: 10.7 us -> 9.6 us  [on_core(): pl.pallas_call(kernel, out_shape=shapes, in_specs=[VMEM] * len(inputs), o...]
where the time goes in v6:
time: 51.9 us; the launch traced here: 51.7 us
  starting transfers between devices  24.1 us (46%)
  waiting for transfers between devices  16.3 us (31%)
  Pallas kernels  9.6 us (18%)
  local copies, waits for them, and re-layouts  1.56 us (3%)
    ppermute x8, starting transfers between devices, exchanged(): mine.append(lax.ppermute(block, ('tm', 'space'), pairs))  19.2 us
    ppermute x8, waiting for transfers between devices, exchanged(): mine.append(lax.ppermute(block, ('tm', 'space'), pairs))  12.3 us
    pallas_call x6, Pallas kernels, on_core(): pl.pallas_call(kernel, out_shape=shapes, in_specs=[VMEM] * len(inputs), o...  9.6 us
    ppermute x9, starting transfers between devices, swapped(): return lax.ppermute(x, 'tm', [(0, 1), (1, 0)])  4.97 us
    ppermute x9, waiting for transfers between devices, swapped(): return lax.ppermute(x, 'tm', [(0, 1), (1, 0)])  3.97 us
    unnamed x4, local copies, waits for them, and re-layouts  1.56 us
  transfers between devices with their start and end apart: 17, of which 8 were waited for; matrix products, arithmetic and copies ran while one was open for 0% of the time, Pallas kernels for 0%

profile of v6, /device:TPU:0, one launch (start us, length us, event | category | flops | bytes accessed | tf_op | source)
XLA Modules:
  0.0 51.7 jit_solution(8836442249412329542)
XLA Ops:
  0.0 0.0 copy-start
  0.0 1.0 %copy-done = f32[2,192,256]{2,1,0:T(8,128)S(1)} copy-done((f32[2,192,256]{2,1,0:T(8,128)S(1)}, f32[2,192,256]{2,1,0:T(8,128)}, u32[]{:S(2)}) %copy-start) | copy-done | bytes 393240
  1.0 0.0 copy-start.1
  1.0 0.4 shard_map.28
  1.4 0.6 %copy-done.1 = f32[2,192,256]{2,1,0:T(8,128)S(1)} copy-done((f32[2,192,256]{2,1,0:T(8,128)S(1)}, f32[2,192,256]{2,1,0:T(8,128)}, u32[]{:S(2)}) %copy-start.1) | copy-done | bytes 393240
  2.0 0.4 shard_map.29
  2.4 0.4 shard_map.30
  2.8 3.0 %collective-permute-start = (f32[400,128]{1,0:T(8,128)S(1)}, f32[400,128]{1,0:T(8,128)S(1)}, u32[]{:S(2)}, u32[]{:S(2)}) collective-permute-start(f32[400,128]{1,0:T(8,128)S(1)} %get-tuple-element.26), channel_id=1, source_target_pairs={{0,1},{1,0},{2,3},{3,2},{4,5},{5,4},{6,7},{7,6},{8,12},{9,13},{10,... | collective-permute-start | bytes 614408 | tf_op jit(solution)/shard_map/ppermute | solution.py:526
  5.8 2.6 %collective-permute-start.1 = (f32[400,128]{1,0:T(8,128)S(1)}, f32[400,128]{1,0:T(8,128)S(1)}, u32[]{:S(2)}, u32[]{:S(2)}) collective-permute-start(f32[400,128]{1,0:T(8,128)S(1)} %get-tuple-element.27), channel_id=1, source_target_pairs={{0,5},{1,4},{2,7},{3,6},{4,1},{5,0},{6,3},{7,2},{8,10},{9,11},{10,... | collective-permute-start | bytes 614408 | tf_op jit(solution)/shard_map/ppermute | solution.py:526
  8.4 2.5 %collective-permute-start.2 = (f32[400,128]{1,0:T(8,128)S(1)}, f32[400,128]{1,0:T(8,128)S(1)}, u32[]{:S(2)}, u32[]{:S(2)}) collective-permute-start(f32[400,128]{1,0:T(8,128)S(1)} %get-tuple-element.28), channel_id=1, source_target_pairs={{0,3},{1,2},{2,1},{3,0},{4,7},{5,6},{6,5},{7,4},{8,14},{9,15},{10,... | collective-permute-start | bytes 614408 | tf_op jit(solution)/shard_map/ppermute | solution.py:526
  10.9 1.9 %collective-permute-start.3 = (f32[400,128]{1,0:T(8,128)S(1)}, f32[400,128]{1,0:T(8,128)S(1)}, u32[]{:S(2)}, u32[]{:S(2)}) collective-permute-start(f32[400,128]{1,0:T(8,128)S(1)} %get-tuple-element.29), channel_id=1, source_target_pairs={{0,7},{1,6},{2,5},{3,4},{4,3},{5,2},{6,1},{7,0},{16,23},{17,22},{1... | collective-permute-start | bytes 614408 | tf_op jit(solution)/shard_map/ppermute | solution.py:526
  12.8 0.0 collective-permute-done.mine_0
  12.8 1.9 %collective-permute-start.4 = (f32[400,128]{1,0:T(8,128)S(1)}, f32[400,128]{1,0:T(8,128)S(1)}, u32[]{:S(2)}, u32[]{:S(2)}) collective-permute-start(f32[400,128]{1,0:T(8,128)S(1)} %collective-permute-done.mine_0), channel_id=1, source_target_pairs={{0,8},{8,0},{1,9},{9,1},{2,10},{10,2},{3,11},{11,3},{4,12},{12,4},... | collective-permute-start | bytes 614408 | tf_op jit(solution)/shard_map/ppermute | solution.py:518
  14.7 8.2 %collective-permute-done.1.mine_1 = f32[400,128]{1,0:T(8,128)S(1)} collective-permute-done((f32[400,128]{1,0:T(8,128)S(1)}, f32[400,128]{1,0:T(8,128)S(1)}, u32[]{:S(2)}, u32[]{:S(2)}) %collective-permute-start.1) | collective-permute-done | bytes 204832 | tf_op jit(solution)/shard_map/ppermute | solution.py:526
  22.9 0.0 collective-permute-start.5
  22.9 0.0 collective-permute-done.2.mine_2
  22.9 0.5 collective-permute-start.6
  23.4 0.0 collective-permute-done.3.mine_3
  23.4 0.1 collective-permute-start.7
  23.5 0.0 collective-permute-done.4.other_0
  23.5 0.9 %collective-permute-done.5.other_1 = f32[400,128]{1,0:T(8,128)S(1)} collective-permute-done((f32[400,128]{1,0:T(8,128)S(1)}, f32[400,128]{1,0:T(8,128)S(1)}, u32[]{:S(2)}, u32[]{:S(2)}) %collective-permute-start.5) | collective-permute-done | bytes 204832 | tf_op jit(solution)/shard_map/ppermute | solution.py:518
  24.4 0.3 collective-permute-done.6.other_2
  24.7 0.3 collective-permute-done.7.other_3
  25.0 6.9 %shard_map.31 = (f32[8,120,128]{2,1,0:T(8,128)S(1)}, f32[5,120,128]{2,1,0:T(8,128)S(1)}) custom-call(f32[400,128]{1,0:T(8,128)S(1)} %get-tuple-element.25.own_block, f32[400,128]{1,0:T(8,128)S(1)} %collective-permute-done.mine_0, f32[400,128]{1,0:T(8,128)S(1)} %collective-permute-done.1.mine_1, f32[400,128]{1,0:T(8,128)S(1)} %collective-permute-done.2.mine_2, ...), custom_call_target="tpu_custom_call" | custom-call | tf_op jit(solution)/shard_map/pallas_call | solution.py:507
  31.9 1.0 %collective-permute-start.8 = (f32[5,120,128]{2,1,0:T(8,128)S(1)}, f32[5,120,128]{2,1,0:T(8,128)S(1)}, u32[]{:S(2)}, u32[]{:S(2)}) collective-permute-start(f32[5,120,128]{2,1,0:T(8,128)S(1)} %get-tuple-element.31), channel_id=1, source_target_pairs={{0,8},{8,0},{1,9},{9,1},{2,10},{10,2},{3,11},{11,3},{4,12},{12,4},... | collective-permute-start | bytes 921608 | tf_op jit(solution)/shard_map/ppermute | solution.py:518
  32.9 1.2 %collective-permute-done.8.other = f32[5,120,128]{2,1,0:T(8,128)S(1)} collective-permute-done((f32[5,120,128]{2,1,0:T(8,128)S(1)}, f32[5,120,128]{2,1,0:T(8,128)S(1)}, u32[]{:S(2)}, u32[]{:S(2)}) %collective-permute-start.8) | collective-permute-done | bytes 307232 | tf_op jit(solution)/shard_map/ppermute | solution.py:518
  34.1 0.1 shard_map.32
  34.2 5.2 %collective-permute-start.9 = (f32[200,128]{1,0:T(8,128)S(1)}, f32[200,128]{1,0:T(8,128)S(1)}, u32[]{:S(2)}, u32[]{:S(2)}) collective-permute-start(f32[200,128]{1,0:T(8,128)S(1)} %get-tuple-element.33), channel_id=1, source_target_pairs={{0,4},{1,5},{2,6},{3,7},{4,0},{5,1},{6,2},{7,3},{8,13},{9,12},{10,... | collective-permute-start | bytes 307208 | tf_op jit(solution)/shard_map/ppermute | solution.py:526
  39.4 0.3 collective-permute-start.10
  39.8 0.7 %collective-permute-start.11 = (f32[200,128]{1,0:T(8,128)S(1)}, f32[200,128]{1,0:T(8,128)S(1)}, u32[]{:S(2)}, u32[]{:S(2)}) collective-permute-start(f32[200,128]{1,0:T(8,128)S(1)} %get-tuple-element.35), channel_id=1, source_target_pairs={{0,1},{1,0},{2,3},{3,2},{4,5},{5,4},{6,7},{7,6},{8,10},{9,11},{10,... | collective-permute-start | bytes 307208 | tf_op jit(solution)/shard_map/ppermute | solution.py:526
  40.4 3.0 %collective-permute-start.12 = (f32[200,128]{1,0:T(8,128)S(1)}, f32[200,128]{1,0:T(8,128)S(1)}, u32[]{:S(2)}, u32[]{:S(2)}) collective-permute-start(f32[200,128]{1,0:T(8,128)S(1)} %get-tuple-element.36), channel_id=1, source_target_pairs={{0,3},{1,2},{2,1},{3,0},{4,7},{5,6},{6,5},{7,4},{16,19},{17,18},{1... | collective-permute-start | bytes 307208 | tf_op jit(solution)/shard_map/ppermute | solution.py:526
  43.4 4.1 %collective-permute-done.9.mine_0 = f32[200,128]{1,0:T(8,128)S(1)} collective-permute-done((f32[200,128]{1,0:T(8,128)S(1)}, f32[200,128]{1,0:T(8,128)S(1)}, u32[]{:S(2)}, u32[]{:S(2)}) %collective-permute-start.9) | collective-permute-done | bytes 102432 | tf_op jit(solution)/shard_map/ppermute | solution.py:526
  47.5 0.0 collective-permute-start.13
  47.5 0.0 collective-permute-done.10.mine_1
  47.6 0.5 collective-permute-start.14
  48.1 0.0 collective-permute-done.11.mine_2
  48.1 1.0 %collective-permute-start.15 = (f32[200,128]{1,0:T(8,128)S(1)}, f32[200,128]{1,0:T(8,128)S(1)}, u32[]{:S(2)}, u32[]{:S(2)}) collective-permute-start(f32[200,128]{1,0:T(8,128)S(1)} %collective-permute-done.11.mine_2), channel_id=1, source_target_pairs={{0,8},{8,0},{1,9},{9,1},{2,10},{10,2},{3,11},{11,3},{4,12},{12,4},... | collective-permute-start | bytes 307208 | tf_op jit(solution)/shard_map/ppermute | solution.py:518
  49.1 0.0 collective-permute-done.12.mine_3
  49.1 0.0 collective-permute-start.16
  49.1 0.0 collective-permute-done.13.other_0
  49.1 0.0 collective-permute-done.14.other_1
  49.1 0.9 %collective-permute-done.15.other_2 = f32[200,128]{1,0:T(8,128)S(1)} collective-permute-done((f32[200,128]{1,0:T(8,128)S(1)}, f32[200,128]{1,0:T(8,128)S(1)}, u32[]{:S(2)}, u32[]{:S(2)}) %collective-permute-start.15) | collective-permute-done | bytes 102432 | tf_op jit(solution)/shard_map/ppermute | solution.py:518
  50.0 0.4 collective-permute-done.16.other_3
  50.4 1.3 %shard_map.33 = f32[2,192,256]{2,1,0:T(8,128)} custom-call(f32[200,128]{1,0:T(8,128)S(1)} %get-tuple-element.32.own_block, f32[200,128]{1,0:T(8,128)S(1)} %collective-permute-done.9.mine_0, f32[200,128]{1,0:T(8,128)S(1)} %collective-permute-done.10.mine_1, f32[200,128]{1,0:T(8,128)S(1)} %collective-permute-done.11.mine_2, ...), custom_call_target="tpu_custom_call" | custom-call | tf_op jit(solution)/shard_map/pallas_call | solution.py:507
Async XLA Ops:
  0.0 1.0 %copy-start = (f32[2,192,256]{2,1,0:T(8,128)S(1)}, f32[2,192,256]{2,1,0:T(8,128)}, u32[]{:S(2)}) copy-start(f32[2,192,256]{2,1,0:T(8,128)} %field.2) | copy-start | bytes 1179652
  1.0 1.0 %copy-start.1 = (f32[2,192,256]{2,1,0:T(8,128)S(1)}, f32[2,192,256]{2,1,0:T(8,128)}, u32[]{:S(2)}) copy-start(f32[2,192,256]{2,1,0:T(8,128)} %field.3) | copy-start | bytes 1179652
  2.8 10.0 %collective-permute-start = (f32[400,128]{1,0:T(8,128)S(1)}, f32[400,128]{1,0:T(8,128)S(1)}, u32[]{:S(2)}, u32[]{:S(2)}) collective-permute-start(f32[400,128]{1,0:T(8,128)S(1)} %get-tuple-element.26), channel_id=1, source_target_pairs={{0,1},{1,0},{2,3},{3,2},{4,5},{5,4},{6,7},{7,6},{8,12},{9,13},{10,... | collective-permute-start | bytes 614408 | tf_op jit(solution)/shard_map/ppermute | solution.py:526
  5.8 17.1 %collective-permute-start.1 = (f32[400,128]{1,0:T(8,128)S(1)}, f32[400,128]{1,0:T(8,128)S(1)}, u32[]{:S(2)}, u32[]{:S(2)}) collective-permute-start(f32[400,128]{1,0:T(8,128)S(1)} %get-tuple-element.27), channel_id=1, source_target_pairs={{0,5},{1,4},{2,7},{3,6},{4,1},{5,0},{6,3},{7,2},{8,10},{9,11},{10,... | collective-permute-start | bytes 614408 | tf_op jit(solution)/shard_map/ppermute | solution.py:526
  8.4 14.5 %collective-permute-start.2 = (f32[400,128]{1,0:T(8,128)S(1)}, f32[400,128]{1,0:T(8,128)S(1)}, u32[]{:S(2)}, u32[]{:S(2)}) collective-permute-start(f32[400,128]{1,0:T(8,128)S(1)} %get-tuple-element.28), channel_id=1, source_target_pairs={{0,3},{1,2},{2,1},{3,0},{4,7},{5,6},{6,5},{7,4},{8,14},{9,15},{10,... | collective-permute-start | bytes 614408 | tf_op jit(solution)/shard_map/ppermute | solution.py:526
  10.9 12.6 %collective-permute-start.3 = (f32[400,128]{1,0:T(8,128)S(1)}, f32[400,128]{1,0:T(8,128)S(1)}, u32[]{:S(2)}, u32[]{:S(2)}) collective-permute-start(f32[400,128]{1,0:T(8,128)S(1)} %get-tuple-element.29), channel_id=1, source_target_pairs={{0,7},{1,6},{2,5},{3,4},{4,3},{5,2},{6,1},{7,0},{16,23},{17,22},{1... | collective-permute-start | bytes 614408 | tf_op jit(solution)/shard_map/ppermute | solution.py:526
  12.8 10.7 %collective-permute-start.4 = (f32[400,128]{1,0:T(8,128)S(1)}, f32[400,128]{1,0:T(8,128)S(1)}, u32[]{:S(2)}, u32[]{:S(2)}) collective-permute-start(f32[400,128]{1,0:T(8,128)S(1)} %collective-permute-done.mine_0), channel_id=1, source_target_pairs={{0,8},{8,0},{1,9},{9,1},{2,10},{10,2},{3,11},{11,3},{4,12},{12,4},... | collective-permute-start | bytes 614408 | tf_op jit(solution)/shard_map/ppermute | solution.py:518
  22.9 1.5 %collective-permute-start.5 = (f32[400,128]{1,0:T(8,128)S(1)}, f32[400,128]{1,0:T(8,128)S(1)}, u32[]{:S(2)}, u32[]{:S(2)}) collective-permute-start(f32[400,128]{1,0:T(8,128)S(1)} %collective-permute-done.1.mine_1), channel_id=1, source_target_pairs={{0,8},{8,0},{1,9},{9,1},{2,10},{10,2},{3,11},{11,3},{4,12},{12,4},... | collective-permute-start | bytes 614408 | tf_op jit(solution)/shard_map/ppermute | solution.py:518
  22.9 1.7 %collective-permute-start.6 = (f32[400,128]{1,0:T(8,128)S(1)}, f32[400,128]{1,0:T(8,128)S(1)}, u32[]{:S(2)}, u32[]{:S(2)}) collective-permute-start(f32[400,128]{1,0:T(8,128)S(1)} %collective-permute-done.2.mine_2), channel_id=1, source_target_pairs={{0,8},{8,0},{1,9},{9,1},{2,10},{10,2},{3,11},{11,3},{4,12},{12,4},... | collective-permute-start | bytes 614408 | tf_op jit(solution)/shard_map/ppermute | solution.py:518
  23.4 1.5 %collective-permute-start.7 = (f32[400,128]{1,0:T(8,128)S(1)}, f32[400,128]{1,0:T(8,128)S(1)}, u32[]{:S(2)}, u32[]{:S(2)}) collective-permute-start(f32[400,128]{1,0:T(8,128)S(1)} %collective-permute-done.3.mine_3), channel_id=1, source_target_pairs={{0,8},{8,0},{1,9},{9,1},{2,10},{10,2},{3,11},{11,3},{4,12},{12,4},... | collective-permute-start | bytes 614408 | tf_op jit(solution)/shard_map/ppermute | solution.py:518
  31.9 2.2 %collective-permute-start.8 = (f32[5,120,128]{2,1,0:T(8,128)S(1)}, f32[5,120,128]{2,1,0:T(8,128)S(1)}, u32[]{:S(2)}, u32[]{:S(2)}) collective-permute-start(f32[5,120,128]{2,1,0:T(8,128)S(1)} %get-tuple-element.31), channel_id=1, source_target_pairs={{0,8},{8,0},{1,9},{9,1},{2,10},{10,2},{3,11},{11,3},{4,12},{12,4},... | collective-permute-start | bytes 921608 | tf_op jit(solution)/shard_map/ppermute | solution.py:518
  34.2 13.3 %collective-permute-start.9 = (f32[200,128]{1,0:T(8,128)S(1)}, f32[200,128]{1,0:T(8,128)S(1)}, u32[]{:S(2)}, u32[]{:S(2)}) collective-permute-start(f32[200,128]{1,0:T(8,128)S(1)} %get-tuple-element.33), channel_id=1, source_target_pairs={{0,4},{1,5},{2,6},{3,7},{4,0},{5,1},{6,2},{7,3},{8,13},{9,12},{10,... | collective-permute-start | bytes 307208 | tf_op jit(solution)/shard_map/ppermute | solution.py:526
  39.4 8.1 %collective-permute-start.10 = (f32[200,128]{1,0:T(8,128)S(1)}, f32[200,128]{1,0:T(8,128)S(1)}, u32[]{:S(2)}, u32[]{:S(2)}) collective-permute-start(f32[200,128]{1,0:T(8,128)S(1)} %get-tuple-element.34), channel_id=1, source_target_pairs={{0,6},{1,7},{2,4},{3,5},{4,2},{5,3},{6,0},{7,1},{8,15},{9,14},{10,... | collective-permute-start | bytes 307208 | tf_op jit(solution)/shard_map/ppermute | solution.py:526
  39.8 8.3 %collective-permute-start.11 = (f32[200,128]{1,0:T(8,128)S(1)}, f32[200,128]{1,0:T(8,128)S(1)}, u32[]{:S(2)}, u32[]{:S(2)}) collective-permute-start(f32[200,128]{1,0:T(8,128)S(1)} %get-tuple-element.35), channel_id=1, source_target_pairs={{0,1},{1,0},{2,3},{3,2},{4,5},{5,4},{6,7},{7,6},{8,10},{9,11},{10,... | collective-permute-start | bytes 307208 | tf_op jit(solution)/shard_map/ppermute | solution.py:526
  40.4 8.6 %collective-permute-start.12 = (f32[200,128]{1,0:T(8,128)S(1)}, f32[200,128]{1,0:T(8,128)S(1)}, u32[]{:S(2)}, u32[]{:S(2)}) collective-permute-start(f32[200,128]{1,0:T(8,128)S(1)} %get-tuple-element.36), channel_id=1, source_target_pairs={{0,3},{1,2},{2,1},{3,0},{4,7},{5,6},{6,5},{7,4},{16,19},{17,18},{1... | collective-permute-start | bytes 307208 | tf_op jit(solution)/shard_map/ppermute | solution.py:526
  47.5 1.5 %collective-permute-start.13 = (f32[200,128]{1,0:T(8,128)S(1)}, f32[200,128]{1,0:T(8,128)S(1)}, u32[]{:S(2)}, u32[]{:S(2)}) collective-permute-start(f32[200,128]{1,0:T(8,128)S(1)} %collective-permute-done.9.mine_0), channel_id=1, source_target_pairs={{0,8},{8,0},{1,9},{9,1},{2,10},{10,2},{3,11},{11,3},{4,12},{12,4},... | collective-permute-start | bytes 307208 | tf_op jit(solution)/shard_map/ppermute | solution.py:518
  47.6 1.5 %collective-permute-start.14 = (f32[200,128]{1,0:T(8,128)S(1)}, f32[200,128]{1,0:T(8,128)S(1)}, u32[]{:S(2)}, u32[]{:S(2)}) collective-permute-start(f32[200,128]{1,0:T(8,128)S(1)} %collective-permute-done.10.mine_1), channel_id=1, source_target_pairs={{0,8},{8,0},{1,9},{9,1},{2,10},{10,2},{3,11},{11,3},{4,12},{12,4},... | collective-permute-start | bytes 307208 | tf_op jit(solution)/shard_map/ppermute | solution.py:518
  48.1 2.0 %collective-permute-start.15 = (f32[200,128]{1,0:T(8,128)S(1)}, f32[200,128]{1,0:T(8,128)S(1)}, u32[]{:S(2)}, u32[]{:S(2)}) collective-permute-start(f32[200,128]{1,0:T(8,128)S(1)} %collective-permute-done.11.mine_2), channel_id=1, source_target_pairs={{0,8},{8,0},{1,9},{9,1},{2,10},{10,2},{3,11},{11,3},{4,12},{12,4},... | collective-permute-start | bytes 307208 | tf_op jit(solution)/shard_map/ppermute | solution.py:518
  49.1 1.3 %collective-permute-start.16 = (f32[200,128]{1,0:T(8,128)S(1)}, f32[200,128]{1,0:T(8,128)S(1)}, u32[]{:S(2)}, u32[]{:S(2)}) collective-permute-start(f32[200,128]{1,0:T(8,128)S(1)} %collective-permute-done.12.mine_3), channel_id=1, source_target_pairs={{0,8},{8,0},{1,9},{9,1},{2,10},{10,2},{3,11},{11,3},{4,12},{12,4},... | collective-permute-start | bytes 307208 | tf_op jit(solution)/shard_map/ppermute | solution.py:518

commit v7 on v6

--- a/solution.py
+++ b/solution.py
@@ -143,8 +143,9 @@
 LANES = 128
 PAD = 8
 SPILL_TURNS = (0, 4, 8)
-WAY_IN = ((1, 4), (5, 2), (3, 6), (7, 0))
-WAY_OUT = ((4, 5), (6, 7), (1, 2), (3, 0))
+WAY_IN = ((1, 4), (5, 2), (3, 6), (7, 7))
+WAY_OUT = ((5, 7), (6, 1), (2, 3), (4, 4))
+JOIN_COST = pl.CostEstimate(flops=10**10, bytes_accessed=10**7, transcendentals=0)
 EDGE_ROWS = 16
 FINE_CHUNKS = ((0, 16), (32, 16), (16, 16))
 HALF_CHUNKS = ((0, 16), (32, 16), (16, 16))
@@ -263,9 +264,16 @@
     for dest, block in zip(served(WAY_IN), blocks):
         back = (8 - 16 * dest) & (LANES - 1)
         quarter = ((iota((rows, LANES), 1) + back) & (LANES - 1)) >> 5
-        for n in range(8):
-            turned = (initial_turned, reaction_turned)[n // 4]
-            x = [turned[(4 * (n % 4) + j) * rows : (4 * (n % 4) + j + 1) * rows, :] for j in range(4)]
+        short = block.shape[0] < 8 * rows
+        for n in range(4 if short else 8):
+
+            def read(j, n=n):
+                at = slice((4 * (n % 4) + j) * rows, (4 * (n % 4) + j + 1) * rows)
+                if short:
+                    return jnp.where(lax.axis_index("tm") == 0, initial_turned[at, :], reaction_turned[at, :])
+                return (initial_turned, reaction_turned)[n // 4][at, :]
+
+            x = [read(j) for j in range(4)]
             x = jnp.where(quarter == 0, x[0], jnp.where(quarter == 1, x[1], jnp.where(quarter == 2, x[2], x[3])))
             block[n * rows : (n + 1) * rows, :] = pltpu.roll(x, back, 1)
         back = (-16 * dest) & (LANES - 1)
@@ -276,7 +284,7 @@
                 edges = (initial_edges, reaction_edges)[n // 2]
                 at = (2 * g + n % 2) * EDGE_ROWS
                 x = jnp.where(slot == 16 * (g // 3) + 4 * (g % 3) + n, edges[at : at + EDGE_ROWS, :], x)
-        block[8 * rows : 8 * rows + EDGE_ROWS, :] = pltpu.roll(x, back, 1)
+        block[block.shape[0] - EDGE_ROWS :, :] = pltpu.roll(x, back, 1)
 
 
 def march_kernel(
@@ -306,13 +314,16 @@
     for masks, mine, other in zip(WAY_IN, (mine_0, mine_1, mine_2), (other_0, other_1, other_2)):
         blocks.append((mine, None, sent_to(masks)))
         blocks.append((other, None, sent_to(masks[::-1])))
-    blocks.append((mine_3, other_3, space ^ WAY_IN[3][0]))
+    blocks.append((mine_3, other_3, space ^ WAY_IN[-1][0]))
     for number, (block, if_second, k) in enumerate(blocks):
 
         def read(first, size, block=block, if_second=if_second):
             if if_second is None:
                 return block[first : first + size, :]
-            return jnp.where(tm == 0, block[first : first + size, :], if_second[first : first + size, :])
+            if first < 4 * rows:
+                return jnp.where(tm == 0, block[first : first + size, :], if_second[first : first + size, :])
+            first -= 4 * rows
+            return jnp.where(tm == 0, if_second[first : first + size, :], block[first : first + size, :])
 
         totals = []
         for n in range(2):
@@ -411,37 +422,45 @@
     for n, (dest, block) in enumerate(zip(served(WAY_OUT), blocks)):
         kept, came = mine[dest, 2 * rows :, :], other[n, 2 * rows :, :]
         change, first = jnp.where(tm == 0, kept, came), jnp.where(tm == 0, came, kept)
+        short = block.shape[0] < 4 * rows
+        if short:
+            change, first = jnp.where(tm == 0, 0.0, came), came
         h = [jnp.where(own, x, roll(x, 16)) for x in (first, change)]
         for e in range(2):
             for odd in range(2):
                 at = pl.ds(e * rows + odd, part, 2)
                 to = pl.ds((2 + e) * rows + odd, part, 2)
-                kept, came = mine[dest, at, :], other[n, at, :]
-                block[at, :] = (h[0] + jnp.where(tm == 0, kept, came)) - h[0]
-                block[to, :] = h[1] + jnp.where(tm == 0, came, kept)
+                if short:
+                    block[at, :] = (h[0] + mine[dest, at, :]) - jnp.where(tm == 0, h[0], 0.0)
+                else:
+                    kept, came = mine[dest, at, :], other[n, at, :]
+                    block[at, :] = (h[0] + jnp.where(tm == 0, kept, came)) - h[0]
+                    block[to, :] = h[1] + jnp.where(tm == 0, came, kept)
         packed = None
         for g, by in enumerate(SPILL_TURNS):
             piece = roll(jnp.where(spill, change[8 * g : 8 * g + 8], 0.0), by)
             packed = piece if packed is None else packed + piece
-        block[4 * rows : 4 * rows + 8, :] = packed
-
-
-def unpack_kernel(own_block, mine_0, mine_1, mine_2, mine_3, other_0, other_1, other_2, other_3, out_hbm, strips, spilled, turned, halves, out, left):
+        block[block.shape[0] - 8 :, :] = packed
+
+
+def join_kernel(own_block, last_block, both):
+    both[0] = own_block[...]
+    both[1] = last_block[...]
+
+
+def unpack_kernel(both, mine_0, mine_1, mine_2, other_0, other_1, other_2, out_hbm, strips, spilled, turned, halves, out, left):
     tm, space = lax.axis_index("tm"), lax.axis_index("space")
     count = strips.shape[0]
     rows = out.shape[1] // 4
     part = rows // 2
-    blocks = [(own_block, None, space)]
+    strips[space] = both[0]
+    strips[space ^ WAY_OUT[-1][0]] = both[1]
+    blocks = []
     for masks, mine, other in zip(WAY_OUT, (mine_0, mine_1, mine_2), (other_0, other_1, other_2)):
-        blocks.append((mine, None, sent_to(masks)))
-        blocks.append((other, None, sent_to(masks[::-1])))
-    blocks.append((mine_3, other_3, space ^ WAY_OUT[3][0]))
-    for block, if_second, k in blocks:
-        slabs = [block[: 2 * rows, :], block[2 * rows :, :]]
-        if if_second is not None:
-            slabs = [jnp.where(tm == 0, x, y) for x, y in zip(slabs, (if_second[: 2 * rows, :], if_second[2 * rows :, :]))]
-        strips[k, : 2 * rows, :] = jnp.where(tm == 0, slabs[0], slabs[1][: 2 * rows])
-        strips[k, 2 * rows :, :] = jnp.where(tm == 0, 0.0, slabs[1][2 * rows :])
+        blocks += [(mine, sent_to(masks)), (other, sent_to(masks[::-1]))]
+    for block, k in blocks:
+        strips[k, : 2 * rows, :] = jnp.where(tm == 0, block[: 2 * rows, :], block[2 * rows : 4 * rows, :])
+        strips[k, 2 * rows :, :] = jnp.where(tm == 0, 0.0, block[4 * rows :, :])
 
     def lined_up(read, first, size):
         quarter = ((iota((size, LANES), 1) - first) & (LANES - 1)) >> 5
@@ -502,13 +521,14 @@
 VMEM = pl.BlockSpec(memory_space=pltpu.VMEM)
 
 
-def on_core(kernel, inputs, out_shapes, scratch=(), out_spec=VMEM):
+def on_core(kernel, inputs, out_shapes, scratch=(), out_spec=VMEM, cost=None):
     shapes = [jax.ShapeDtypeStruct(s, jnp.float32) for s in out_shapes]
     return pl.pallas_call(
         kernel,
         out_shape=shapes,
         in_specs=[VMEM] * len(inputs),
         out_specs=[out_spec] * len(shapes),
+        cost_estimate=cost,
         scratch_shapes=[pltpu.VMEM(s, jnp.float32) if isinstance(s, tuple) else s for s in scratch],
         compiler_params=pltpu.CompilerParams(vmem_limit_bytes=48 * 1024 * 1024),
     )(*inputs)
@@ -520,11 +540,11 @@
 
 def exchanged(blocks, way):
     count = lax.axis_size("space")
-    mine = []
+    came = []
     for block, masks in zip(blocks, way):
-        pairs = [(t * count + i, t * count + (i ^ masks[t])) for t in range(2) if masks[t] for i in range(count)]
-        mine.append(lax.ppermute(block, ("tm", "space"), pairs))
-    return mine, [swapped(x) for x in mine]
+        pairs = [(t * count + i, t * count + (i ^ masks[t])) for t in range(2) for i in range(count)]
+        came.append(lax.ppermute(block, ("tm", "space"), pairs))
+    return came
 
 
 def strips_local(initial, reaction):
@@ -540,10 +560,11 @@
             functools.partial(prepare_kernel, turns),
             [field],
             [(16 * rows, LANES), (4 * rows, LANES)],
-            [(16 * rows, LANES), (4 * rows, LANES), (2 * rows, LANES)],
+            [(16 * rows, LANES), (4 * rows + PAD, LANES), (2 * rows, LANES)],
         )
-    *blocks, own_block = on_core(fill_kernel, prepared, [block] * 5)
-    mine, other = exchanged(blocks, WAY_IN)
+    *blocks, own_block = on_core(fill_kernel, prepared, [block] * 3 + [(4 * rows + EDGE_ROWS, LANES), block])
+    mine = exchanged(blocks, WAY_IN)
+    other = [swapped(x) for x in mine]
     fine = ((planes + 2) * (rows + 2 * PAD), LANES)
     wide = ((count + 2) * (rows + 2 * PAD), LANES)
     small = ((count + 2) * (part + 2 * PAD), LANES)
@@ -556,15 +577,17 @@
         + [(planes * rows, LANES)] * 2
         + [wide, wide, (count * rows, LANES), small, small]
         + [small_cells] * 2
-        + [(planes * rows, LANES)],
+        + [(planes * rows + PAD, LANES)],
     )
-    *blocks, own_block = on_core(send_kernel, [strip, swapped(given)], [(4 * rows + 8, LANES)] * 5)
-    mine, other = exchanged(blocks, WAY_OUT)
+    *blocks, own_block = on_core(send_kernel, [strip, swapped(given)], [(4 * rows + 8, LANES)] * 3 + [(2 * rows + 8, LANES)] * 2)
+    *mine, last = exchanged(blocks, WAY_OUT)
+    other = [swapped(x) for x in mine]
+    (both,) = on_core(join_kernel, [own_block, last], [(2, 2 * rows + 8, LANES)], cost=JOIN_COST)
     (out,) = on_core(
         unpack_kernel,
-        [own_block, *mine, *other],
+        [both, *mine, *other],
         [initial.shape],
-        [(count, 2 * rows + 8, LANES), (nx, LANES), (nx, LANES), (16 * rows, LANES), initial.shape, pltpu.SemaphoreType.DMA((2,))],
+        [(count, 2 * rows + 8, LANES), (nx + PAD, LANES), (nx, LANES), (16 * rows, LANES), initial.shape, pltpu.SemaphoreType.DMA((2,))],
         pl.BlockSpec(memory_space=pltpu.HBM),
     )
     return out[None]

time: 51.9 us -> 49.7 us (0.958)
  waiting for transfers between devices: 16.3 us -> 15.1 us
  starting transfers between devices: 24.1 us -> 23.2 us
    ppermute x8, starting transfers between devices: 19.2 us -> 17.5 us  [exchanged(): came.append(lax.ppermute(block, ('tm', 'space'), pairs))]
    ppermute x9 -> x8, waiting for transfers between devices: 3.97 us -> 2.55 us  [swapped(): return lax.ppermute(x, 'tm', [(0, 1), (1, 0)])]
    ppermute x9 -> x8, starting transfers between devices: 4.97 us -> 5.72 us  [swapped(): return lax.ppermute(x, 'tm', [(0, 1), (1, 0)])]
    pallas_call x6 -> x7, Pallas kernels: 9.6 us -> 9.57 us  [on_core(): pl.pallas_call(kernel, out_shape=shapes, in_specs=[VMEM] * len(inputs), o...]
  transfers between devices with their start and end apart: 17 -> 16, of which waited for: 8 -> 7; matrix products, arithmetic and copies ran while one was open for 0% -> 0% of each run, Pallas kernels for 0% -> 0%
where the time goes in v7:
time: 49.7 us; the launch traced here: 49.5 us
  starting transfers between devices  23.2 us (47%)
  waiting for transfers between devices  15.1 us (30%)
  Pallas kernels  9.57 us (19%)
  local copies, waits for them, and re-layouts  1.56 us (3%)
    ppermute x8, starting transfers between devices, exchanged(): came.append(lax.ppermute(block, ('tm', 'space'), pairs))  17.5 us
    ppermute x8, waiting for transfers between devices, exchanged(): came.append(lax.ppermute(block, ('tm', 'space'), pairs))  12.5 us
    pallas_call x7, Pallas kernels, on_core(): pl.pallas_call(kernel, out_shape=shapes, in_specs=[VMEM] * len(inputs), o...  9.57 us
    ppermute x8, starting transfers between devices, swapped(): return lax.ppermute(x, 'tm', [(0, 1), (1, 0)])  5.72 us
    ppermute x8, waiting for transfers between devices, swapped(): return lax.ppermute(x, 'tm', [(0, 1), (1, 0)])  2.55 us
    unnamed x4, local copies, waits for them, and re-layouts  1.56 us
  transfers between devices with their start and end apart: 16, of which 7 were waited for; matrix products, arithmetic and copies ran while one was open for 0% of the time, Pallas kernels for 0%

profile of v7, /device:TPU:0, one launch (start us, length us, event | category | flops | bytes accessed | tf_op | source)
XLA Modules:
  0.0 49.5 jit_solution(5293576214231840574)
XLA Ops:
  0.0 0.0 copy-start
  0.0 1.0 %copy-done = f32[2,192,256]{2,1,0:T(8,128)S(1)} copy-done((f32[2,192,256]{2,1,0:T(8,128)S(1)}, f32[2,192,256]{2,1,0:T(8,128)}, u32[]{:S(2)}) %copy-start) | copy-done | bytes 393240
  1.0 0.0 copy-start.1
  1.0 0.4 shard_map.28
  1.4 0.6 %copy-done.1 = f32[2,192,256]{2,1,0:T(8,128)S(1)} copy-done((f32[2,192,256]{2,1,0:T(8,128)S(1)}, f32[2,192,256]{2,1,0:T(8,128)}, u32[]{:S(2)}) %copy-start.1) | copy-done | bytes 393240
  2.0 0.4 shard_map.29
  2.4 0.4 shard_map.30
  2.8 3.0 %collective-permute-start = (f32[400,128]{1,0:T(8,128)S(1)}, f32[400,128]{1,0:T(8,128)S(1)}, u32[]{:S(2)}, u32[]{:S(2)}) collective-permute-start(f32[400,128]{1,0:T(8,128)S(1)} %get-tuple-element.26), channel_id=1, source_target_pairs={{0,1},{1,0},{2,3},{3,2},{4,5},{5,4},{6,7},{7,6},{8,12},{9,13},{10,... | collective-permute-start | bytes 614408 | tf_op jit(solution)/shard_map/ppermute | solution.py:546
  5.8 2.6 %collective-permute-start.1 = (f32[400,128]{1,0:T(8,128)S(1)}, f32[400,128]{1,0:T(8,128)S(1)}, u32[]{:S(2)}, u32[]{:S(2)}) collective-permute-start(f32[400,128]{1,0:T(8,128)S(1)} %get-tuple-element.27), channel_id=1, source_target_pairs={{0,5},{1,4},{2,7},{3,6},{4,1},{5,0},{6,3},{7,2},{8,10},{9,11},{10,... | collective-permute-start | bytes 614408 | tf_op jit(solution)/shard_map/ppermute | solution.py:546
  8.4 2.5 %collective-permute-start.2 = (f32[400,128]{1,0:T(8,128)S(1)}, f32[400,128]{1,0:T(8,128)S(1)}, u32[]{:S(2)}, u32[]{:S(2)}) collective-permute-start(f32[400,128]{1,0:T(8,128)S(1)} %get-tuple-element.28), channel_id=1, source_target_pairs={{0,3},{1,2},{2,1},{3,0},{4,7},{5,6},{6,5},{7,4},{8,14},{9,15},{10,... | collective-permute-start | bytes 614408 | tf_op jit(solution)/shard_map/ppermute | solution.py:546
  10.9 0.0 collective-permute-start.3
  10.9 0.0 collective-permute-done.mine_0
  10.9 3.8 %collective-permute-start.4 = (f32[400,128]{1,0:T(8,128)S(1)}, f32[400,128]{1,0:T(8,128)S(1)}, u32[]{:S(2)}, u32[]{:S(2)}) collective-permute-start(f32[400,128]{1,0:T(8,128)S(1)} %collective-permute-done.mine_0), channel_id=1, source_target_pairs={{0,8},{8,0},{1,9},{9,1},{2,10},{10,2},{3,11},{11,3},{4,12},{12,4},... | collective-permute-start | bytes 614408 | tf_op jit(solution)/shard_map/ppermute | solution.py:538
  14.7 8.3 %collective-permute-done.1.mine_1 = f32[400,128]{1,0:T(8,128)S(1)} collective-permute-done((f32[400,128]{1,0:T(8,128)S(1)}, f32[400,128]{1,0:T(8,128)S(1)}, u32[]{:S(2)}, u32[]{:S(2)}) %collective-permute-start.1) | collective-permute-done | bytes 204832 | tf_op jit(solution)/shard_map/ppermute | solution.py:546
  23.0 0.0 collective-permute-start.5
  23.0 0.0 collective-permute-done.2.mine_2
  23.0 0.5 %collective-permute-start.6 = (f32[400,128]{1,0:T(8,128)S(1)}, f32[400,128]{1,0:T(8,128)S(1)}, u32[]{:S(2)}, u32[]{:S(2)}) collective-permute-start(f32[400,128]{1,0:T(8,128)S(1)} %collective-permute-done.2.mine_2), channel_id=1, source_target_pairs={{0,8},{8,0},{1,9},{9,1},{2,10},{10,2},{3,11},{11,3},{4,12},{12,4},... | collective-permute-start | bytes 614408 | tf_op jit(solution)/shard_map/ppermute | solution.py:538
  23.5 0.0 collective-permute-done.3.mine_3
  23.5 0.1 collective-permute-start.7
  23.6 1.3 %collective-permute-done.7.other_3 = f32[208,128]{1,0:T(8,128)S(1)} collective-permute-done((f32[208,128]{1,0:T(8,128)S(1)}, f32[208,128]{1,0:T(8,128)S(1)}, u32[]{:S(2)}, u32[]{:S(2)}) %collective-permute-start.7) | collective-permute-done | bytes 106528 | tf_op jit(solution)/shard_map/ppermute | solution.py:538
  24.9 0.0 collective-permute-done.4.other_0
  24.9 0.0 collective-permute-done.5.other_1
  24.9 0.0 collective-permute-done.6.other_2
  24.9 6.9 %shard_map.31 = (f32[8,120,128]{2,1,0:T(8,128)S(1)}, f32[5,120,128]{2,1,0:T(8,128)S(1)}) custom-call(f32[400,128]{1,0:T(8,128)S(1)} %get-tuple-element.25.own_block, f32[400,128]{1,0:T(8,128)S(1)} %collective-permute-done.mine_0, f32[400,128]{1,0:T(8,128)S(1)} %collective-permute-done.1.mine_1, f32[400,128]{1,0:T(8,128)S(1)} %collective-permute-done.2.mine_2, ...), custom_call_target="tpu_custom_call" | custom-call | tf_op jit(solution)/shard_map/pallas_call | solution.py:526
  31.9 1.0 %collective-permute-start.8 = (f32[5,120,128]{2,1,0:T(8,128)S(1)}, f32[5,120,128]{2,1,0:T(8,128)S(1)}, u32[]{:S(2)}, u32[]{:S(2)}) collective-permute-start(f32[5,120,128]{2,1,0:T(8,128)S(1)} %get-tuple-element.31), channel_id=1, source_target_pairs={{0,8},{8,0},{1,9},{9,1},{2,10},{10,2},{3,11},{11,3},{4,12},{12,4},... | collective-permute-start | bytes 921608 | tf_op jit(solution)/shard_map/ppermute | solution.py:538
  32.8 1.2 %collective-permute-done.8.other = f32[5,120,128]{2,1,0:T(8,128)S(1)} collective-permute-done((f32[5,120,128]{2,1,0:T(8,128)S(1)}, f32[5,120,128]{2,1,0:T(8,128)S(1)}, u32[]{:S(2)}, u32[]{:S(2)}) %collective-permute-start.8) | collective-permute-done | bytes 307232 | tf_op jit(solution)/shard_map/ppermute | solution.py:538
  34.1 0.1 shard_map.32
  34.2 5.0 %collective-permute-start.10 = (f32[200,128]{1,0:T(8,128)S(1)}, f32[200,128]{1,0:T(8,128)S(1)}, u32[]{:S(2)}, u32[]{:S(2)}) collective-permute-start(f32[200,128]{1,0:T(8,128)S(1)} %get-tuple-element.34), channel_id=1, source_target_pairs={{0,5},{1,4},{2,7},{3,6},{4,1},{5,0},{6,3},{7,2},{8,15},{9,14},{10,... | collective-permute-start | bytes 307208 | tf_op jit(solution)/shard_map/ppermute | solution.py:546
  39.2 0.7 %collective-permute-start.11 = (f32[200,128]{1,0:T(8,128)S(1)}, f32[200,128]{1,0:T(8,128)S(1)}, u32[]{:S(2)}, u32[]{:S(2)}) collective-permute-start(f32[200,128]{1,0:T(8,128)S(1)} %get-tuple-element.35), channel_id=1, source_target_pairs={{0,6},{1,7},{2,4},{3,5},{4,2},{5,3},{6,0},{7,1},{8,9},{9,8},{10,11... | collective-permute-start | bytes 307208 | tf_op jit(solution)/shard_map/ppermute | solution.py:546
  39.9 0.0 collective-permute-start.12
  39.9 3.7 %collective-permute-start.9 = (f32[104,128]{1,0:T(8,128)S(1)}, f32[104,128]{1,0:T(8,128)S(1)}, u32[]{:S(2)}, u32[]{:S(2)}) collective-permute-start(f32[104,128]{1,0:T(8,128)S(1)} %get-tuple-element.33), channel_id=1, source_target_pairs={{0,4},{1,5},{2,6},{3,7},{4,0},{5,1},{6,2},{7,3},{8,12},{9,13},{10,... | collective-permute-start | bytes 159752 | tf_op jit(solution)/shard_map/ppermute | solution.py:546
  43.6 1.4 %collective-permute-done.10.mine_0 = f32[200,128]{1,0:T(8,128)S(1)} collective-permute-done((f32[200,128]{1,0:T(8,128)S(1)}, f32[200,128]{1,0:T(8,128)S(1)}, u32[]{:S(2)}, u32[]{:S(2)}) %collective-permute-start.10) | collective-permute-done | bytes 102432 | tf_op jit(solution)/shard_map/ppermute | solution.py:546
  45.0 0.0 collective-permute-start.13
  45.0 0.8 %collective-permute-done.11.mine_1 = f32[200,128]{1,0:T(8,128)S(1)} collective-permute-done((f32[200,128]{1,0:T(8,128)S(1)}, f32[200,128]{1,0:T(8,128)S(1)}, u32[]{:S(2)}, u32[]{:S(2)}) %collective-permute-start.11) | collective-permute-done | bytes 102432 | tf_op jit(solution)/shard_map/ppermute | solution.py:546
  45.8 0.0 collective-permute-start.14
  45.8 0.2 collective-permute-done.12.mine_2
  46.0 0.4 collective-permute-start.15
  46.3 1.8 %collective-permute-done.9.last_block = f32[104,128]{1,0:T(8,128)S(1)} collective-permute-done((f32[104,128]{1,0:T(8,128)S(1)}, f32[104,128]{1,0:T(8,128)S(1)}, u32[]{:S(2)}, u32[]{:S(2)}) %collective-permute-start.9) | collective-permute-done | bytes 53280 | tf_op jit(solution)/shard_map/ppermute | solution.py:546
  48.2 0.0 collective-permute-done.13.other_0
  48.2 0.0 collective-permute-done.14.other_1
  48.2 0.0 collective-permute-done.15.other_2
  48.2 1.3 %shard_map.34 = f32[2,192,256]{2,1,0:T(8,128)} custom-call(f32[2,104,128]{2,1,0:T(8,128)S(1)} %shard_map.33.both, f32[200,128]{1,0:T(8,128)S(1)} %collective-permute-done.10.mine_0, f32[200,128]{1,0:T(8,128)S(1)} %collective-permute-done.11.mine_1, f32[200,128]{1,0:T(8,128)S(1)} %collective-permute-done.12.mine_2, ...), custom_call_target="tpu_custom_call" | custom-call | tf_op jit(solution)/shard_map/pallas_call | solution.py:526
  (1 shorter events, 0.0 us)
Async XLA Ops:
  0.0 1.0 %copy-start = (f32[2,192,256]{2,1,0:T(8,128)S(1)}, f32[2,192,256]{2,1,0:T(8,128)}, u32[]{:S(2)}) copy-start(f32[2,192,256]{2,1,0:T(8,128)} %field.2) | copy-start | bytes 1179652
  1.0 1.0 %copy-start.1 = (f32[2,192,256]{2,1,0:T(8,128)S(1)}, f32[2,192,256]{2,1,0:T(8,128)}, u32[]{:S(2)}) copy-start(f32[2,192,256]{2,1,0:T(8,128)} %field.3) | copy-start | bytes 1179652
  2.8 8.1 %collective-permute-start = (f32[400,128]{1,0:T(8,128)S(1)}, f32[400,128]{1,0:T(8,128)S(1)}, u32[]{:S(2)}, u32[]{:S(2)}) collective-permute-start(f32[400,128]{1,0:T(8,128)S(1)} %get-tuple-element.26), channel_id=1, source_target_pairs={{0,1},{1,0},{2,3},{3,2},{4,5},{5,4},{6,7},{7,6},{8,12},{9,13},{10,... | collective-permute-start | bytes 614408 | tf_op jit(solution)/shard_map/ppermute | solution.py:546
  5.8 17.2 %collective-permute-start.1 = (f32[400,128]{1,0:T(8,128)S(1)}, f32[400,128]{1,0:T(8,128)S(1)}, u32[]{:S(2)}, u32[]{:S(2)}) collective-permute-start(f32[400,128]{1,0:T(8,128)S(1)} %get-tuple-element.27), channel_id=1, source_target_pairs={{0,5},{1,4},{2,7},{3,6},{4,1},{5,0},{6,3},{7,2},{8,10},{9,11},{10,... | collective-permute-start | bytes 614408 | tf_op jit(solution)/shard_map/ppermute | solution.py:546
  8.4 14.6 %collective-permute-start.2 = (f32[400,128]{1,0:T(8,128)S(1)}, f32[400,128]{1,0:T(8,128)S(1)}, u32[]{:S(2)}, u32[]{:S(2)}) collective-permute-start(f32[400,128]{1,0:T(8,128)S(1)} %get-tuple-element.28), channel_id=1, source_target_pairs={{0,3},{1,2},{2,1},{3,0},{4,7},{5,6},{6,5},{7,4},{8,14},{9,15},{10,... | collective-permute-start | bytes 614408 | tf_op jit(solution)/shard_map/ppermute | solution.py:546
  10.9 12.6 %collective-permute-start.3 = (f32[208,128]{1,0:T(8,128)S(1)}, f32[208,128]{1,0:T(8,128)S(1)}, u32[]{:S(2)}, u32[]{:S(2)}) collective-permute-start(f32[208,128]{1,0:T(8,128)S(1)} %get-tuple-element.29), channel_id=1, source_target_pairs={{0,7},{1,6},{2,5},{3,4},{4,3},{5,2},{6,1},{7,0},{8,15},{9,14},{10,... | collective-permute-start | bytes 319496 | tf_op jit(solution)/shard_map/ppermute | solution.py:546
  10.9 14.0 %collective-permute-start.4 = (f32[400,128]{1,0:T(8,128)S(1)}, f32[400,128]{1,0:T(8,128)S(1)}, u32[]{:S(2)}, u32[]{:S(2)}) collective-permute-start(f32[400,128]{1,0:T(8,128)S(1)} %collective-permute-done.mine_0), channel_id=1, source_target_pairs={{0,8},{8,0},{1,9},{9,1},{2,10},{10,2},{3,11},{11,3},{4,12},{12,4},... | collective-permute-start | bytes 614408 | tf_op jit(solution)/shard_map/ppermute | solution.py:538
  23.0 1.9 %collective-permute-start.5 = (f32[400,128]{1,0:T(8,128)S(1)}, f32[400,128]{1,0:T(8,128)S(1)}, u32[]{:S(2)}, u32[]{:S(2)}) collective-permute-start(f32[400,128]{1,0:T(8,128)S(1)} %collective-permute-done.1.mine_1), channel_id=1, source_target_pairs={{0,8},{8,0},{1,9},{9,1},{2,10},{10,2},{3,11},{11,3},{4,12},{12,4},... | collective-permute-start | bytes 614408 | tf_op jit(solution)/shard_map/ppermute | solution.py:538
  23.0 1.9 %collective-permute-start.6 = (f32[400,128]{1,0:T(8,128)S(1)}, f32[400,128]{1,0:T(8,128)S(1)}, u32[]{:S(2)}, u32[]{:S(2)}) collective-permute-start(f32[400,128]{1,0:T(8,128)S(1)} %collective-permute-done.2.mine_2), channel_id=1, source_target_pairs={{0,8},{8,0},{1,9},{9,1},{2,10},{10,2},{3,11},{11,3},{4,12},{12,4},... | collective-permute-start | bytes 614408 | tf_op jit(solution)/shard_map/ppermute | solution.py:538
  23.5 1.4 %collective-permute-start.7 = (f32[208,128]{1,0:T(8,128)S(1)}, f32[208,128]{1,0:T(8,128)S(1)}, u32[]{:S(2)}, u32[]{:S(2)}) collective-permute-start(f32[208,128]{1,0:T(8,128)S(1)} %collective-permute-done.3.mine_3), channel_id=1, source_target_pairs={{0,8},{8,0},{1,9},{9,1},{2,10},{10,2},{3,11},{11,3},{4,12},{12,4},... | collective-permute-start | bytes 319496 | tf_op jit(solution)/shard_map/ppermute | solution.py:538
  31.9 2.2 %collective-permute-start.8 = (f32[5,120,128]{2,1,0:T(8,128)S(1)}, f32[5,120,128]{2,1,0:T(8,128)S(1)}, u32[]{:S(2)}, u32[]{:S(2)}) collective-permute-start(f32[5,120,128]{2,1,0:T(8,128)S(1)} %get-tuple-element.31), channel_id=1, source_target_pairs={{0,8},{8,0},{1,9},{9,1},{2,10},{10,2},{3,11},{11,3},{4,12},{12,4},... | collective-permute-start | bytes 921608 | tf_op jit(solution)/shard_map/ppermute | solution.py:538
  34.2 10.8 %collective-permute-start.10 = (f32[200,128]{1,0:T(8,128)S(1)}, f32[200,128]{1,0:T(8,128)S(1)}, u32[]{:S(2)}, u32[]{:S(2)}) collective-permute-start(f32[200,128]{1,0:T(8,128)S(1)} %get-tuple-element.34), channel_id=1, source_target_pairs={{0,5},{1,4},{2,7},{3,6},{4,1},{5,0},{6,3},{7,2},{8,15},{9,14},{10,... | collective-permute-start | bytes 307208 | tf_op jit(solution)/shard_map/ppermute | solution.py:546
  39.2 6.6 %collective-permute-start.11 = (f32[200,128]{1,0:T(8,128)S(1)}, f32[200,128]{1,0:T(8,128)S(1)}, u32[]{:S(2)}, u32[]{:S(2)}) collective-permute-start(f32[200,128]{1,0:T(8,128)S(1)} %get-tuple-element.35), channel_id=1, source_target_pairs={{0,6},{1,7},{2,4},{3,5},{4,2},{5,3},{6,0},{7,1},{8,9},{9,8},{10,11... | collective-permute-start | bytes 307208 | tf_op jit(solution)/shard_map/ppermute | solution.py:546
  39.9 6.1 %collective-permute-start.12 = (f32[200,128]{1,0:T(8,128)S(1)}, f32[200,128]{1,0:T(8,128)S(1)}, u32[]{:S(2)}, u32[]{:S(2)}) collective-permute-start(f32[200,128]{1,0:T(8,128)S(1)} %get-tuple-element.36), channel_id=1, source_target_pairs={{0,2},{1,3},{2,0},{3,1},{4,6},{5,7},{6,4},{7,5},{8,11},{9,10},{10,... | collective-permute-start | bytes 307208 | tf_op jit(solution)/shard_map/ppermute | solution.py:546
  39.9 8.2 %collective-permute-start.9 = (f32[104,128]{1,0:T(8,128)S(1)}, f32[104,128]{1,0:T(8,128)S(1)}, u32[]{:S(2)}, u32[]{:S(2)}) collective-permute-start(f32[104,128]{1,0:T(8,128)S(1)} %get-tuple-element.33), channel_id=1, source_target_pairs={{0,4},{1,5},{2,6},{3,7},{4,0},{5,1},{6,2},{7,3},{8,12},{9,13},{10,... | collective-permute-start | bytes 159752 | tf_op jit(solution)/shard_map/ppermute | solution.py:546
  45.0 3.2 %collective-permute-start.13 = (f32[200,128]{1,0:T(8,128)S(1)}, f32[200,128]{1,0:T(8,128)S(1)}, u32[]{:S(2)}, u32[]{:S(2)}) collective-permute-start(f32[200,128]{1,0:T(8,128)S(1)} %collective-permute-done.10.mine_0), channel_id=1, source_target_pairs={{0,8},{8,0},{1,9},{9,1},{2,10},{10,2},{3,11},{11,3},{4,12},{12,4},... | collective-permute-start | bytes 307208 | tf_op jit(solution)/shard_map/ppermute | solution.py:538
  45.8 2.4 %collective-permute-start.14 = (f32[200,128]{1,0:T(8,128)S(1)}, f32[200,128]{1,0:T(8,128)S(1)}, u32[]{:S(2)}, u32[]{:S(2)}) collective-permute-start(f32[200,128]{1,0:T(8,128)S(1)} %collective-permute-done.11.mine_1), channel_id=1, source_target_pairs={{0,8},{8,0},{1,9},{9,1},{2,10},{10,2},{3,11},{11,3},{4,12},{12,4},... | collective-permute-start | bytes 307208 | tf_op jit(solution)/shard_map/ppermute | solution.py:538
  46.0 2.2 %collective-permute-start.15 = (f32[200,128]{1,0:T(8,128)S(1)}, f32[200,128]{1,0:T(8,128)S(1)}, u32[]{:S(2)}, u32[]{:S(2)}) collective-permute-start(f32[200,128]{1,0:T(8,128)S(1)} %collective-permute-done.12.mine_2), channel_id=1, source_target_pairs={{0,8},{8,0},{1,9},{9,1},{2,10},{10,2},{3,11},{11,3},{4,12},{12,4},... | collective-permute-start | bytes 307208 | tf_op jit(solution)/shard_map/ppermute | solution.py:538

commit v8 on v7

--- a/solution.py
+++ b/solution.py
@@ -144,9 +144,10 @@
 PAD = 8
 SPILL_TURNS = (0, 4, 8)
 WAY_IN = ((1, 4), (5, 2), (3, 6), (7, 7))
-WAY_OUT = ((5, 7), (6, 1), (2, 3), (4, 4))
+WAY_OUT = ((5, 7), (1, 6), (2, 3), (4, 4))
 JOIN_COST = pl.CostEstimate(flops=10**10, bytes_accessed=10**7, transcendentals=0)
 EDGE_ROWS = 16
+PACK_ROOM = 54080
 FINE_CHUNKS = ((0, 16), (32, 16), (16, 16))
 HALF_CHUNKS = ((0, 16), (32, 16), (16, 16))
 QUARTER_CHUNKS = ((0, 24),)
@@ -221,7 +222,16 @@
     return [sent_to(masks[::-1] if other_core else masks) for masks in way] + [lax.axis_index("space")]
 
 
-def prepare_kernel(turns, field, turned, edges, split, sums, coarse):
+def given_rows(way, part):
+    sizes = [part if a == b else 5 * part for a, b in way] + [part]
+    return [(sum(sizes[:n]), sum(sizes[: n + 1])) for n in range(len(sizes))]
+
+
+def by_kind(way):
+    return [m for m in way if m[0] != m[1]], [m for m in way if m[0] == m[1]]
+
+
+def prepare(turns, field, arriving, turned, edges, split, sums, coarse):
     rows = field.shape[1] // 4
     part = rows // 2
     lane = iota((rows, LANES), 1)
@@ -229,6 +239,8 @@
     even_odd = jnp.where(low_half, 2 * lane, 2 * lane - (LANES - 1))
     odd_even = jnp.where(low_half, 2 * lane + 1, 2 * lane - LANES)
     for z in range(2):
+        if z == 0:
+            arriving[0].wait()
         for j in range(4):
             at = slice(j * rows, (j + 1) * rows)
             for n, (x, lanes) in enumerate(((field[z, at, :LANES], even_odd), (field[z, at, LANES:], odd_even))):
@@ -259,7 +271,17 @@
             edges[to : to + EDGE_ROWS, :] = roll(x, place + by)
 
 
-def fill_kernel(initial_turned, initial_edges, reaction_turned, reaction_edges, *blocks):
+def pack_kernel(initial_hbm, reaction_hbm, *refs):
+    blocks, (initial, reaction, initial_turned, reaction_turned, initial_edges, reaction_edges), scratch = refs[:5], refs[5:11], refs[11:]
+    *scratch, arrived = scratch
+    copies = [
+        [pltpu.make_async_copy(source, target, arrived.at[n])]
+        for n, (source, target) in enumerate(((initial_hbm, initial), (reaction_hbm, reaction)))
+    ]
+    for copy in copies[0] + copies[1]:
+        copy.start()
+    prepare((12, -20), initial, copies[0], initial_turned, initial_edges, *scratch)
+    prepare((20, -12), reaction, copies[1], reaction_turned, reaction_edges, *scratch)
     rows = initial_turned.shape[0] // 16
     for dest, block in zip(served(WAY_IN), blocks):
         back = (8 - 16 * dest) & (LANES - 1)
@@ -408,8 +430,8 @@
             at = (k + 1) * small_height + PAD
             strip[k, 2 * rows :, :] = small_a[at : at + part, :] * small_scale
 
-    for n, dest in enumerate(served(WAY_OUT, True)):
-        given[n] = strip[dest]
+    for n, (dest, (first, last)) in enumerate(zip(served(WAY_OUT, True), given_rows(WAY_OUT, part))):
+        given[first:last, :] = strip[dest, 5 * part - (last - first) :, :]
 
 
 def send_kernel(mine, other, *blocks):
@@ -419,8 +441,8 @@
     in_quarter = iota((part, LANES), 1) & 31
     own = inside(in_quarter, 8, 24)
     spill = (inside(in_quarter, 4, 8) | inside(in_quarter, 24, 28))[:8]
-    for n, (dest, block) in enumerate(zip(served(WAY_OUT), blocks)):
-        kept, came = mine[dest, 2 * rows :, :], other[n, 2 * rows :, :]
+    for dest, block, (first_row, last_row) in zip(served(WAY_OUT), blocks, given_rows(WAY_OUT, part)):
+        kept, came = mine[dest, 2 * rows :, :], other[last_row - part : last_row, :]
         change, first = jnp.where(tm == 0, kept, came), jnp.where(tm == 0, came, kept)
         short = block.shape[0] < 4 * rows
         if short:
@@ -433,7 +455,7 @@
                 if short:
                     block[at, :] = (h[0] + mine[dest, at, :]) - jnp.where(tm == 0, h[0], 0.0)
                 else:
-                    kept, came = mine[dest, at, :], other[n, at, :]
+                    kept, came = mine[dest, at, :], other[pl.ds(first_row + e * rows + odd, part, 2), :]
                     block[at, :] = (h[0] + jnp.where(tm == 0, kept, came)) - h[0]
                     block[to, :] = h[1] + jnp.where(tm == 0, came, kept)
         packed = None
@@ -443,20 +465,24 @@
         block[block.shape[0] - 8 :, :] = packed
 
 
-def join_kernel(own_block, last_block, both):
-    both[0] = own_block[...]
-    both[1] = last_block[...]
-
-
-def unpack_kernel(both, mine_0, mine_1, mine_2, other_0, other_1, other_2, out_hbm, strips, spilled, turned, halves, out, left):
+def join_kernel(*refs):
+    *blocks, joined = refs
+    for n, block in enumerate(blocks):
+        joined[n] = block[...]
+
+
+def unpack_kernel(joined, *refs):
+    shared, alone = by_kind(WAY_OUT)
+    *came, out_hbm, strips, spilled, turned, halves, out, left = refs
     tm, space = lax.axis_index("tm"), lax.axis_index("space")
     count = strips.shape[0]
     rows = out.shape[1] // 4
     part = rows // 2
-    strips[space] = both[0]
-    strips[space ^ WAY_OUT[-1][0]] = both[1]
+    strips[space] = joined[0]
+    for n, masks in enumerate(alone):
+        strips[space ^ masks[0]] = joined[n + 1]
     blocks = []
-    for masks, mine, other in zip(WAY_OUT, (mine_0, mine_1, mine_2), (other_0, other_1, other_2)):
+    for masks, mine, other in zip(shared, came[: len(shared)], came[len(shared) :]):
         blocks += [(mine, sent_to(masks)), (other, sent_to(masks[::-1]))]
     for block, k in blocks:
         strips[k, : 2 * rows, :] = jnp.where(tm == 0, block[: 2 * rows, :], block[2 * rows : 4 * rows, :])
@@ -519,18 +545,19 @@
 
 
 VMEM = pl.BlockSpec(memory_space=pltpu.VMEM)
-
-
-def on_core(kernel, inputs, out_shapes, scratch=(), out_spec=VMEM, cost=None):
+HBM = pl.BlockSpec(memory_space=pltpu.HBM)
+
+
+def on_core(kernel, inputs, out_shapes, scratch=(), in_spec=VMEM, out_spec=VMEM, cost=None, room=48 * 1024):
     shapes = [jax.ShapeDtypeStruct(s, jnp.float32) for s in out_shapes]
     return pl.pallas_call(
         kernel,
         out_shape=shapes,
-        in_specs=[VMEM] * len(inputs),
+        in_specs=[in_spec] * len(inputs),
         out_specs=[out_spec] * len(shapes),
         cost_estimate=cost,
         scratch_shapes=[pltpu.VMEM(s, jnp.float32) if isinstance(s, tuple) else s for s in scratch],
-        compiler_params=pltpu.CompilerParams(vmem_limit_bytes=48 * 1024 * 1024),
+        compiler_params=pltpu.CompilerParams(vmem_limit_bytes=room * 1024),
     )(*inputs)
 
 
@@ -554,15 +581,17 @@
     part = rows // 2
     planes = 2 * count
     block = (8 * rows + EDGE_ROWS, LANES)
-    prepared = []
-    for field, turns in ((initial, (12, -20)), (reaction, (20, -12))):
-        prepared += on_core(
-            functools.partial(prepare_kernel, turns),
-            [field],
-            [(16 * rows, LANES), (4 * rows, LANES)],
-            [(16 * rows, LANES), (4 * rows + PAD, LANES), (2 * rows, LANES)],
-        )
-    *blocks, own_block = on_core(fill_kernel, prepared, [block] * 3 + [(4 * rows + EDGE_ROWS, LANES), block])
+    *blocks, own_block = on_core(
+        pack_kernel,
+        [initial, reaction],
+        [block] * 3 + [(4 * rows + EDGE_ROWS, LANES), block],
+        [initial.shape] * 2
+        + [(16 * rows, LANES)] * 2
+        + [(4 * rows, LANES)] * 2
+        + [(16 * rows, LANES), (4 * rows + PAD, LANES), (2 * rows, LANES), pltpu.SemaphoreType.DMA((2,))],
+        in_spec=HBM,
+        room=PACK_ROOM,
+    )
     mine = exchanged(blocks, WAY_IN)
     other = [swapped(x) for x in mine]
     fine = ((planes + 2) * (rows + 2 * PAD), LANES)
@@ -572,23 +601,25 @@
     strip, given = on_core(
         march_kernel,
         [own_block, *mine, *other],
-        [(count, 5 * part, LANES), (len(WAY_OUT) + 1, 5 * part, LANES)],
+        [(count, 5 * part, LANES), (given_rows(WAY_OUT, part)[-1][1], LANES)],
         [fine] * 4
         + [(planes * rows, LANES)] * 2
         + [wide, wide, (count * rows, LANES), small, small]
         + [small_cells] * 2
         + [(planes * rows + PAD, LANES)],
     )
-    *blocks, own_block = on_core(send_kernel, [strip, swapped(given)], [(4 * rows + 8, LANES)] * 3 + [(2 * rows + 8, LANES)] * 2)
-    *mine, last = exchanged(blocks, WAY_OUT)
+    *blocks, own_block = on_core(send_kernel, [strip, swapped(given)], [((2 if a == b else 4) * rows + 8, LANES) for a, b in WAY_OUT + ((0, 0),)])
+    came = list(zip(exchanged(blocks, WAY_OUT), WAY_OUT))
+    mine = [x for x, (a, b) in came if a != b]
     other = [swapped(x) for x in mine]
-    (both,) = on_core(join_kernel, [own_block, last], [(2, 2 * rows + 8, LANES)], cost=JOIN_COST)
+    alone = [own_block] + [x for x, (a, b) in came if a == b]
+    (joined,) = on_core(join_kernel, alone, [(len(alone), 2 * rows + 8, LANES)], cost=JOIN_COST)
     (out,) = on_core(
         unpack_kernel,
-        [both, *mine, *other],
+        [joined, *mine, *other],
         [initial.shape],
         [(count, 2 * rows + 8, LANES), (nx + PAD, LANES), (nx, LANES), (16 * rows, LANES), initial.shape, pltpu.SemaphoreType.DMA((2,))],
-        pl.BlockSpec(memory_space=pltpu.HBM),
+        out_spec=HBM,
     )
     return out[None]
 

time: 49.7 us -> 48.2 us (0.970)
  starting transfers between devices: 23.2 us -> 21.3 us
  local copies, waits for them, and re-layouts: 1.56 us -> 0 us
  waiting for transfers between devices: 15.1 us -> 16.1 us
  Pallas kernels: 9.57 us -> 10.5 us
    ppermute x8, starting transfers between devices: 17.5 us -> 15.4 us  [exchanged(): came.append(lax.ppermute(block, ('tm', 'space'), pairs))]
    unnamed x4 -> x0, local copies, waits for them, and re-layouts: 1.56 us -> none
    ppermute x8, waiting for transfers between devices: 12.5 us -> 13.7 us  [exchanged(): came.append(lax.ppermute(block, ('tm', 'space'), pairs))]
    pallas_call x7 -> x5, Pallas kernels: 9.57 us -> 10.5 us  [on_core(): pl.pallas_call(kernel, out_shape=shapes, in_specs=[in_spec] * len(inputs)...]
  transfers between devices with their start and end apart: 16 -> 16, of which waited for: 7 -> 6; matrix products, arithmetic and copies ran while one was open for 0% -> 0% of each run, Pallas kernels for 0% -> 0%
where the time goes in v8:
time: 48.2 us; the launch traced here: 47.9 us
  starting transfers between devices  21.3 us (44%)
  waiting for transfers between devices  16.1 us (33%)
  Pallas kernels  10.5 us (22%)
    ppermute x8, starting transfers between devices, exchanged(): came.append(lax.ppermute(block, ('tm', 'space'), pairs))  15.4 us
    ppermute x8, waiting for transfers between devices, exchanged(): came.append(lax.ppermute(block, ('tm', 'space'), pairs))  13.7 us
    pallas_call x5, Pallas kernels, on_core(): pl.pallas_call(kernel, out_shape=shapes, in_specs=[in_spec] * len(inputs)...  10.5 us
    ppermute x8, starting transfers between devices, swapped(): return lax.ppermute(x, 'tm', [(0, 1), (1, 0)])  5.88 us
    ppermute x8, waiting for transfers between devices, swapped(): return lax.ppermute(x, 'tm', [(0, 1), (1, 0)])  2.41 us
  transfers between devices with their start and end apart: 16, of which 6 were waited for; matrix products, arithmetic and copies ran while one was open for 0% of the time, Pallas kernels for 0%

profile of v8, /device:TPU:0, one launch (start us, length us, event | category | flops | bytes accessed | tf_op | source)
XLA Modules:
  0.0 47.9 jit_solution(7187521141333502763)
XLA Ops:
  0.0 2.1 %shard_map.28 = (f32[400,128]{1,0:T(8,128)S(1)}, f32[400,128]{1,0:T(8,128)S(1)}, f32[400,128]{1,0:T(8,128)S(1)}, f32[208,128]{1,0:T(8,128)S(1)}, f32[400,128]{1,0:T(8,128)S(1)}) custom-call(f32[2,192,256]{2,1,0:T(8,128)} %initial_hbm.1, f32[2,192,256]{2,1,0:T(8,128)} %reaction_hbm.1), custom_call_target="tpu_custom_call" | custom-call | tf_op jit(solution)/shard_map/pallas_call | solution.py:553
  2.2 3.0 %collective-permute-start = (f32[400,128]{1,0:T(8,128)S(1)}, f32[400,128]{1,0:T(8,128)S(1)}, u32[]{:S(2)}, u32[]{:S(2)}) collective-permute-start(f32[400,128]{1,0:T(8,128)S(1)} %get-tuple-element.18), channel_id=1, source_target_pairs={{0,1},{1,0},{2,3},{3,2},{4,5},{5,4},{6,7},{7,6},{8,12},{9,13},{10,... | collective-permute-start | bytes 614408 | tf_op jit(solution)/shard_map/ppermute | solution.py:573
  5.2 2.6 %collective-permute-start.1 = (f32[400,128]{1,0:T(8,128)S(1)}, f32[400,128]{1,0:T(8,128)S(1)}, u32[]{:S(2)}, u32[]{:S(2)}) collective-permute-start(f32[400,128]{1,0:T(8,128)S(1)} %get-tuple-element.19), channel_id=1, source_target_pairs={{0,5},{1,4},{2,7},{3,6},{4,1},{5,0},{6,3},{7,2},{8,10},{9,11},{10,... | collective-permute-start | bytes 614408 | tf_op jit(solution)/shard_map/ppermute | solution.py:573
  7.7 2.5 %collective-permute-start.2 = (f32[400,128]{1,0:T(8,128)S(1)}, f32[400,128]{1,0:T(8,128)S(1)}, u32[]{:S(2)}, u32[]{:S(2)}) collective-permute-start(f32[400,128]{1,0:T(8,128)S(1)} %get-tuple-element.20), channel_id=1, source_target_pairs={{0,3},{1,2},{2,1},{3,0},{4,7},{5,6},{6,5},{7,4},{8,14},{9,15},{10,... | collective-permute-start | bytes 614408 | tf_op jit(solution)/shard_map/ppermute | solution.py:573
  10.2 0.0 collective-permute-start.3
  10.2 0.0 collective-permute-done.mine_0
  10.2 3.8 %collective-permute-start.4 = (f32[400,128]{1,0:T(8,128)S(1)}, f32[400,128]{1,0:T(8,128)S(1)}, u32[]{:S(2)}, u32[]{:S(2)}) collective-permute-start(f32[400,128]{1,0:T(8,128)S(1)} %collective-permute-done.mine_0), channel_id=1, source_target_pairs={{0,8},{8,0},{1,9},{9,1},{2,10},{10,2},{3,11},{11,3},{4,12},{12,4},... | collective-permute-start | bytes 614408 | tf_op jit(solution)/shard_map/ppermute | solution.py:565
  14.0 8.3 %collective-permute-done.1.mine_1 = f32[400,128]{1,0:T(8,128)S(1)} collective-permute-done((f32[400,128]{1,0:T(8,128)S(1)}, f32[400,128]{1,0:T(8,128)S(1)}, u32[]{:S(2)}, u32[]{:S(2)}) %collective-permute-start.1) | collective-permute-done | bytes 204832 | tf_op jit(solution)/shard_map/ppermute | solution.py:573
  22.4 0.0 collective-permute-start.5
  22.4 0.0 collective-permute-done.2.mine_2
  22.4 0.5 %collective-permute-start.6 = (f32[400,128]{1,0:T(8,128)S(1)}, f32[400,128]{1,0:T(8,128)S(1)}, u32[]{:S(2)}, u32[]{:S(2)}) collective-permute-start(f32[400,128]{1,0:T(8,128)S(1)} %collective-permute-done.2.mine_2), channel_id=1, source_target_pairs={{0,8},{8,0},{1,9},{9,1},{2,10},{10,2},{3,11},{11,3},{4,12},{12,4},... | collective-permute-start | bytes 614408 | tf_op jit(solution)/shard_map/ppermute | solution.py:565
  22.9 0.0 collective-permute-done.3.mine_3
  22.9 0.1 collective-permute-start.7
  22.9 1.3 %collective-permute-done.7.other_3 = f32[208,128]{1,0:T(8,128)S(1)} collective-permute-done((f32[208,128]{1,0:T(8,128)S(1)}, f32[208,128]{1,0:T(8,128)S(1)}, u32[]{:S(2)}, u32[]{:S(2)}) %collective-permute-start.7) | collective-permute-done | bytes 106528 | tf_op jit(solution)/shard_map/ppermute | solution.py:565
  24.3 0.0 collective-permute-done.4.other_0
  24.3 0.0 collective-permute-done.5.other_1
  24.3 0.0 collective-permute-done.6.other_2
  24.3 6.9 %shard_map.29 = (f32[8,120,128]{2,1,0:T(8,128)S(1)}, f32[408,128]{1,0:T(8,128)S(1)}) custom-call(f32[400,128]{1,0:T(8,128)S(1)} %get-tuple-element.17.own_block, f32[400,128]{1,0:T(8,128)S(1)} %collective-permute-done.mine_0, f32[400,128]{1,0:T(8,128)S(1)} %collective-permute-done.1.mine_1, f32[400,128]{1,0:T(8,128)S(1)} %collective-permute-done.2.mine_2, ...), custom_call_target="tpu_custom_call" | custom-call | tf_op jit(solution)/shard_map/pallas_call | solution.py:553
  31.2 1.0 %collective-permute-start.8 = (f32[408,128]{1,0:T(8,128)S(1)}, f32[408,128]{1,0:T(8,128)S(1)}, u32[]{:S(2)}, u32[]{:S(2)}) collective-permute-start(f32[408,128]{1,0:T(8,128)S(1)} %get-tuple-element.23), channel_id=1, source_target_pairs={{0,8},{8,0},{1,9},{9,1},{2,10},{10,2},{3,11},{11,3},{4,12},{12,4},... | collective-permute-start | bytes 626696 | tf_op jit(solution)/shard_map/ppermute | solution.py:565
  32.2 1.1 %collective-permute-done.8.other = f32[408,128]{1,0:T(8,128)S(1)} collective-permute-done((f32[408,128]{1,0:T(8,128)S(1)}, f32[408,128]{1,0:T(8,128)S(1)}, u32[]{:S(2)}, u32[]{:S(2)}) %collective-permute-start.8) | collective-permute-done | bytes 208928 | tf_op jit(solution)/shard_map/ppermute | solution.py:565
  33.2 0.1 shard_map.30
  33.4 5.0 %collective-permute-start.10 = (f32[200,128]{1,0:T(8,128)S(1)}, f32[200,128]{1,0:T(8,128)S(1)}, u32[]{:S(2)}, u32[]{:S(2)}) collective-permute-start(f32[200,128]{1,0:T(8,128)S(1)} %get-tuple-element.26), channel_id=1, source_target_pairs={{0,5},{1,4},{2,7},{3,6},{4,1},{5,0},{6,3},{7,2},{8,15},{9,14},{10,... | collective-permute-start | bytes 307208 | tf_op jit(solution)/shard_map/ppermute | solution.py:573
  38.4 1.4 %collective-permute-start.11 = (f32[200,128]{1,0:T(8,128)S(1)}, f32[200,128]{1,0:T(8,128)S(1)}, u32[]{:S(2)}, u32[]{:S(2)}) collective-permute-start(f32[200,128]{1,0:T(8,128)S(1)} %get-tuple-element.27), channel_id=1, source_target_pairs={{0,1},{1,0},{2,3},{3,2},{4,5},{5,4},{6,7},{7,6},{8,14},{9,15},{10,... | collective-permute-start | bytes 307208 | tf_op jit(solution)/shard_map/ppermute | solution.py:573
  39.8 0.0 collective-permute-start.12
  39.8 0.9 %collective-permute-start.9 = (f32[104,128]{1,0:T(8,128)S(1)}, f32[104,128]{1,0:T(8,128)S(1)}, u32[]{:S(2)}, u32[]{:S(2)}) collective-permute-start(f32[104,128]{1,0:T(8,128)S(1)} %get-tuple-element.25), channel_id=1, source_target_pairs={{0,4},{1,5},{2,6},{3,7},{4,0},{5,1},{6,2},{7,3},{8,12},{9,13},{10,... | collective-permute-start | bytes 159752 | tf_op jit(solution)/shard_map/ppermute | solution.py:573
  40.7 3.9 %collective-permute-done.10.refs_0_ = f32[200,128]{1,0:T(8,128)S(1)} collective-permute-done((f32[200,128]{1,0:T(8,128)S(1)}, f32[200,128]{1,0:T(8,128)S(1)}, u32[]{:S(2)}, u32[]{:S(2)}) %collective-permute-start.10) | collective-permute-done | bytes 102432 | tf_op jit(solution)/shard_map/ppermute | solution.py:573
  44.6 0.0 collective-permute-start.13
  44.6 0.0 collective-permute-done.11.refs_1_
  44.6 0.5 %collective-permute-start.14 = (f32[200,128]{1,0:T(8,128)S(1)}, f32[200,128]{1,0:T(8,128)S(1)}, u32[]{:S(2)}, u32[]{:S(2)}) collective-permute-start(f32[200,128]{1,0:T(8,128)S(1)} %collective-permute-done.11.refs_1_), channel_id=1, source_target_pairs={{0,8},{8,0},{1,9},{9,1},{2,10},{10,2},{3,11},{11,3},{4,12},{12,4},... | collective-permute-start | bytes 307208 | tf_op jit(solution)/shard_map/ppermute | solution.py:565
  45.1 0.2 collective-permute-done.12.refs_2_
  45.3 0.0 collective-permute-start.15
  45.3 1.3 %collective-permute-done.9.refs_1_ = f32[104,128]{1,0:T(8,128)S(1)} collective-permute-done((f32[104,128]{1,0:T(8,128)S(1)}, f32[104,128]{1,0:T(8,128)S(1)}, u32[]{:S(2)}, u32[]{:S(2)}) %collective-permute-start.9) | collective-permute-done | bytes 53280 | tf_op jit(solution)/shard_map/ppermute | solution.py:573
  46.6 0.0 collective-permute-done.13.refs_3_
  46.6 0.0 collective-permute-done.14.refs_4_
  46.6 0.0 collective-permute-done.15.refs_5_
  46.7 1.3 %shard_map.32 = f32[2,192,256]{2,1,0:T(8,128)} custom-call(f32[2,104,128]{2,1,0:T(8,128)S(1)} %shard_map.31.joined, f32[200,128]{1,0:T(8,128)S(1)} %collective-permute-done.10.refs_0_, f32[200,128]{1,0:T(8,128)S(1)} %collective-permute-done.11.refs_1_, f32[200,128]{1,0:T(8,128)S(1)} %collective-permute-done.12.refs_2_, ...), custom_call_target="tpu_custom_call" | custom-call | tf_op jit(solution)/shard_map/pallas_call | solution.py:553
  (1 shorter events, 0.0 us)
Async XLA Ops:
  2.2 8.1 %collective-permute-start = (f32[400,128]{1,0:T(8,128)S(1)}, f32[400,128]{1,0:T(8,128)S(1)}, u32[]{:S(2)}, u32[]{:S(2)}) collective-permute-start(f32[400,128]{1,0:T(8,128)S(1)} %get-tuple-element.18), channel_id=1, source_target_pairs={{0,1},{1,0},{2,3},{3,2},{4,5},{5,4},{6,7},{7,6},{8,12},{9,13},{10,... | collective-permute-start | bytes 614408 | tf_op jit(solution)/shard_map/ppermute | solution.py:573
  5.2 17.2 %collective-permute-start.1 = (f32[400,128]{1,0:T(8,128)S(1)}, f32[400,128]{1,0:T(8,128)S(1)}, u32[]{:S(2)}, u32[]{:S(2)}) collective-permute-start(f32[400,128]{1,0:T(8,128)S(1)} %get-tuple-element.19), channel_id=1, source_target_pairs={{0,5},{1,4},{2,7},{3,6},{4,1},{5,0},{6,3},{7,2},{8,10},{9,11},{10,... | collective-permute-start | bytes 614408 | tf_op jit(solution)/shard_map/ppermute | solution.py:573
  7.7 14.6 %collective-permute-start.2 = (f32[400,128]{1,0:T(8,128)S(1)}, f32[400,128]{1,0:T(8,128)S(1)}, u32[]{:S(2)}, u32[]{:S(2)}) collective-permute-start(f32[400,128]{1,0:T(8,128)S(1)} %get-tuple-element.20), channel_id=1, source_target_pairs={{0,3},{1,2},{2,1},{3,0},{4,7},{5,6},{6,5},{7,4},{8,14},{9,15},{10,... | collective-permute-start | bytes 614408 | tf_op jit(solution)/shard_map/ppermute | solution.py:573
  10.2 12.6 %collective-permute-start.3 = (f32[208,128]{1,0:T(8,128)S(1)}, f32[208,128]{1,0:T(8,128)S(1)}, u32[]{:S(2)}, u32[]{:S(2)}) collective-permute-start(f32[208,128]{1,0:T(8,128)S(1)} %get-tuple-element.21), channel_id=1, source_target_pairs={{0,7},{1,6},{2,5},{3,4},{4,3},{5,2},{6,1},{7,0},{8,15},{9,14},{10,... | collective-permute-start | bytes 319496 | tf_op jit(solution)/shard_map/ppermute | solution.py:573
  10.2 14.0 %collective-permute-start.4 = (f32[400,128]{1,0:T(8,128)S(1)}, f32[400,128]{1,0:T(8,128)S(1)}, u32[]{:S(2)}, u32[]{:S(2)}) collective-permute-start(f32[400,128]{1,0:T(8,128)S(1)} %collective-permute-done.mine_0), channel_id=1, source_target_pairs={{0,8},{8,0},{1,9},{9,1},{2,10},{10,2},{3,11},{11,3},{4,12},{12,4},... | collective-permute-start | bytes 614408 | tf_op jit(solution)/shard_map/ppermute | solution.py:565
  22.4 1.9 %collective-permute-start.5 = (f32[400,128]{1,0:T(8,128)S(1)}, f32[400,128]{1,0:T(8,128)S(1)}, u32[]{:S(2)}, u32[]{:S(2)}) collective-permute-start(f32[400,128]{1,0:T(8,128)S(1)} %collective-permute-done.1.mine_1), channel_id=1, source_target_pairs={{0,8},{8,0},{1,9},{9,1},{2,10},{10,2},{3,11},{11,3},{4,12},{12,4},... | collective-permute-start | bytes 614408 | tf_op jit(solution)/shard_map/ppermute | solution.py:565
  22.4 1.9 %collective-permute-start.6 = (f32[400,128]{1,0:T(8,128)S(1)}, f32[400,128]{1,0:T(8,128)S(1)}, u32[]{:S(2)}, u32[]{:S(2)}) collective-permute-start(f32[400,128]{1,0:T(8,128)S(1)} %collective-permute-done.2.mine_2), channel_id=1, source_target_pairs={{0,8},{8,0},{1,9},{9,1},{2,10},{10,2},{3,11},{11,3},{4,12},{12,4},... | collective-permute-start | bytes 614408 | tf_op jit(solution)/shard_map/ppermute | solution.py:565
  22.9 1.4 %collective-permute-start.7 = (f32[208,128]{1,0:T(8,128)S(1)}, f32[208,128]{1,0:T(8,128)S(1)}, u32[]{:S(2)}, u32[]{:S(2)}) collective-permute-start(f32[208,128]{1,0:T(8,128)S(1)} %collective-permute-done.3.mine_3), channel_id=1, source_target_pairs={{0,8},{8,0},{1,9},{9,1},{2,10},{10,2},{3,11},{11,3},{4,12},{12,4},... | collective-permute-start | bytes 319496 | tf_op jit(solution)/shard_map/ppermute | solution.py:565
  31.2 2.1 %collective-permute-start.8 = (f32[408,128]{1,0:T(8,128)S(1)}, f32[408,128]{1,0:T(8,128)S(1)}, u32[]{:S(2)}, u32[]{:S(2)}) collective-permute-start(f32[408,128]{1,0:T(8,128)S(1)} %get-tuple-element.23), channel_id=1, source_target_pairs={{0,8},{8,0},{1,9},{9,1},{2,10},{10,2},{3,11},{11,3},{4,12},{12,4},... | collective-permute-start | bytes 626696 | tf_op jit(solution)/shard_map/ppermute | solution.py:565
  33.4 11.2 %collective-permute-start.10 = (f32[200,128]{1,0:T(8,128)S(1)}, f32[200,128]{1,0:T(8,128)S(1)}, u32[]{:S(2)}, u32[]{:S(2)}) collective-permute-start(f32[200,128]{1,0:T(8,128)S(1)} %get-tuple-element.26), channel_id=1, source_target_pairs={{0,5},{1,4},{2,7},{3,6},{4,1},{5,0},{6,3},{7,2},{8,15},{9,14},{10,... | collective-permute-start | bytes 307208 | tf_op jit(solution)/shard_map/ppermute | solution.py:573
  38.4 6.3 %collective-permute-start.11 = (f32[200,128]{1,0:T(8,128)S(1)}, f32[200,128]{1,0:T(8,128)S(1)}, u32[]{:S(2)}, u32[]{:S(2)}) collective-permute-start(f32[200,128]{1,0:T(8,128)S(1)} %get-tuple-element.27), channel_id=1, source_target_pairs={{0,1},{1,0},{2,3},{3,2},{4,5},{5,4},{6,7},{7,6},{8,14},{9,15},{10,... | collective-permute-start | bytes 307208 | tf_op jit(solution)/shard_map/ppermute | solution.py:573
  39.8 5.5 %collective-permute-start.12 = (f32[200,128]{1,0:T(8,128)S(1)}, f32[200,128]{1,0:T(8,128)S(1)}, u32[]{:S(2)}, u32[]{:S(2)}) collective-permute-start(f32[200,128]{1,0:T(8,128)S(1)} %get-tuple-element.28), channel_id=1, source_target_pairs={{0,2},{1,3},{2,0},{3,1},{4,6},{5,7},{6,4},{7,5},{8,11},{9,10},{10,... | collective-permute-start | bytes 307208 | tf_op jit(solution)/shard_map/ppermute | solution.py:573
  39.8 6.8 %collective-permute-start.9 = (f32[104,128]{1,0:T(8,128)S(1)}, f32[104,128]{1,0:T(8,128)S(1)}, u32[]{:S(2)}, u32[]{:S(2)}) collective-permute-start(f32[104,128]{1,0:T(8,128)S(1)} %get-tuple-element.25), channel_id=1, source_target_pairs={{0,4},{1,5},{2,6},{3,7},{4,0},{5,1},{6,2},{7,3},{8,12},{9,13},{10,... | collective-permute-start | bytes 159752 | tf_op jit(solution)/shard_map/ppermute | solution.py:573
  44.6 2.0 %collective-permute-start.13 = (f32[200,128]{1,0:T(8,128)S(1)}, f32[200,128]{1,0:T(8,128)S(1)}, u32[]{:S(2)}, u32[]{:S(2)}) collective-permute-start(f32[200,128]{1,0:T(8,128)S(1)} %collective-permute-done.10.refs_0_), channel_id=1, source_target_pairs={{0,8},{8,0},{1,9},{9,1},{2,10},{10,2},{3,11},{11,3},{4,12},{12,4},... | collective-permute-start | bytes 307208 | tf_op jit(solution)/shard_map/ppermute | solution.py:565
  44.6 2.0 %collective-permute-start.14 = (f32[200,128]{1,0:T(8,128)S(1)}, f32[200,128]{1,0:T(8,128)S(1)}, u32[]{:S(2)}, u32[]{:S(2)}) collective-permute-start(f32[200,128]{1,0:T(8,128)S(1)} %collective-permute-done.11.refs_1_), channel_id=1, source_target_pairs={{0,8},{8,0},{1,9},{9,1},{2,10},{10,2},{3,11},{11,3},{4,12},{12,4},... | collective-permute-start | bytes 307208 | tf_op jit(solution)/shard_map/ppermute | solution.py:565
  45.3 1.3 %collective-permute-start.15 = (f32[200,128]{1,0:T(8,128)S(1)}, f32[200,128]{1,0:T(8,128)S(1)}, u32[]{:S(2)}, u32[]{:S(2)}) collective-permute-start(f32[200,128]{1,0:T(8,128)S(1)} %collective-permute-done.12.refs_2_), channel_id=1, source_target_pairs={{0,8},{8,0},{1,9},{9,1},{2,10},{10,2},{3,11},{11,3},{4,12},{12,4},... | collective-permute-start | bytes 307208 | tf_op jit(solution)/shard_map/ppermute | solution.py:565

commit v9 on v8

--- a/solution.py
+++ b/solution.py
@@ -538,8 +538,10 @@
             even, odd = even + spilled[at, :], odd + turned[at, :]
             out[z, at, :LANES] = take(jnp.where(low_half, even, odd), from_first)
             out[z, at, LANES:] = take(jnp.where(low_half, odd, even), from_second)
-        copies.append(pltpu.make_async_copy(out.at[z], out_hbm.at[z], left.at[z]))
-        copies[-1].start()
+            if j % 2 == 1:
+                sent = pl.ds((j - 1) * rows, 2 * rows)
+                copies.append(pltpu.make_async_copy(out.at[z, sent], out_hbm.at[z, sent], left.at[2 * z + j // 2]))
+                copies[-1].start()
     for copy in copies:
         copy.wait()
 
@@ -618,7 +620,7 @@
         unpack_kernel,
         [joined, *mine, *other],
         [initial.shape],
-        [(count, 2 * rows + 8, LANES), (nx + PAD, LANES), (nx, LANES), (16 * rows, LANES), initial.shape, pltpu.SemaphoreType.DMA((2,))],
+        [(count, 2 * rows + 8, LANES), (nx + PAD, LANES), (nx, LANES), (16 * rows, LANES), initial.shape, pltpu.SemaphoreType.DMA((4,))],
         out_spec=HBM,
     )
     return out[None]

time: 48.2 us -> 48.2 us (level)
  no operation moved by 1% of the time
where the time goes in v9:
time: 48.2 us; the launch traced here: 47.9 us
  starting transfers between devices  21.3 us (44%)
  waiting for transfers between devices  16.1 us (33%)
  Pallas kernels  10.4 us (22%)
    ppermute x8, starting transfers between devices, exchanged(): came.append(lax.ppermute(block, ('tm', 'space'), pairs))  15.4 us
    ppermute x8, waiting for transfers between devices, exchanged(): came.append(lax.ppermute(block, ('tm', 'space'), pairs))  13.7 us
    pallas_call x5, Pallas kernels, on_core(): pl.pallas_call(kernel, out_shape=shapes, in_specs=[in_spec] * len(inputs)...  10.4 us
    ppermute x8, starting transfers between devices, swapped(): return lax.ppermute(x, 'tm', [(0, 1), (1, 0)])  5.88 us
    ppermute x8, waiting for transfers between devices, swapped(): return lax.ppermute(x, 'tm', [(0, 1), (1, 0)])  2.41 us
  transfers between devices with their start and end apart: 16, of which 6 were waited for; matrix products, arithmetic and copies ran while one was open for 0% of the time, Pallas kernels for 0%

profile of v9, /device:TPU:0, one launch (start us, length us, event | category | flops | bytes accessed | tf_op | source)
XLA Modules:
  0.0 47.9 jit_solution(7367773687207210750)
XLA Ops:
  0.0 2.1 %shard_map.28 = (f32[400,128]{1,0:T(8,128)S(1)}, f32[400,128]{1,0:T(8,128)S(1)}, f32[400,128]{1,0:T(8,128)S(1)}, f32[208,128]{1,0:T(8,128)S(1)}, f32[400,128]{1,0:T(8,128)S(1)}) custom-call(f32[2,192,256]{2,1,0:T(8,128)} %initial_hbm.1, f32[2,192,256]{2,1,0:T(8,128)} %reaction_hbm.1), custom_call_target="tpu_custom_call" | custom-call | tf_op jit(solution)/shard_map/pallas_call | solution.py:555
  2.2 3.0 %collective-permute-start = (f32[400,128]{1,0:T(8,128)S(1)}, f32[400,128]{1,0:T(8,128)S(1)}, u32[]{:S(2)}, u32[]{:S(2)}) collective-permute-start(f32[400,128]{1,0:T(8,128)S(1)} %get-tuple-element.18), channel_id=1, source_target_pairs={{0,1},{1,0},{2,3},{3,2},{4,5},{5,4},{6,7},{7,6},{8,12},{9,13},{10,... | collective-permute-start | bytes 614408 | tf_op jit(solution)/shard_map/ppermute | solution.py:575
  5.2 2.6 %collective-permute-start.1 = (f32[400,128]{1,0:T(8,128)S(1)}, f32[400,128]{1,0:T(8,128)S(1)}, u32[]{:S(2)}, u32[]{:S(2)}) collective-permute-start(f32[400,128]{1,0:T(8,128)S(1)} %get-tuple-element.19), channel_id=1, source_target_pairs={{0,5},{1,4},{2,7},{3,6},{4,1},{5,0},{6,3},{7,2},{8,10},{9,11},{10,... | collective-permute-start | bytes 614408 | tf_op jit(solution)/shard_map/ppermute | solution.py:575
  7.7 2.5 %collective-permute-start.2 = (f32[400,128]{1,0:T(8,128)S(1)}, f32[400,128]{1,0:T(8,128)S(1)}, u32[]{:S(2)}, u32[]{:S(2)}) collective-permute-start(f32[400,128]{1,0:T(8,128)S(1)} %get-tuple-element.20), channel_id=1, source_target_pairs={{0,3},{1,2},{2,1},{3,0},{4,7},{5,6},{6,5},{7,4},{8,14},{9,15},{10,... | collective-permute-start | bytes 614408 | tf_op jit(solution)/shard_map/ppermute | solution.py:575
  10.2 0.0 collective-permute-start.3
  10.2 0.0 collective-permute-done.mine_0
  10.2 3.8 %collective-permute-start.4 = (f32[400,128]{1,0:T(8,128)S(1)}, f32[400,128]{1,0:T(8,128)S(1)}, u32[]{:S(2)}, u32[]{:S(2)}) collective-permute-start(f32[400,128]{1,0:T(8,128)S(1)} %collective-permute-done.mine_0), channel_id=1, source_target_pairs={{0,8},{8,0},{1,9},{9,1},{2,10},{10,2},{3,11},{11,3},{4,12},{12,4},... | collective-permute-start | bytes 614408 | tf_op jit(solution)/shard_map/ppermute | solution.py:567
  14.0 8.3 %collective-permute-done.1.mine_1 = f32[400,128]{1,0:T(8,128)S(1)} collective-permute-done((f32[400,128]{1,0:T(8,128)S(1)}, f32[400,128]{1,0:T(8,128)S(1)}, u32[]{:S(2)}, u32[]{:S(2)}) %collective-permute-start.1) | collective-permute-done | bytes 204832 | tf_op jit(solution)/shard_map/ppermute | solution.py:575
  22.4 0.0 collective-permute-start.5
  22.4 0.0 collective-permute-done.2.mine_2
  22.4 0.5 %collective-permute-start.6 = (f32[400,128]{1,0:T(8,128)S(1)}, f32[400,128]{1,0:T(8,128)S(1)}, u32[]{:S(2)}, u32[]{:S(2)}) collective-permute-start(f32[400,128]{1,0:T(8,128)S(1)} %collective-permute-done.2.mine_2), channel_id=1, source_target_pairs={{0,8},{8,0},{1,9},{9,1},{2,10},{10,2},{3,11},{11,3},{4,12},{12,4},... | collective-permute-start | bytes 614408 | tf_op jit(solution)/shard_map/ppermute | solution.py:567
  22.9 0.0 collective-permute-done.3.mine_3
  22.9 0.1 collective-permute-start.7
  22.9 1.3 %collective-permute-done.7.other_3 = f32[208,128]{1,0:T(8,128)S(1)} collective-permute-done((f32[208,128]{1,0:T(8,128)S(1)}, f32[208,128]{1,0:T(8,128)S(1)}, u32[]{:S(2)}, u32[]{:S(2)}) %collective-permute-start.7) | collective-permute-done | bytes 106528 | tf_op jit(solution)/shard_map/ppermute | solution.py:567
  24.3 0.0 collective-permute-done.4.other_0
  24.3 0.0 collective-permute-done.5.other_1
  24.3 0.0 collective-permute-done.6.other_2
  24.3 6.9 %shard_map.29 = (f32[8,120,128]{2,1,0:T(8,128)S(1)}, f32[408,128]{1,0:T(8,128)S(1)}) custom-call(f32[400,128]{1,0:T(8,128)S(1)} %get-tuple-element.17.own_block, f32[400,128]{1,0:T(8,128)S(1)} %collective-permute-done.mine_0, f32[400,128]{1,0:T(8,128)S(1)} %collective-permute-done.1.mine_1, f32[400,128]{1,0:T(8,128)S(1)} %collective-permute-done.2.mine_2, ...), custom_call_target="tpu_custom_call" | custom-call | tf_op jit(solution)/shard_map/pallas_call | solution.py:555
  31.2 1.0 %collective-permute-start.8 = (f32[408,128]{1,0:T(8,128)S(1)}, f32[408,128]{1,0:T(8,128)S(1)}, u32[]{:S(2)}, u32[]{:S(2)}) collective-permute-start(f32[408,128]{1,0:T(8,128)S(1)} %get-tuple-element.23), channel_id=1, source_target_pairs={{0,8},{8,0},{1,9},{9,1},{2,10},{10,2},{3,11},{11,3},{4,12},{12,4},... | collective-permute-start | bytes 626696 | tf_op jit(solution)/shard_map/ppermute | solution.py:567
  32.2 1.1 %collective-permute-done.8.other = f32[408,128]{1,0:T(8,128)S(1)} collective-permute-done((f32[408,128]{1,0:T(8,128)S(1)}, f32[408,128]{1,0:T(8,128)S(1)}, u32[]{:S(2)}, u32[]{:S(2)}) %collective-permute-start.8) | collective-permute-done | bytes 208928 | tf_op jit(solution)/shard_map/ppermute | solution.py:567
  33.2 0.1 shard_map.30
  33.4 5.0 %collective-permute-start.10 = (f32[200,128]{1,0:T(8,128)S(1)}, f32[200,128]{1,0:T(8,128)S(1)}, u32[]{:S(2)}, u32[]{:S(2)}) collective-permute-start(f32[200,128]{1,0:T(8,128)S(1)} %get-tuple-element.26), channel_id=1, source_target_pairs={{0,5},{1,4},{2,7},{3,6},{4,1},{5,0},{6,3},{7,2},{8,15},{9,14},{10,... | collective-permute-start | bytes 307208 | tf_op jit(solution)/shard_map/ppermute | solution.py:575
  38.4 1.4 %collective-permute-start.11 = (f32[200,128]{1,0:T(8,128)S(1)}, f32[200,128]{1,0:T(8,128)S(1)}, u32[]{:S(2)}, u32[]{:S(2)}) collective-permute-start(f32[200,128]{1,0:T(8,128)S(1)} %get-tuple-element.27), channel_id=1, source_target_pairs={{0,1},{1,0},{2,3},{3,2},{4,5},{5,4},{6,7},{7,6},{8,14},{9,15},{10,... | collective-permute-start | bytes 307208 | tf_op jit(solution)/shard_map/ppermute | solution.py:575
  39.8 0.0 collective-permute-start.12
  39.8 0.9 %collective-permute-start.9 = (f32[104,128]{1,0:T(8,128)S(1)}, f32[104,128]{1,0:T(8,128)S(1)}, u32[]{:S(2)}, u32[]{:S(2)}) collective-permute-start(f32[104,128]{1,0:T(8,128)S(1)} %get-tuple-element.25), channel_id=1, source_target_pairs={{0,4},{1,5},{2,6},{3,7},{4,0},{5,1},{6,2},{7,3},{8,12},{9,13},{10,... | collective-permute-start | bytes 159752 | tf_op jit(solution)/shard_map/ppermute | solution.py:575
  40.7 3.9 %collective-permute-done.10.refs_0_ = f32[200,128]{1,0:T(8,128)S(1)} collective-permute-done((f32[200,128]{1,0:T(8,128)S(1)}, f32[200,128]{1,0:T(8,128)S(1)}, u32[]{:S(2)}, u32[]{:S(2)}) %collective-permute-start.10) | collective-permute-done | bytes 102432 | tf_op jit(solution)/shard_map/ppermute | solution.py:575
  44.6 0.0 collective-permute-start.13
  44.6 0.0 collective-permute-done.11.refs_1_
  44.6 0.5 %collective-permute-start.14 = (f32[200,128]{1,0:T(8,128)S(1)}, f32[200,128]{1,0:T(8,128)S(1)}, u32[]{:S(2)}, u32[]{:S(2)}) collective-permute-start(f32[200,128]{1,0:T(8,128)S(1)} %collective-permute-done.11.refs_1_), channel_id=1, source_target_pairs={{0,8},{8,0},{1,9},{9,1},{2,10},{10,2},{3,11},{11,3},{4,12},{12,4},... | collective-permute-start | bytes 307208 | tf_op jit(solution)/shard_map/ppermute | solution.py:567
  45.1 0.2 collective-permute-done.12.refs_2_
  45.3 0.0 collective-permute-start.15
  45.3 1.3 %collective-permute-done.9.refs_1_ = f32[104,128]{1,0:T(8,128)S(1)} collective-permute-done((f32[104,128]{1,0:T(8,128)S(1)}, f32[104,128]{1,0:T(8,128)S(1)}, u32[]{:S(2)}, u32[]{:S(2)}) %collective-permute-start.9) | collective-permute-done | bytes 53280 | tf_op jit(solution)/shard_map/ppermute | solution.py:575
  46.6 0.0 collective-permute-done.13.refs_3_
  46.6 0.0 collective-permute-done.14.refs_4_
  46.6 0.0 collective-permute-done.15.refs_5_
  46.7 1.3 %shard_map.32 = f32[2,192,256]{2,1,0:T(8,128)} custom-call(f32[2,104,128]{2,1,0:T(8,128)S(1)} %shard_map.31.joined, f32[200,128]{1,0:T(8,128)S(1)} %collective-permute-done.10.refs_0_, f32[200,128]{1,0:T(8,128)S(1)} %collective-permute-done.11.refs_1_, f32[200,128]{1,0:T(8,128)S(1)} %collective-permute-done.12.refs_2_, ...), custom_call_target="tpu_custom_call" | custom-call | tf_op jit(solution)/shard_map/pallas_call | solution.py:555
  (1 shorter events, 0.0 us)
Async XLA Ops:
  2.2 8.1 %collective-permute-start = (f32[400,128]{1,0:T(8,128)S(1)}, f32[400,128]{1,0:T(8,128)S(1)}, u32[]{:S(2)}, u32[]{:S(2)}) collective-permute-start(f32[400,128]{1,0:T(8,128)S(1)} %get-tuple-element.18), channel_id=1, source_target_pairs={{0,1},{1,0},{2,3},{3,2},{4,5},{5,4},{6,7},{7,6},{8,12},{9,13},{10,... | collective-permute-start | bytes 614408 | tf_op jit(solution)/shard_map/ppermute | solution.py:575
  5.2 17.2 %collective-permute-start.1 = (f32[400,128]{1,0:T(8,128)S(1)}, f32[400,128]{1,0:T(8,128)S(1)}, u32[]{:S(2)}, u32[]{:S(2)}) collective-permute-start(f32[400,128]{1,0:T(8,128)S(1)} %get-tuple-element.19), channel_id=1, source_target_pairs={{0,5},{1,4},{2,7},{3,6},{4,1},{5,0},{6,3},{7,2},{8,10},{9,11},{10,... | collective-permute-start | bytes 614408 | tf_op jit(solution)/shard_map/ppermute | solution.py:575
  7.7 14.6 %collective-permute-start.2 = (f32[400,128]{1,0:T(8,128)S(1)}, f32[400,128]{1,0:T(8,128)S(1)}, u32[]{:S(2)}, u32[]{:S(2)}) collective-permute-start(f32[400,128]{1,0:T(8,128)S(1)} %get-tuple-element.20), channel_id=1, source_target_pairs={{0,3},{1,2},{2,1},{3,0},{4,7},{5,6},{6,5},{7,4},{8,14},{9,15},{10,... | collective-permute-start | bytes 614408 | tf_op jit(solution)/shard_map/ppermute | solution.py:575
  10.2 12.6 %collective-permute-start.3 = (f32[208,128]{1,0:T(8,128)S(1)}, f32[208,128]{1,0:T(8,128)S(1)}, u32[]{:S(2)}, u32[]{:S(2)}) collective-permute-start(f32[208,128]{1,0:T(8,128)S(1)} %get-tuple-element.21), channel_id=1, source_target_pairs={{0,7},{1,6},{2,5},{3,4},{4,3},{5,2},{6,1},{7,0},{8,15},{9,14},{10,... | collective-permute-start | bytes 319496 | tf_op jit(solution)/shard_map/ppermute | solution.py:575
  10.2 14.0 %collective-permute-start.4 = (f32[400,128]{1,0:T(8,128)S(1)}, f32[400,128]{1,0:T(8,128)S(1)}, u32[]{:S(2)}, u32[]{:S(2)}) collective-permute-start(f32[400,128]{1,0:T(8,128)S(1)} %collective-permute-done.mine_0), channel_id=1, source_target_pairs={{0,8},{8,0},{1,9},{9,1},{2,10},{10,2},{3,11},{11,3},{4,12},{12,4},... | collective-permute-start | bytes 614408 | tf_op jit(solution)/shard_map/ppermute | solution.py:567
  22.4 1.9 %collective-permute-start.5 = (f32[400,128]{1,0:T(8,128)S(1)}, f32[400,128]{1,0:T(8,128)S(1)}, u32[]{:S(2)}, u32[]{:S(2)}) collective-permute-start(f32[400,128]{1,0:T(8,128)S(1)} %collective-permute-done.1.mine_1), channel_id=1, source_target_pairs={{0,8},{8,0},{1,9},{9,1},{2,10},{10,2},{3,11},{11,3},{4,12},{12,4},... | collective-permute-start | bytes 614408 | tf_op jit(solution)/shard_map/ppermute | solution.py:567
  22.4 1.9 %collective-permute-start.6 = (f32[400,128]{1,0:T(8,128)S(1)}, f32[400,128]{1,0:T(8,128)S(1)}, u32[]{:S(2)}, u32[]{:S(2)}) collective-permute-start(f32[400,128]{1,0:T(8,128)S(1)} %collective-permute-done.2.mine_2), channel_id=1, source_target_pairs={{0,8},{8,0},{1,9},{9,1},{2,10},{10,2},{3,11},{11,3},{4,12},{12,4},... | collective-permute-start | bytes 614408 | tf_op jit(solution)/shard_map/ppermute | solution.py:567
  22.9 1.4 %collective-permute-start.7 = (f32[208,128]{1,0:T(8,128)S(1)}, f32[208,128]{1,0:T(8,128)S(1)}, u32[]{:S(2)}, u32[]{:S(2)}) collective-permute-start(f32[208,128]{1,0:T(8,128)S(1)} %collective-permute-done.3.mine_3), channel_id=1, source_target_pairs={{0,8},{8,0},{1,9},{9,1},{2,10},{10,2},{3,11},{11,3},{4,12},{12,4},... | collective-permute-start | bytes 319496 | tf_op jit(solution)/shard_map/ppermute | solution.py:567
  31.2 2.1 %collective-permute-start.8 = (f32[408,128]{1,0:T(8,128)S(1)}, f32[408,128]{1,0:T(8,128)S(1)}, u32[]{:S(2)}, u32[]{:S(2)}) collective-permute-start(f32[408,128]{1,0:T(8,128)S(1)} %get-tuple-element.23), channel_id=1, source_target_pairs={{0,8},{8,0},{1,9},{9,1},{2,10},{10,2},{3,11},{11,3},{4,12},{12,4},... | collective-permute-start | bytes 626696 | tf_op jit(solution)/shard_map/ppermute | solution.py:567
  33.4 11.2 %collective-permute-start.10 = (f32[200,128]{1,0:T(8,128)S(1)}, f32[200,128]{1,0:T(8,128)S(1)}, u32[]{:S(2)}, u32[]{:S(2)}) collective-permute-start(f32[200,128]{1,0:T(8,128)S(1)} %get-tuple-element.26), channel_id=1, source_target_pairs={{0,5},{1,4},{2,7},{3,6},{4,1},{5,0},{6,3},{7,2},{8,15},{9,14},{10,... | collective-permute-start | bytes 307208 | tf_op jit(solution)/shard_map/ppermute | solution.py:575
  38.4 6.3 %collective-permute-start.11 = (f32[200,128]{1,0:T(8,128)S(1)}, f32[200,128]{1,0:T(8,128)S(1)}, u32[]{:S(2)}, u32[]{:S(2)}) collective-permute-start(f32[200,128]{1,0:T(8,128)S(1)} %get-tuple-element.27), channel_id=1, source_target_pairs={{0,1},{1,0},{2,3},{3,2},{4,5},{5,4},{6,7},{7,6},{8,14},{9,15},{10,... | collective-permute-start | bytes 307208 | tf_op jit(solution)/shard_map/ppermute | solution.py:575
  39.8 5.5 %collective-permute-start.12 = (f32[200,128]{1,0:T(8,128)S(1)}, f32[200,128]{1,0:T(8,128)S(1)}, u32[]{:S(2)}, u32[]{:S(2)}) collective-permute-start(f32[200,128]{1,0:T(8,128)S(1)} %get-tuple-element.28), channel_id=1, source_target_pairs={{0,2},{1,3},{2,0},{3,1},{4,6},{5,7},{6,4},{7,5},{8,11},{9,10},{10,... | collective-permute-start | bytes 307208 | tf_op jit(solution)/shard_map/ppermute | solution.py:575
  39.8 6.8 %collective-permute-start.9 = (f32[104,128]{1,0:T(8,128)S(1)}, f32[104,128]{1,0:T(8,128)S(1)}, u32[]{:S(2)}, u32[]{:S(2)}) collective-permute-start(f32[104,128]{1,0:T(8,128)S(1)} %get-tuple-element.25), channel_id=1, source_target_pairs={{0,4},{1,5},{2,6},{3,7},{4,0},{5,1},{6,2},{7,3},{8,12},{9,13},{10,... | collective-permute-start | bytes 159752 | tf_op jit(solution)/shard_map/ppermute | solution.py:575
  44.6 2.0 %collective-permute-start.13 = (f32[200,128]{1,0:T(8,128)S(1)}, f32[200,128]{1,0:T(8,128)S(1)}, u32[]{:S(2)}, u32[]{:S(2)}) collective-permute-start(f32[200,128]{1,0:T(8,128)S(1)} %collective-permute-done.10.refs_0_), channel_id=1, source_target_pairs={{0,8},{8,0},{1,9},{9,1},{2,10},{10,2},{3,11},{11,3},{4,12},{12,4},... | collective-permute-start | bytes 307208 | tf_op jit(solution)/shard_map/ppermute | solution.py:567
  44.6 2.0 %collective-permute-start.14 = (f32[200,128]{1,0:T(8,128)S(1)}, f32[200,128]{1,0:T(8,128)S(1)}, u32[]{:S(2)}, u32[]{:S(2)}) collective-permute-start(f32[200,128]{1,0:T(8,128)S(1)} %collective-permute-done.11.refs_1_), channel_id=1, source_target_pairs={{0,8},{8,0},{1,9},{9,1},{2,10},{10,2},{3,11},{11,3},{4,12},{12,4},... | collective-permute-start | bytes 307208 | tf_op jit(solution)/shard_map/ppermute | solution.py:567
  45.3 1.3 %collective-permute-start.15 = (f32[200,128]{1,0:T(8,128)S(1)}, f32[200,128]{1,0:T(8,128)S(1)}, u32[]{:S(2)}, u32[]{:S(2)}) collective-permute-start(f32[200,128]{1,0:T(8,128)S(1)} %collective-permute-done.12.refs_2_), channel_id=1, source_target_pairs={{0,8},{8,0},{1,9},{9,1},{2,10},{10,2},{3,11},{11,3},{4,12},{12,4},... | collective-permute-start | bytes 307208 | tf_op jit(solution)/shard_map/ppermute | solution.py:567
